TPU v7x, 256 devices: a whole 4x4x8 slice. The times are simulated.
256 devices in a mesh: ocn: 8 (over z), atm: 32 (over y, x, core).
Axes of the slice: x: 4, y: 4, z: 8, core: 2. Of those that a mesh axis runs over, the one named last changes fastest.
Arguments:
- atm_fields: bfloat16 [2048, 32, 128], P('atm'), may hold values from -6 to 6
- weights: bfloat16 [98304, 128, 128], P(('ocn', 'atm')), may hold values from -0.5 to 0.5
- surf_temp: float32 [98304, 128], P(('ocn', 'atm')), may hold values from -6 to 6
- surf_hum: float32 [98304, 128], P(('ocn', 'atm')), may hold values from -6 to 6
- roughness: float32 [98304, 128], P(('ocn', 'atm')), may hold values from 0.0001 to 0.1
- cell_area: float32 [98304, 128], P(('ocn', 'atm')), may hold values from 0.2 to 2
- need_list: int32 [256, 32, 4], P(('ocn', 'atm')), may hold values from 0 to 63
- use_slot: int32 [98304], P(('ocn', 'atm')), may hold values from 0 to 127, as said below
- ocean_block: int32 [98304], P(('ocn', 'atm')), may hold values from 0 to 31
- ocean_cell: int32 [98304, 128], P(('ocn', 'atm')), may hold values from 0 to 127
- cell_count: int32 [98304], P(('ocn', 'atm')), may hold values from 1 to 128, as said below
- ice_mask: int32 [98304, 128], P(('ocn', 'atm')), may hold values 0 or 1
Outputs:
- atm_flux: float32 [2048, 4, 128], P('atm')
- ocean_flux: float32 [256, 32, 128], P(('ocn', 'atm'))
Inputs may be any that keep to these rules, and one draw needn't show every extreme that they name: `use_slot`: within the 384 exchange blocks of each device every slot value appears at least once. `cell_count`: each device has a block with 128 live cells and one with a single live cell.
All inputs are finite; a program needn't handle non-finite values. No bound on the sum of `ice_mask` on one device may be relied on, other than what follows from the above.
Results may differ from a plain program's by a relative error of at most 0.00087.
Values may be sent and summed in bfloat16 or wider, within the bound.
No kernel may reach another device: no remote copies, remote signals or barrier semaphores. Data moves between devices by JAX's collectives and lax.ppermute only.
A program may use at most 128 MiB of HBM per device.

v0:
```python
import math

import jax
import jax.numpy as jnp
from jax import lax
from jax.sharding import PartitionSpec as P

F = 32
BLK = 128
ACELL = 128
OCELL = 128
CAP = 4
ITERS = 8
OBD = 1


ref_height = 10.0
karman = 0.4
buoyancy = 0.5
flux_scale = 40.0


def similarity(wind_speed, temp_diff, hum_diff, log_mom, log_heat, psi_mom, psi_heat):
    fric_vel = karman * wind_speed / (log_mom - psi_mom)
    temp_scale = karman * temp_diff / (log_heat - psi_heat)
    hum_scale = karman * hum_diff / (log_heat - psi_heat)
    return (fric_vel, temp_scale, hum_scale)


def bulk_fluxes(mapped, surf_temp, surf_hum, roughness, ice_frac):
    wind_u = 6.0 * mapped[:, 0]
    wind_v = 6.0 * mapped[:, 1]
    wind_speed = jnp.sqrt(wind_u * wind_u + wind_v * wind_v + 1.0)
    temp_diff = mapped[:, 2] - surf_temp
    hum_diff = (mapped[:, 3] - surf_hum) * (1.0 - 0.6 * ice_frac)
    log_mom = jnp.log(ref_height / roughness)
    log_heat = log_mom + math.log(10.0)
    psi_mom = jnp.zeros_like(wind_speed)
    psi_heat = jnp.zeros_like(wind_speed)
    for sweep in range(ITERS):
        fric_vel, temp_scale, hum_scale = similarity(
            wind_speed, temp_diff, hum_diff, log_mom, log_heat, psi_mom, psi_heat
        )
        stability = jnp.clip(
            ref_height * karman * buoyancy * (temp_scale + 0.2 * hum_scale) / (fric_vel * fric_vel),
            -5.0,
            1.0,
        )
        unstable = jnp.minimum(stability, 0.0)
        root_term = jnp.sqrt(jnp.sqrt(1.0 - 16.0 * unstable))
        square_term = jnp.log((1.0 + root_term * root_term) / 2.0)
        psi_mom = jnp.where(
            stability >= 0.0,
            -5.0 * stability,
            2.0 * jnp.log((1.0 + root_term) / 2.0)
            + square_term
            - 2.0 * jnp.arctan(root_term)
            + math.pi / 2.0,
        )
        psi_heat = jnp.where(stability >= 0.0, -5.0 * stability, 2.0 * square_term)
    fric_vel, temp_scale, hum_scale = similarity(
        wind_speed, temp_diff, hum_diff, log_mom, log_heat, psi_mom, psi_heat
    )
    return jnp.stack(
        [
            flux_scale * fric_vel * fric_vel * wind_u / wind_speed,
            flux_scale * fric_vel * fric_vel * wind_v / wind_speed,
            -flux_scale * fric_vel * temp_scale,
            -flux_scale * fric_vel * hum_scale,
        ],
        axis=1,
    )


def per_device(
    atm_fields,
    weights,
    surf_temp,
    surf_hum,
    roughness,
    cell_area,
    need_list,
    use_slot,
    ocean_block,
    ocean_cell,
    cell_count,
    ice_mask,
):
    owners = lax.axis_size("atm")
    local_blocks = atm_fields.shape[0]
    slot_total = owners * CAP
    block_total = weights.shape[0]
    wanted = need_list[0]
    requests = lax.all_to_all(wanted, "atm", split_axis=0, concat_axis=0, tiled=True)
    served = atm_fields[requests.reshape(-1)].reshape(owners, CAP, F, ACELL)
    arrived = lax.all_to_all(served, "atm", split_axis=0, concat_axis=0, tiled=True)
    table = arrived.reshape(slot_total, F, ACELL)
    picked = table[use_slot]
    mapped = jnp.einsum("kfa,kba->kfb", picked, weights, preferred_element_type=jnp.float32)
    ice_frac = ice_mask.astype(jnp.float32)
    flux4 = bulk_fluxes(mapped, surf_temp, surf_hum, roughness, ice_frac)
    is_live = (jnp.arange(BLK, dtype=jnp.int32)[None, :] < cell_count[:, None]).astype(jnp.float32)
    cell_weight = cell_area * is_live
    weighted = (cell_weight[:, None, :] * flux4).astype(jnp.bfloat16)
    contrib = jnp.einsum("kcb,kba->kca", weighted, weights, preferred_element_type=jnp.float32)
    slot_hot = (use_slot[:, None] == jnp.arange(slot_total, dtype=jnp.int32)[None, :]).astype(
        jnp.float32
    )
    slot_sums = jnp.dot(
        slot_hot.T, contrib.reshape(block_total, 4 * ACELL), precision=lax.Precision.HIGHEST
    )
    returned = lax.all_to_all(
        slot_sums.reshape(owners, CAP, 4 * ACELL), "atm", split_axis=0, concat_axis=0, tiled=True
    )
    owner_hot = (
        requests.reshape(-1)[:, None] == jnp.arange(local_blocks, dtype=jnp.int32)[None, :]
    ).astype(jnp.float32)
    owner_sums = jnp.dot(
        owner_hot.T, returned.reshape(slot_total, 4 * ACELL), precision=lax.Precision.HIGHEST
    )
    atm_flux = lax.psum(owner_sums, "ocn").reshape(local_blocks, 4, ACELL)
    passive = mapped[:, 4:] * (1.0 - 0.7 * ice_frac)[:, None, :]
    ocean_values = cell_weight[:, None, :] * jnp.concatenate([flux4, passive], axis=1)
    cell_hot = (ocean_cell[:, :, None] == jnp.arange(OCELL, dtype=jnp.int32)[None, None, :]).astype(
        jnp.float32
    )
    partial_sum = jnp.einsum(
        "kfb,kbc->kfc", ocean_values, cell_hot, precision=lax.Precision.HIGHEST
    )
    flat_partial = partial_sum.reshape(block_total, F * OCELL)
    targets = jnp.arange(lax.axis_size("atm") * OBD, dtype=jnp.int32)
    picker = (ocean_block[None, :] == targets[:, None]).astype(jnp.float32)
    ocean_rows = lax.psum_scatter(
        jnp.dot(picker, flat_partial, precision=lax.Precision.HIGHEST),
        "atm",
        scatter_dimension=0,
        tiled=True,
    )
    ocean_flux = ocean_rows.reshape(OBD, F, OCELL)
    return (atm_flux, ocean_flux)


def solution(mesh):
    placed = (
        P("atm", None, None),
        P(("ocn", "atm"), None, None),
        P(("ocn", "atm"), None),
        P(("ocn", "atm"), None),
        P(("ocn", "atm"), None),
        P(("ocn", "atm"), None),
        P(("ocn", "atm"), None, None),
        P(("ocn", "atm")),
        P(("ocn", "atm")),
        P(("ocn", "atm"), None),
        P(("ocn", "atm")),
        P(("ocn", "atm"), None),
    )
    return jax.shard_map(
        per_device,
        mesh=mesh,
        in_specs=placed,
        out_specs=(P("atm", None, None), P(("ocn", "atm"), None, None)),
        check_vma=False,
    )
```

profile of v0, /device:TPU:2, one launch (start us, length us, event | category | flops | bytes accessed | tf_op | source)
XLA Modules:
  0.0 347.1 jit_solution(1982289157801807212)
XLA Ops:
  7.2 0.0 copy-start
  7.2 0.8 copy.35
  8.0 13.6 %all_to_all.19 = s32[32,1,4]{2,1,0:T(1,128)S(1)} all-to-all(s32[32,1,4]{2,1,0:T(1,128)S(1)} %copy.35), channel_id=1, replica_groups=mesh['ocn'=8,'atm'=32] {'atm'}, dimensions={0} | all-to-all | bytes 1024 | tf_op jit(solution)/shard_map/all_to_all | solution.py:94
  21.6 0.1 reshape.90
  21.7 0.0 copy-done
  21.7 1.7 gather_fusion
  23.4 5.0 %all-to-all-start.1 = ((bf16[32,4,32,128]{3,2,1,0:T(8,128)(2,1)}), bf16[32,4,32,128]{3,2,1,0:T(8,128)(2,1)S(1)}, u32[]{:S(2)}, u32[]{:S(2)}) async-start(bf16[32,4,32,128]{3,2,1,0:T(8,128)(2,1)} %bitcast.2), calls=%async_computation.1 | async-start | bytes 2097152 | tf_op jit(solution)/shard_map/all_to_all | solution.py:96
  28.4 0.7 compare_select_fusion
  29.1 1.0 fusion.16
  30.2 14.5 %all-to-all-done.1 = bf16[32,4,32,128]{3,2,1,0:T(8,128)(2,1)S(1)} async-done(((bf16[32,4,32,128]{3,2,1,0:T(8,128)(2,1)}), bf16[32,4,32,128]{3,2,1,0:T(8,128)(2,1)S(1)}, u32[]{:S(2)}, u32[]{:S(2)}) %all-to-all-start.1) | async-done | bytes 1048608 | tf_op jit(solution)/shard_map/all_to_all | solution.py:96
  44.6 3.2 gather_fusion.1
  47.9 14.9 %fusion.27 = f32[384,32,128]{2,1,0:T(8,128)} fusion(bf16[384,32,128]{2,1,0:T(8,128)(2,1)} %gather_fusion.1, bf16[384,128,128]{2,1,0:T(8,128)(2,1)} %param.13), kind=kOutput, calls=%fused_computation.64 | convolution fusion | flops 402653184 | bytes 22020096 | tf_op jit(solution)/shard_map/kfa,kba->kfb/dot_general | solution.py:99
  62.8 4.0 %fusion.26 = (f32[384,1,128]{2,1,0:T(1,128)S(1)}, f32[384,1,128]{2,1,0:T(1,128)S(1)}, f32[384,1,128]{2,1,0:T(1,128)S(1)}, f32[384,1,128]{2,1,0:T(1,128)S(1)}) fusion(f32[384,32,128]{2,1,0:T(8,128)} %fusion.27), kind=kLoop, calls=%fused_computation.63 | loop fusion | bytes 1572864 | tf_op jit(solution)/shard_map/slice | solution.py:34
  66.8 0.0 copy-done.2
  66.8 0.0 copy-done.3
  66.8 0.0 copy-done.4
  66.8 0.0 copy-done.5
  66.8 5.4 %fusion.15 = (f32[384,128]{1,0:T(8,128)S(1)}, f32[384,128]{1,0:T(8,128)S(1)}, f32[384,128]{1,0:T(8,128)S(1)}) fusion(f32[384,1,128]{2,0,1:T(8,128)S(1)} %bitcast.87, f32[384,1,128]{2,0,1:T(8,128)S(1)} %bitcast.85, f32[384,128]{1,0:T(8,128)S(1)} %copy-done.2, s32[384,128]{1,0:T(8,128)S(1)} %copy-done.3, f32[384,128]{1,0:T(8,128)S(1)} %bitcast.89, ...), kind=kLoop, calls=%fused_computation.24 | loop fusion | flops 12337152 | bytes 2162688 | tf_op jit(solution)/shard_map/div | solution.py:66
  72.2 0.4 divide_multiply_fusion.1
  72.6 0.0 copy-done.1
  72.6 3.6 %slice_multiply_fusion = f32[384,28,128]{2,1,0:T(8,128)} fusion(f32[384,32,128]{2,1,0:T(8,128)S(1)} %copy-done.1, f32[384,128]{1,0:T(8,128)S(1)} %get-tuple-element.11), kind=kLoop, calls=%fused_computation.8 | loop fusion | flops 1376256 | bytes 11206656 | tf_op jit(solution)/shard_map/mul | solution.py:122
  76.3 30.8 %concatenate.4 = f32[384,32,128]{2,1,0:T(8,128)} concatenate(f32[384,1,128]{2,1,0:T(1,128)S(1)} %bitcast.81, f32[384,1,128]{2,1,0:T(1,128)S(1)} %bitcast.79, f32[384,1,128]{2,1,0:T(1,128)S(1)} %bitcast.75, f32[384,1,128]{2,1,0:T(1,128)S(1)} %bitcast.77, f32[384,28,128]{2,1,0:T(8,128)} %slice_multiply_fusion), dimensions={1} | concatenate | bytes 12582912 | tf_op jit(solution)/shard_map/concatenate | solution.py:123
  107.1 6.4 %fusion.8 = f32[384,4,128]{2,1,0:T(4,128)S(1)} fusion(bf16[384,128,128]{2,1,0:T(8,128)(2,1)} %param.13, f32[384,1,128]{2,1,0:T(1,128)S(1)} %bitcast.78, f32[384,1,128]{2,1,0:T(1,128)S(1)} %bitcast.76, f32[384,1,128]{2,1,0:T(1,128)S(1)} %bitcast.80, f32[384,1,128]{2,1,0:T(1,128)S(1)} %bitcast.82, f32[384,128]{1,0:T(8,128)S(1)} %fusion.16), kind=kOutput, calls=%fused_computation.13 | convolution fusion | flops 51314688 | bytes 14352384 | tf_op jit(solution)/shard_map/kcb,kba->kca/dot_general | solution.py:105
  113.4 0.3 reshape.115
  113.8 0.0 copy-done.7
  113.8 0.5 fusion.17
  114.3 0.9 copy.42
  115.1 5.2 %all-to-all-start.2 = ((f32[32,4,512]{2,1,0:T(4,128)}), f32[32,4,512]{2,1,0:T(4,128)S(1)}, u32[]{:S(2)}, u32[]{:S(2)}) async-start(f32[32,4,512]{2,1,0:T(4,128)} %copy.42), calls=%async_computation.2 | async-start | bytes 524288 | tf_op jit(solution)/shard_map/all_to_all | solution.py:112
  120.3 0.0 copy-start.8
  120.3 0.0 all-reduce.6.cloned.1.call-start
  120.4 20.6 %fusion = f32[384,32,128]{2,1,0:T(8,128)S(1)} fusion(s32[384,128]{1,0:T(8,128)S(1)} %copy-done.6, f32[384,32,128]{2,1,0:T(8,128)} %concatenate.4, f32[384,128]{1,0:T(8,128)S(1)} %fusion.16), kind=kOutput, calls=%fused_computation.3 | convolution fusion | flops 2423783424 | bytes 12976128 | tf_op jit(solution)/shard_map/kfb,kbc->kfc/dot_general | solution.py:127
  141.0 0.0 copy-start.9
  141.0 6.6 %fusion.2 = f32[32,4096]{1,0:T(8,128)} fusion(f32[48,8,32,128]{3,2,1,0:T(8,128)S(1)} %bitcast.73, s32[384]{0:T(512)S(1)} %copy-done.8), kind=kOutput, calls=%fused_computation.5 | convolution fusion | flops 603992064 | bytes 6817280 | tf_op jit(solution)/shard_map/dot_general | solution.py:134
  147.6 0.0 all-reduce.6.cloned.1.call-update
  147.7 0.0 all-reduce.4.cloned.1.call-start
  147.7 0.6 dynamic-slice
  148.4 0.5 broadcast.204
  148.9 0.7 reduce.5
  149.6 0.1 eq.72
  149.7 0.0 all-to-all-done.2
  149.7 0.1 reshape.94
  149.8 0.3 fusion.21
  150.1 0.7 reshape.95
  150.8 0.0 all-reduce.4.cloned.1.call-update
  150.8 112.9 %all-reduce.6.cloned.1.call-done = f32[32,4096]{1,0:T(8,128)} async-done(((f32[32,4096]{1,0:T(8,128)}), f32[32,4096]{1,0:T(8,128)}) %all-reduce.6.cloned.1.call-update) | async-done | bytes 524304
  263.7 2.2 constant_dynamic-slice_fusion
  265.9 72.8 %all-reduce.4.cloned.1.call-done = f32[64,4,128]{2,1,0:T(4,128)} async-done(((f32[64,4,128]{2,1,0:T(4,128)}), f32[64,4,128]{2,1,0:T(4,128)}) %all-reduce.4.cloned.1.call-update) | async-done | bytes 131088 | tf_op jit(solution)/shard_map/psum | solution.py:121
  338.7 1.6 copy.56
  (14 shorter events, 0.0 us)
Async XLA Ops:
  7.2 14.5 %copy-start = (bf16[64,32,128]{2,1,0:T(8,128)(2,1)S(1)}, bf16[64,32,128]{2,1,0:T(8,128)(2,1)}, u32[]{:S(2)}) copy-start(bf16[64,32,128]{2,1,0:T(8,128)(2,1)} %param.12) | copy-start | bytes 1572868
  23.4 21.3 %all-to-all-start.1 = ((bf16[32,4,32,128]{3,2,1,0:T(8,128)(2,1)}), bf16[32,4,32,128]{3,2,1,0:T(8,128)(2,1)S(1)}, u32[]{:S(2)}, u32[]{:S(2)}) async-start(bf16[32,4,32,128]{3,2,1,0:T(8,128)(2,1)} %bitcast.2), calls=%async_computation.1 | async-start | bytes 2097152 | tf_op jit(solution)/shard_map/all_to_all | solution.py:96
  47.8 18.9 %copy-start.2 = (f32[384,128]{1,0:T(8,128)S(1)}, f32[384,128]{1,0:T(8,128)}, u32[]{:S(2)}) copy-start(f32[384,128]{1,0:T(8,128)} %param.16) | copy-start | bytes 589828
  47.8 18.9 %copy-start.3 = (s32[384,128]{1,0:T(8,128)S(1)}, s32[384,128]{1,0:T(8,128)}, u32[]{:S(2)}) copy-start(s32[384,128]{1,0:T(8,128)} %param.23) | copy-start | bytes 589828
  47.9 18.9 %copy-start.4 = (f32[384,128]{1,0:T(8,128)S(1)}, f32[384,128]{1,0:T(8,128)}, u32[]{:S(2)}) copy-start(f32[384,128]{1,0:T(8,128)} %param.15) | copy-start | bytes 589828
  47.9 18.9 %copy-start.5 = (f32[384,128]{1,0:T(8,128)S(1)}, f32[384,128]{1,0:T(8,128)}, u32[]{:S(2)}) copy-start(f32[384,128]{1,0:T(8,128)} %param.14) | copy-start | bytes 589828
  62.8 9.9 %copy-start.1 = (f32[384,32,128]{2,1,0:T(8,128)S(1)}, f32[384,32,128]{2,1,0:T(8,128)}, u32[]{:S(2)}) copy-start(f32[384,32,128]{2,1,0:T(8,128)} %fusion.27) | copy-start | bytes 18874372
  107.0 6.7 %copy-start.7 = (s32[384]{0:T(512)S(1)}, s32[384]{0:T(512)}, u32[]{:S(2)}) copy-start(s32[384]{0:T(512)} %param.19) | copy-start | bytes 4612
  107.1 13.3 %copy-start.6 = (s32[384,128]{1,0:T(8,128)S(1)}, s32[384,128]{1,0:T(8,128)}, u32[]{:S(2)}) copy-start(s32[384,128]{1,0:T(8,128)} %param.21) | copy-start | bytes 589828
  115.1 34.5 %all-to-all-start.2 = ((f32[32,4,512]{2,1,0:T(4,128)}), f32[32,4,512]{2,1,0:T(4,128)S(1)}, u32[]{:S(2)}, u32[]{:S(2)}) async-start(f32[32,4,512]{2,1,0:T(4,128)} %copy.42), calls=%async_computation.2 | async-start | bytes 524288 | tf_op jit(solution)/shard_map/all_to_all | solution.py:112
  120.3 20.7 %copy-start.8 = (s32[384]{0:T(512)S(1)}, s32[384]{0:T(512)}, u32[]{:S(2)}) copy-start(s32[384]{0:T(512)} %param.20) | copy-start | bytes 4612
  120.3 143.4 %all-reduce.6.cloned.1.call-start = ((), (), s32[]{:S(2)}) async-start(), calls=%async_computation.4 | async-start | bytes 1048576
  141.0 6.7 %copy-start.9 = (u32[256]{0:T(256)S(1)}, u32[256]{0:T(256)}, u32[]{:S(2)}) copy-start(u32[256]{0:T(256)} %constant.72) | copy-start | bytes 3076
  147.7 191.0 %all-reduce.4.cloned.1.call-start = ((), (), s32[]{:S(2)}) async-start(), calls=%async_computation.3 | async-start | bytes 262144 | tf_op jit(solution)/shard_map/psum | solution.py:121
Sparse Core Ops, SparseCore 0:
  147.8 115.8 all-reduce.5
  266.7 71.9 all-reduce.3
where the time goes:
time: 348 us; the launch traced here: 347 us
  waiting for transfers between devices  200 us (57%)
  matrix products  49.3 us (14%)
  local copies, waits for them, and re-layouts  47.6 us (14%)
  between operations  14.3 us (4%)
  blocking collectives  13.6 us (4%)
  other arithmetic  11.9 us (3%)
  starting transfers between devices  10.3 us (3%)
    unnamed x3, waiting for transfers between devices  113 us
    psum x1, waiting for transfers between devices, per_device(): atm_flux = lax.psum(owner_sums, 'ocn').reshape(local_blocks, 4, ACELL)  72.8 us
    concatenate x1, local copies, waits for them, and re-layouts, per_device(): jnp.concatenate([flux4, passive], axis=1)  30.8 us
    dot_general x1, matrix products, per_device(): jnp.einsum('kfb,kbc->kfc', ocean_values, cell_hot, precision=lax.Precisio...  20.6 us
    dot_general x1, matrix products, per_device(): jnp.einsum('kfa,kba->kfb', picked, weights, preferred_element_type=jnp.fl...  14.9 us
    all_to_all x1, waiting for transfers between devices, per_device(): lax.all_to_all(served, 'atm', split_axis=0, concat_axis=0, tiled=True)  14.5 us
    all_to_all x1, blocking collectives, per_device(): lax.all_to_all(wanted, 'atm', split_axis=0, concat_axis=0, tiled=True)  13.6 us
  transfers between devices with their start and end apart: 4, of which 3 were waited for; matrix products, arithmetic and copies ran while one was open for 10% of the time, Pallas kernels for 0%

commit v1 on v0

v1 whole, which is shorter than its diff:
```python
import math

import jax
import jax.numpy as jnp
from jax import lax
from jax.experimental import pallas as pl
from jax.experimental.pallas import tpu as pltpu
from jax.sharding import PartitionSpec as P

F = 32
BLK = 128
ACELL = 128
OCELL = 128
CAP = 4
ITERS = 8

ref_height = 10.0
karman = 0.4
buoyancy = 0.5
flux_scale = 40.0

CHUNK = 64
GROUP = 8
MIB = 1 << 20
VMEM = pltpu.VMEM
SMEM = pltpu.SMEM

ARCTAN = (
    0.9999999952,
    -0.3333319239,
    0.1999324926,
    -0.1416585733,
    0.1012280370,
    -0.0507783010,
)


def arctan_half(t):
    z = t * t
    total = jnp.full_like(z, ARCTAN[-1])
    for c in ARCTAN[-2::-1]:
        total = total * z + c
    return total * t


def flux_rows(mapped_u, mapped_v, mapped_t, mapped_q, surf_temp, surf_hum, hum_factor, log_mom):
    wind_u = 6.0 * mapped_u
    wind_v = 6.0 * mapped_v
    square_speed = wind_u * wind_u + wind_v * wind_v + 1.0
    wind_speed = jnp.sqrt(square_speed)
    temp_diff = mapped_t - surf_temp
    hum_diff = (mapped_q - surf_hum) * hum_factor
    log_heat = log_mom + math.log(10.0)
    gain = (ref_height * buoyancy) * (temp_diff + 0.2 * hum_diff) / square_speed
    from_mom = log_mom
    from_heat = log_heat
    for sweep in range(ITERS):
        stability = jnp.clip(gain * from_mom * from_mom / from_heat, -5.0, 1.0)
        unstable = jnp.minimum(stability, 0.0)
        square = jnp.sqrt(1.0 - 16.0 * unstable)
        root = jnp.sqrt(square)
        half_square = 0.5 + 0.5 * square
        half_root = 0.5 + 0.5 * root
        log_square = jnp.log(half_square)
        log_both = jnp.log(half_root * half_root * half_square)
        turn = arctan_half((root - 1.0) / (root + 1.0))
        stable = stability >= 0.0
        psi_stable = -5.0 * stability
        psi_mom = jnp.where(stable, psi_stable, log_both - 2.0 * turn)
        psi_heat = jnp.where(stable, psi_stable, 2.0 * log_square)
        from_mom = log_mom - psi_mom
        from_heat = log_heat - psi_heat
    fric_vel = karman * wind_speed / from_mom
    drag = flux_scale * fric_vel * fric_vel / wind_speed
    carry = -flux_scale * karman * fric_vel / from_heat
    return drag * wind_u, drag * wind_v, carry * temp_diff, carry * hum_diff


def serve_body(requests, fields, out):
    def owner(d, _):
        for c in range(CAP):
            out[d * CAP + c] = fields[requests[d, c]]
        return 0

    lax.fori_loop(0, out.shape[0] // CAP, owner, 0)


def serve(requests, fields):
    return pl.pallas_call(
        serve_body,
        out_shape=jax.ShapeDtypeStruct((requests.size,) + fields.shape[1:], fields.dtype),
        in_specs=[pl.BlockSpec(memory_space=SMEM), pl.BlockSpec(memory_space=VMEM)],
        out_specs=pl.BlockSpec(memory_space=VMEM),
        compiler_params=pltpu.CompilerParams(vmem_limit_bytes=8 * MIB),
        name="serve",
    )(requests, fields)


def couple_body(
    use_slot,
    ocean_block,
    table,
    weights,
    surf_temp,
    surf_hum,
    hum_factor,
    log_mom,
    cell_weight,
    passive_weight,
    ocean_cell,
    slot_sums,
    ocean_sums,
    rows,
):
    step = pl.program_id(0)

    @pl.when(step == 0)
    def _():
        slot_sums[...] = jnp.zeros_like(slot_sums)
        ocean_sums[...] = jnp.zeros_like(ocean_sums)

    first = step * CHUNK

    def map_group(g, _):
        for i in range(GROUP):
            k = g * GROUP + i
            rows[pl.ds(pl.multiple_of(k * F, F), F), :] = lax.dot_general(
                table[use_slot[first + k]],
                weights[k],
                (((1,), (1,)), ((), ())),
                preferred_element_type=jnp.float32,
            )
        return 0

    lax.fori_loop(0, CHUNK // GROUP, map_group, 0)

    fluxes = flux_rows(
        *(rows[pl.ds(f, CHUNK, stride=F), :] for f in range(4)),
        surf_temp[...],
        surf_hum[...],
        hum_factor[...],
        log_mom[...],
    )
    for f in range(4):
        rows[pl.ds(f, CHUNK, stride=F), :] = cell_weight[...] * fluxes[f]

    cells = lax.broadcasted_iota(jnp.int32, (OCELL, BLK), 0)
    field = lax.broadcasted_iota(jnp.int32, (F, BLK), 0)

    def sum_group(g, _):
        for i in range(GROUP):
            k = g * GROUP + i
            value = rows[pl.ds(pl.multiple_of(k * F, F), F), :]
            value = jnp.where(field < 4, value, value * passive_weight[pl.ds(k, 1), :])
            high = value.astype(jnp.bfloat16)
            low = (value - high.astype(jnp.float32)).astype(jnp.bfloat16)
            contrib = jnp.dot(high[:16], weights[k], preferred_element_type=jnp.float32)
            slot = use_slot[first + k]
            slot_sums[slot] = slot_sums[slot] + contrib[:4]
            hot = jnp.where(cells == ocean_cell[pl.ds(k, 1), :], 1.0, 0.0).astype(jnp.bfloat16)
            both = lax.dot_general(
                jnp.concatenate([high, low], axis=0),
                hot,
                (((1,), (1,)), ((), ())),
                preferred_element_type=jnp.float32,
            )
            target = ocean_block[first + k]
            ocean_sums[target] = ocean_sums[target] + (both[:F] + both[F:])
        return 0

    lax.fori_loop(0, CHUNK // GROUP, sum_group, 0)


def couple(use_slot, ocean_block, table, weights, cells, ocean_cell, owners):
    blocks = weights.shape[0]
    whole = lambda shape: pl.BlockSpec(shape, lambda s, *_: (0,) * len(shape))
    part = pl.BlockSpec((CHUNK, BLK), lambda s, *_: (s, 0))
    return pl.pallas_call(
        couple_body,
        out_shape=(
            jax.ShapeDtypeStruct((table.shape[0], 4, ACELL), jnp.float32),
            jax.ShapeDtypeStruct((owners, F, OCELL), jnp.float32),
        ),
        grid_spec=pltpu.PrefetchScalarGridSpec(
            num_scalar_prefetch=2,
            grid=(blocks // CHUNK,),
            in_specs=[
                whole(table.shape),
                pl.BlockSpec((CHUNK, BLK, ACELL), lambda s, *_: (s, 0, 0)),
            ]
            + [part] * 7,
            out_specs=(whole((table.shape[0], 4, ACELL)), whole((owners, F, OCELL))),
            scratch_shapes=[pltpu.VMEM((CHUNK * F, BLK), jnp.float32)],
        ),
        compiler_params=pltpu.CompilerParams(vmem_limit_bytes=32 * MIB),
        name="couple",
    )(use_slot, ocean_block, table, weights, *cells, ocean_cell)


def gather_sums_body(place, requests, returned, *rest):
    outs, sums = rest[:-1], rest[-1]
    sums[...] = jnp.zeros_like(sums)

    def owner(d, _):
        for c in range(CAP):
            b = requests[d, c]
            sums[b] = sums[b] + returned[d * CAP + c]
        return 0

    lax.fori_loop(0, returned.shape[0] // CAP, owner, 0)
    ranks = len(outs)
    share = sums.shape[0] // ranks
    for s in range(ranks):
        out_of = lax.rem(place[0] + s, ranks)
        outs[s][...] = sums[pl.ds(out_of * share, share)]


def gather_sums(place, requests, returned, local_blocks, ranks):
    share = (local_blocks // ranks,) + returned.shape[1:]
    return pl.pallas_call(
        gather_sums_body,
        out_shape=[jax.ShapeDtypeStruct(share, jnp.float32)] * ranks,
        in_specs=[
            pl.BlockSpec(memory_space=SMEM),
            pl.BlockSpec(memory_space=SMEM),
            pl.BlockSpec(memory_space=VMEM),
        ],
        out_specs=[pl.BlockSpec(memory_space=VMEM)] * ranks,
        scratch_shapes=[pltpu.VMEM((local_blocks,) + returned.shape[1:], jnp.float32)],
        compiler_params=pltpu.CompilerParams(vmem_limit_bytes=8 * MIB),
        name="gather_sums",
    )(place, requests, returned)


def lay_out_body(place, *rest):
    parts, out = rest[:-1], rest[-1]
    ranks = len(parts)
    share = out.shape[0] // ranks
    for s in range(ranks):
        owner = lax.rem(place[0] + (ranks - s), ranks)
        out[pl.ds(owner * share, share)] = parts[s][...]


def lay_out(place, parts):
    ranks = len(parts)
    shape = (parts[0].shape[0] * ranks,) + parts[0].shape[1:]
    return pl.pallas_call(
        lay_out_body,
        out_shape=jax.ShapeDtypeStruct(shape, jnp.float32),
        in_specs=[pl.BlockSpec(memory_space=SMEM)] + [pl.BlockSpec(memory_space=VMEM)] * ranks,
        out_specs=pl.BlockSpec(memory_space=VMEM),
        compiler_params=pltpu.CompilerParams(vmem_limit_bytes=8 * MIB),
        name="lay_out",
    )(place, *parts)


def shift(x, axis, by):
    ranks = lax.axis_size(axis)
    return lax.ppermute(x, axis, [(i, (i + by) % ranks) for i in range(ranks)])


def per_device(
    atm_fields,
    weights,
    surf_temp,
    surf_hum,
    roughness,
    cell_area,
    need_list,
    use_slot,
    ocean_block,
    ocean_cell,
    cell_count,
    ice_mask,
):
    owners = lax.axis_size("atm")
    ranks = lax.axis_size("ocn")
    local_blocks = atm_fields.shape[0]
    place = lax.axis_index("ocn").astype(jnp.int32).reshape(1)
    requests = lax.all_to_all(need_list[0], "atm", split_axis=0, concat_axis=0, tiled=True)
    table = lax.all_to_all(serve(requests, atm_fields), "atm", split_axis=0, concat_axis=0, tiled=True)
    ice_frac = ice_mask.astype(jnp.float32)
    is_live = jnp.arange(BLK, dtype=jnp.int32)[None, :] < cell_count[:, None]
    cell_weight = jnp.where(is_live, cell_area, 0.0)
    cells = (
        surf_temp,
        surf_hum,
        1.0 - 0.6 * ice_frac,
        jnp.log(ref_height / roughness),
        cell_weight,
        cell_weight * (1.0 - 0.7 * ice_frac),
    )
    slot_sums, ocean_sums = couple(
        use_slot, ocean_block, table, weights, cells, ocean_cell, owners
    )
    returned = lax.all_to_all(slot_sums, "atm", split_axis=0, concat_axis=0, tiled=True)
    ocean_parts = lax.all_to_all(ocean_sums, "atm", split_axis=0, concat_axis=0, tiled=True)
    shares = gather_sums(place, requests, returned, local_blocks, ranks)
    mine = shares[0]
    for s in range(1, ranks):
        mine = mine + shift(shares[s], "ocn", s)
    atm_flux = lay_out(place, [mine] + [shift(mine, "ocn", s) for s in range(1, ranks)])
    ocean_flux = jnp.sum(ocean_parts, axis=0, keepdims=True)
    return (atm_flux, ocean_flux)


def solution(mesh):
    placed = (
        P("atm", None, None),
        P(("ocn", "atm"), None, None),
        P(("ocn", "atm"), None),
        P(("ocn", "atm"), None),
        P(("ocn", "atm"), None),
        P(("ocn", "atm"), None),
        P(("ocn", "atm"), None, None),
        P(("ocn", "atm")),
        P(("ocn", "atm")),
        P(("ocn", "atm"), None),
        P(("ocn", "atm")),
        P(("ocn", "atm"), None),
    )
    return jax.shard_map(
        per_device,
        mesh=mesh,
        in_specs=placed,
        out_specs=(P("atm", None, None), P(("ocn", "atm"), None, None)),
        check_vma=False,
    )
```

time: 348 us -> 144 us (0.41)
  waiting for transfers between devices: 200 us -> 19.3 us
  matrix products: 49.3 us -> 0 us
  Pallas kernels: 0 us -> 41 us
  local copies, waits for them, and re-layouts: 47.6 us -> 10.5 us
  starting transfers between devices: 10.3 us -> 43 us
  between operations: 14.3 us -> 0.71 us
  blocking collectives: 13.6 us -> 25.8 us
  other arithmetic: 11.9 us -> 2.79 us
    unnamed x3 -> x0, waiting for transfers between devices: 113 us -> none
    psum x1 -> x0, waiting for transfers between devices: 72.8 us -> none  [per_device(): atm_flux = lax.psum(owner_sums, 'ocn').reshape(local_blocks, 4, ACELL)]
    dot_general x6 -> x0, matrix products: 49.3 us -> none  [the longest x1 20.6 us: per_device(): jnp.einsum('kfb,kbc->kfc', ocean_values, cell_hot, precision=lax.Precisio...]
    pallas_call x0 -> x4, Pallas kernels: none -> 41 us  [the longest x1 36.8 us: couple(): pl.pallas_call(couple_body, out_shape=(jax.ShapeDtypeStruct((table.shape[...]
    ppermute x0 -> x14, starting transfers between devices: none -> 33 us  [shift(): return lax.ppermute(x, axis, [(i, (i + by) % ranks) for i in range(ranks)])]
    concatenate x1 -> x0, local copies, waits for them, and re-layouts: 30.8 us -> none  [per_device(): jnp.concatenate([flux4, passive], axis=1)]
    all_to_all x1 -> x2, blocking collectives: 13.6 us -> 25.8 us  [the longest x1 13.6 us: per_device(): lax.all_to_all(need_list[0], 'atm', split_axis=0, concat_axis=0, tiled=True)]
    div x1 -> x0, other arithmetic: 5.38 us -> none  [bulk_fluxes(): flux_scale * fric_vel * fric_vel * wind_u / wind_speed]
  transfers between devices with their start and end apart: 4 -> 16, of which waited for: 3 -> 4; matrix products, arithmetic and copies ran while one was open for 10% -> 1% of each run, Pallas kernels for 0% -> 1%
where the time goes in v1:
time: 144 us; the launch traced here: 143 us
  starting transfers between devices  43 us (30%)
  Pallas kernels  41 us (28%)
  blocking collectives  25.8 us (18%)
  waiting for transfers between devices  19.3 us (13%)
  local copies, waits for them, and re-layouts  10.5 us (7%)
  other arithmetic  2.79 us (2%)
    pallas_call x1, Pallas kernels, couple(): pl.pallas_call(couple_body, out_shape=(jax.ShapeDtypeStruct((table.shape[...  36.8 us
    ppermute x14, starting transfers between devices, shift(): return lax.ppermute(x, axis, [(i, (i + by) % ranks) for i in range(ranks)])  33 us
    all_to_all x1, waiting for transfers between devices, per_device(): lax.all_to_all(serve(requests, atm_fields), 'atm', split_axis=0, concat_a...  14.1 us
    all_to_all x1, blocking collectives, per_device(): lax.all_to_all(need_list[0], 'atm', split_axis=0, concat_axis=0, tiled=True)  13.6 us
    all_to_all x1, blocking collectives, per_device(): lax.all_to_all(slot_sums, 'atm', split_axis=0, concat_axis=0, tiled=True)  12.2 us
    unnamed x14, local copies, waits for them, and re-layouts  9.76 us
    ppermute x14, waiting for transfers between devices, shift(): return lax.ppermute(x, axis, [(i, (i + by) % ranks) for i in range(ranks)])  5.2 us
    all_to_all x1, starting transfers between devices, per_device(): lax.all_to_all(serve(requests, atm_fields), 'atm', split_axis=0, concat_a...  5.03 us
  transfers between devices with their start and end apart: 16, of which 4 were waited for; matrix products, arithmetic and copies ran while one was open for 1% of the time, Pallas kernels for 1%

profile of v1, /device:TPU:2, one launch (start us, length us, event | category | flops | bytes accessed | tf_op | source)
XLA Modules:
  0.0 143.1 jit_solution(5650748676764655061)
XLA Ops:
  0.6 0.8 copy.16
  1.4 13.6 %all_to_all.26 = s32[32,1,4]{2,1,0:T(1,128)S(1)} all-to-all(s32[32,1,4]{2,1,0:T(1,128)S(1)} %copy.16), channel_id=1, replica_groups=mesh['ocn'=8,'atm'=32] {'atm'}, dimensions={0} | all-to-all | bytes 1024 | tf_op jit(solution)/shard_map/all_to_all | solution.py:280
  14.9 1.0 copy-done.1
  16.0 2.1 %serve.1 = bf16[128,32,128]{2,1,0:T(8,128)(2,1)} custom-call(s32[32,4]{1,0:T(8,128)S(1)} %bitcast.13, bf16[64,32,128]{2,1,0:T(8,128)(2,1)S(1)} %copy-done.1), custom_call_target="tpu_custom_call" | custom-call | tf_op jit(solution)/shard_map/serve/pallas_call | solution.py:89
  18.1 5.0 %all-to-all-start.1 = ((bf16[128,32,128]{2,1,0:T(8,128)(2,1)}), bf16[128,32,128]{2,1,0:T(8,128)(2,1)S(1)}, u32[]{:S(2)}, u32[]{:S(2)}) async-start(bf16[128,32,128]{2,1,0:T(8,128)(2,1)} %serve.1), calls=%async_computation.1 | async-start | bytes 2097152 | tf_op jit(solution)/shard_map/all_to_all | solution.py:281
  23.1 1.0 divide_log_fusion.log_mom
  24.1 1.1 subtract_multiply_fusion
  25.3 14.1 %all-to-all-done.1.table = bf16[128,32,128]{2,1,0:T(8,128)(2,1)S(1)} async-done(((bf16[128,32,128]{2,1,0:T(8,128)(2,1)}), bf16[128,32,128]{2,1,0:T(8,128)(2,1)S(1)}, u32[]{:S(2)}, u32[]{:S(2)}) %all-to-all-start.1) | async-done | bytes 1048608 | tf_op jit(solution)/shard_map/all_to_all | solution.py:281
  39.4 4.6 %copy-done = bf16[384,128,128]{2,1,0:T(8,128)(2,1)S(1)} copy-done((bf16[384,128,128]{2,1,0:T(8,128)(2,1)S(1)}, bf16[384,128,128]{2,1,0:T(8,128)(2,1)}, u32[]{:S(2)}) %copy-start) | copy-done | bytes 12582936
  43.9 0.9 copy-done.2
  44.9 0.9 copy-done.3
  45.8 0.9 copy-done.4
  46.7 0.7 copy-done.5
  47.4 0.7 copy-done.6
  48.1 36.8 %couple.1 = (f32[128,4,128]{2,1,0:T(4,128)S(1)}, f32[32,32,128]{2,1,0:T(8,128)}) custom-call(s32[384]{0:T(512)S(1)} %copy-done.5, s32[384]{0:T(512)S(1)} %copy-done.6, bf16[128,32,128]{2,1,0:T(8,128)(2,1)S(1)} %all-to-all-done.1.table, bf16[384,128,128]{2,1,0:T(8,128)(2,1)S(1)} %copy-done, f32[384,128]{1,0:T(8,128)S(1)} %copy-done.2, ...), custom_call_target="tpu_custom_call" | custom-call | tf_op jit(solution)/shard_map/couple/pallas_call | solution.py:178
  84.9 12.2 %all_to_all.27.returned = f32[128,4,128]{2,1,0:T(4,128)S(1)} all-to-all(f32[128,4,128]{2,1,0:T(4,128)S(1)} %get-tuple-element.12), channel_id=1, replica_groups=mesh['ocn'=8,'atm'=32] {'atm'}, dimensions={0} | all-to-all | bytes 524288 | tf_op jit(solution)/shard_map/all_to_all | solution.py:296
  97.1 5.0 %all-to-all-start.3 = ((f32[32,32,128]{2,1,0:T(8,128)}), f32[32,32,128]{2,1,0:T(8,128)S(1)}, u32[]{:S(2)}, u32[]{:S(2)}) async-start(f32[32,32,128]{2,1,0:T(8,128)} %get-tuple-element.21), calls=%async_computation.3 | async-start | bytes 1048576 | tf_op jit(solution)/shard_map/all_to_all | solution.py:297
  102.1 1.4 gather_sums.1
  103.5 5.9 %collective-permute-start.6 = (f32[8,4,128]{2,1,0:T(4,128)S(1)}, f32[8,4,128]{2,1,0:T(4,128)S(1)}, u32[]{:S(2)}, u32[]{:S(2)}) collective-permute-start(f32[8,4,128]{2,1,0:T(4,128)S(1)} %get-tuple-element.20), channel_id=1, source_target_pairs={{0,224},{32,0},{64,32},{96,64},{128,96},{160,128},{192,160},{224,1... | collective-permute-start | bytes 49160 | tf_op jit(solution)/shard_map/ppermute | solution.py:259
  109.4 1.5 %collective-permute-start.5 = (f32[8,4,128]{2,1,0:T(4,128)S(1)}, f32[8,4,128]{2,1,0:T(4,128)S(1)}, u32[]{:S(2)}, u32[]{:S(2)}) collective-permute-start(f32[8,4,128]{2,1,0:T(4,128)S(1)} %get-tuple-element.19), channel_id=1, source_target_pairs={{0,192},{32,224},{64,0},{96,32},{128,64},{160,96},{192,128},{224,1... | collective-permute-start | bytes 49160 | tf_op jit(solution)/shard_map/ppermute | solution.py:259
  110.9 0.4 collective-permute-start.4
  111.3 5.0 %collective-permute-start.3 = (f32[8,4,128]{2,1,0:T(4,128)S(1)}, f32[8,4,128]{2,1,0:T(4,128)S(1)}, u32[]{:S(2)}, u32[]{:S(2)}) collective-permute-start(f32[8,4,128]{2,1,0:T(4,128)S(1)} %get-tuple-element.17), channel_id=1, source_target_pairs={{0,128},{32,160},{64,192},{96,224},{128,0},{160,32},{192,64},{224,... | collective-permute-start | bytes 49160 | tf_op jit(solution)/shard_map/ppermute | solution.py:259
  116.4 0.0 collective-permute-start.2
  116.4 0.0 collective-permute-done.6
  116.4 2.5 %collective-permute-start.1 = (f32[8,4,128]{2,1,0:T(4,128)S(1)}, f32[8,4,128]{2,1,0:T(4,128)S(1)}, u32[]{:S(2)}, u32[]{:S(2)}) collective-permute-start(f32[8,4,128]{2,1,0:T(4,128)S(1)} %get-tuple-element.15), channel_id=1, source_target_pairs={{0,64},{32,96},{64,128},{96,160},{128,192},{160,224},{192,0},{224,... | collective-permute-start | bytes 49160 | tf_op jit(solution)/shard_map/ppermute | solution.py:259
  118.8 0.0 collective-permute-done.5
  118.8 1.9 %collective-permute-start = (f32[8,4,128]{2,1,0:T(4,128)S(1)}, f32[8,4,128]{2,1,0:T(4,128)S(1)}, u32[]{:S(2)}, u32[]{:S(2)}) collective-permute-start(f32[8,4,128]{2,1,0:T(4,128)S(1)} %get-tuple-element.14), channel_id=1, source_target_pairs={{0,32},{32,64},{64,96},{96,128},{128,160},{160,192},{192,224},{224... | collective-permute-start | bytes 49160 | tf_op jit(solution)/shard_map/ppermute | solution.py:259
  120.8 0.0 collective-permute-done.4
  120.8 0.0 collective-permute-done.3
  120.8 2.4 %collective-permute-done.2 = f32[8,4,128]{2,1,0:T(4,128)S(1)} collective-permute-done((f32[8,4,128]{2,1,0:T(4,128)S(1)}, f32[8,4,128]{2,1,0:T(4,128)S(1)}, u32[]{:S(2)}, u32[]{:S(2)}) %collective-permute-start.2) | collective-permute-done | bytes 16416 | tf_op jit(solution)/shard_map/ppermute | solution.py:259
  123.1 0.0 collective-permute-done.1
  123.1 0.7 collective-permute-done
  123.8 0.8 collective-permute-start.7
  124.6 2.7 %collective-permute-start.8 = (f32[8,4,128]{2,1,0:T(4,128)S(1)}, f32[8,4,128]{2,1,0:T(4,128)S(1)}, u32[]{:S(2)}, u32[]{:S(2)}) collective-permute-start(f32[8,4,128]{2,1,0:T(4,128)S(1)} %bitcast.16), channel_id=1, source_target_pairs={{0,64},{32,96},{64,128},{96,160},{128,192},{160,224},{192,0},{224,... | collective-permute-start | bytes 49160 | tf_op jit(solution)/shard_map/ppermute | solution.py:259
  127.3 1.7 %collective-permute-start.9 = (f32[8,4,128]{2,1,0:T(4,128)S(1)}, f32[8,4,128]{2,1,0:T(4,128)S(1)}, u32[]{:S(2)}, u32[]{:S(2)}) collective-permute-start(f32[8,4,128]{2,1,0:T(4,128)S(1)} %bitcast.17), channel_id=1, source_target_pairs={{0,96},{32,128},{64,160},{96,192},{128,224},{160,0},{192,32},{224,... | collective-permute-start | bytes 49160 | tf_op jit(solution)/shard_map/ppermute | solution.py:259
  128.9 2.6 %collective-permute-start.10 = (f32[8,4,128]{2,1,0:T(4,128)S(1)}, f32[8,4,128]{2,1,0:T(4,128)S(1)}, u32[]{:S(2)}, u32[]{:S(2)}) collective-permute-start(f32[8,4,128]{2,1,0:T(4,128)S(1)} %bitcast.18), channel_id=1, source_target_pairs={{0,128},{32,160},{64,192},{96,224},{128,0},{160,32},{192,64},{224,... | collective-permute-start | bytes 49160 | tf_op jit(solution)/shard_map/ppermute | solution.py:259
  131.5 2.4 %collective-permute-start.11 = (f32[8,4,128]{2,1,0:T(4,128)S(1)}, f32[8,4,128]{2,1,0:T(4,128)S(1)}, u32[]{:S(2)}, u32[]{:S(2)}) collective-permute-start(f32[8,4,128]{2,1,0:T(4,128)S(1)} %bitcast.19), channel_id=1, source_target_pairs={{0,160},{32,192},{64,224},{96,0},{128,32},{160,64},{192,96},{224,1... | collective-permute-start | bytes 49160 | tf_op jit(solution)/shard_map/ppermute | solution.py:259
  134.0 0.0 collective-permute-done.7.rest_1_
  134.0 4.0 %collective-permute-start.12 = (f32[8,4,128]{2,1,0:T(4,128)S(1)}, f32[8,4,128]{2,1,0:T(4,128)S(1)}, u32[]{:S(2)}, u32[]{:S(2)}) collective-permute-start(f32[8,4,128]{2,1,0:T(4,128)S(1)} %bitcast.20), channel_id=1, source_target_pairs={{0,192},{32,224},{64,0},{96,32},{128,64},{160,96},{192,128},{224,1... | collective-permute-start | bytes 49160 | tf_op jit(solution)/shard_map/ppermute | solution.py:259
  138.0 0.0 collective-permute-done.8.rest_2_
  138.0 1.6 %collective-permute-start.13 = (f32[8,4,128]{2,1,0:T(4,128)S(1)}, f32[8,4,128]{2,1,0:T(4,128)S(1)}, u32[]{:S(2)}, u32[]{:S(2)}) collective-permute-start(f32[8,4,128]{2,1,0:T(4,128)S(1)} %bitcast.21), channel_id=1, source_target_pairs={{0,224},{32,0},{64,32},{96,64},{128,96},{160,128},{192,160},{224,1... | collective-permute-start | bytes 49160 | tf_op jit(solution)/shard_map/ppermute | solution.py:259
  139.6 0.0 collective-permute-done.9.rest_3_
  139.6 0.0 collective-permute-done.10.rest_4_
  139.6 0.0 collective-permute-done.12.rest_6_
  139.6 2.1 %collective-permute-done.13.rest_7_ = f32[8,4,128]{2,1,0:T(4,128)S(1)} collective-permute-done((f32[8,4,128]{2,1,0:T(4,128)S(1)}, f32[8,4,128]{2,1,0:T(4,128)S(1)}, u32[]{:S(2)}, u32[]{:S(2)}) %collective-permute-start.13) | collective-permute-done | bytes 16416 | tf_op jit(solution)/shard_map/ppermute | solution.py:259
  141.7 0.7 lay_out.1
  142.4 0.0 all-to-all-done.3
  142.4 0.7 reduce_sum.9
  (9 shorter events, 0.0 us)
Async XLA Ops:
  14.9 1.0 copy-start.1
  18.1 21.3 %all-to-all-start.1 = ((bf16[128,32,128]{2,1,0:T(8,128)(2,1)}), bf16[128,32,128]{2,1,0:T(8,128)(2,1)S(1)}, u32[]{:S(2)}, u32[]{:S(2)}) async-start(bf16[128,32,128]{2,1,0:T(8,128)(2,1)} %serve.1), calls=%async_computation.1 | async-start | bytes 2097152 | tf_op jit(solution)/shard_map/all_to_all | solution.py:281
  39.4 4.6 %copy-start = (bf16[384,128,128]{2,1,0:T(8,128)(2,1)S(1)}, bf16[384,128,128]{2,1,0:T(8,128)(2,1)}, u32[]{:S(2)}) copy-start(bf16[384,128,128]{2,1,0:T(8,128)(2,1)} %weights.1) | copy-start | bytes 37748740
  43.9 0.9 copy-start.2
  44.9 0.9 copy-start.3
  45.8 0.9 copy-start.4
  46.7 0.7 copy-start.5
  47.4 0.7 copy-start.6
  97.1 45.4 %all-to-all-start.3 = ((f32[32,32,128]{2,1,0:T(8,128)}), f32[32,32,128]{2,1,0:T(8,128)S(1)}, u32[]{:S(2)}, u32[]{:S(2)}) async-start(f32[32,32,128]{2,1,0:T(8,128)} %get-tuple-element.21), calls=%async_computation.3 | async-start | bytes 1048576 | tf_op jit(solution)/shard_map/all_to_all | solution.py:297
  103.5 12.9 %collective-permute-start.6 = (f32[8,4,128]{2,1,0:T(4,128)S(1)}, f32[8,4,128]{2,1,0:T(4,128)S(1)}, u32[]{:S(2)}, u32[]{:S(2)}) collective-permute-start(f32[8,4,128]{2,1,0:T(4,128)S(1)} %get-tuple-element.20), channel_id=1, source_target_pairs={{0,224},{32,0},{64,32},{96,64},{128,96},{160,128},{192,160},{224,1... | collective-permute-start | bytes 49160 | tf_op jit(solution)/shard_map/ppermute | solution.py:259
  109.4 9.4 %collective-permute-start.5 = (f32[8,4,128]{2,1,0:T(4,128)S(1)}, f32[8,4,128]{2,1,0:T(4,128)S(1)}, u32[]{:S(2)}, u32[]{:S(2)}) collective-permute-start(f32[8,4,128]{2,1,0:T(4,128)S(1)} %get-tuple-element.19), channel_id=1, source_target_pairs={{0,192},{32,224},{64,0},{96,32},{128,64},{160,96},{192,128},{224,1... | collective-permute-start | bytes 49160 | tf_op jit(solution)/shard_map/ppermute | solution.py:259
  110.9 9.9 %collective-permute-start.4 = (f32[8,4,128]{2,1,0:T(4,128)S(1)}, f32[8,4,128]{2,1,0:T(4,128)S(1)}, u32[]{:S(2)}, u32[]{:S(2)}) collective-permute-start(f32[8,4,128]{2,1,0:T(4,128)S(1)} %get-tuple-element.18), channel_id=1, source_target_pairs={{0,160},{32,192},{64,224},{96,0},{128,32},{160,64},{192,96},{224,1... | collective-permute-start | bytes 49160 | tf_op jit(solution)/shard_map/ppermute | solution.py:259
  111.3 9.4 %collective-permute-start.3 = (f32[8,4,128]{2,1,0:T(4,128)S(1)}, f32[8,4,128]{2,1,0:T(4,128)S(1)}, u32[]{:S(2)}, u32[]{:S(2)}) collective-permute-start(f32[8,4,128]{2,1,0:T(4,128)S(1)} %get-tuple-element.17), channel_id=1, source_target_pairs={{0,128},{32,160},{64,192},{96,224},{128,0},{160,32},{192,64},{224,... | collective-permute-start | bytes 49160 | tf_op jit(solution)/shard_map/ppermute | solution.py:259
  116.4 6.7 %collective-permute-start.2 = (f32[8,4,128]{2,1,0:T(4,128)S(1)}, f32[8,4,128]{2,1,0:T(4,128)S(1)}, u32[]{:S(2)}, u32[]{:S(2)}) collective-permute-start(f32[8,4,128]{2,1,0:T(4,128)S(1)} %get-tuple-element.16), channel_id=1, source_target_pairs={{0,96},{32,128},{64,160},{96,192},{128,224},{160,0},{192,32},{224,... | collective-permute-start | bytes 49160 | tf_op jit(solution)/shard_map/ppermute | solution.py:259
  116.4 6.7 %collective-permute-start.1 = (f32[8,4,128]{2,1,0:T(4,128)S(1)}, f32[8,4,128]{2,1,0:T(4,128)S(1)}, u32[]{:S(2)}, u32[]{:S(2)}) collective-permute-start(f32[8,4,128]{2,1,0:T(4,128)S(1)} %get-tuple-element.15), channel_id=1, source_target_pairs={{0,64},{32,96},{64,128},{96,160},{128,192},{160,224},{192,0},{224,... | collective-permute-start | bytes 49160 | tf_op jit(solution)/shard_map/ppermute | solution.py:259
  118.8 5.0 %collective-permute-start = (f32[8,4,128]{2,1,0:T(4,128)S(1)}, f32[8,4,128]{2,1,0:T(4,128)S(1)}, u32[]{:S(2)}, u32[]{:S(2)}) collective-permute-start(f32[8,4,128]{2,1,0:T(4,128)S(1)} %get-tuple-element.14), channel_id=1, source_target_pairs={{0,32},{32,64},{64,96},{96,128},{128,160},{160,192},{192,224},{224... | collective-permute-start | bytes 49160 | tf_op jit(solution)/shard_map/ppermute | solution.py:259
  123.8 10.2 %collective-permute-start.7 = (f32[8,4,128]{2,1,0:T(4,128)S(1)}, f32[8,4,128]{2,1,0:T(4,128)S(1)}, u32[]{:S(2)}, u32[]{:S(2)}) collective-permute-start(f32[8,4,128]{2,1,0:T(4,128)S(1)} %bitcast.15), channel_id=1, source_target_pairs={{0,32},{32,64},{64,96},{96,128},{128,160},{160,192},{192,224},{224... | collective-permute-start | bytes 49160 | tf_op jit(solution)/shard_map/ppermute | solution.py:259
  124.6 13.4 %collective-permute-start.8 = (f32[8,4,128]{2,1,0:T(4,128)S(1)}, f32[8,4,128]{2,1,0:T(4,128)S(1)}, u32[]{:S(2)}, u32[]{:S(2)}) collective-permute-start(f32[8,4,128]{2,1,0:T(4,128)S(1)} %bitcast.16), channel_id=1, source_target_pairs={{0,64},{32,96},{64,128},{96,160},{128,192},{160,224},{192,0},{224,... | collective-permute-start | bytes 49160 | tf_op jit(solution)/shard_map/ppermute | solution.py:259
  127.3 12.3 %collective-permute-start.9 = (f32[8,4,128]{2,1,0:T(4,128)S(1)}, f32[8,4,128]{2,1,0:T(4,128)S(1)}, u32[]{:S(2)}, u32[]{:S(2)}) collective-permute-start(f32[8,4,128]{2,1,0:T(4,128)S(1)} %bitcast.17), channel_id=1, source_target_pairs={{0,96},{32,128},{64,160},{96,192},{128,224},{160,0},{192,32},{224,... | collective-permute-start | bytes 49160 | tf_op jit(solution)/shard_map/ppermute | solution.py:259
  128.9 10.6 %collective-permute-start.10 = (f32[8,4,128]{2,1,0:T(4,128)S(1)}, f32[8,4,128]{2,1,0:T(4,128)S(1)}, u32[]{:S(2)}, u32[]{:S(2)}) collective-permute-start(f32[8,4,128]{2,1,0:T(4,128)S(1)} %bitcast.18), channel_id=1, source_target_pairs={{0,128},{32,160},{64,192},{96,224},{128,0},{160,32},{192,64},{224,... | collective-permute-start | bytes 49160 | tf_op jit(solution)/shard_map/ppermute | solution.py:259
  131.5 8.0 %collective-permute-start.11 = (f32[8,4,128]{2,1,0:T(4,128)S(1)}, f32[8,4,128]{2,1,0:T(4,128)S(1)}, u32[]{:S(2)}, u32[]{:S(2)}) collective-permute-start(f32[8,4,128]{2,1,0:T(4,128)S(1)} %bitcast.19), channel_id=1, source_target_pairs={{0,160},{32,192},{64,224},{96,0},{128,32},{160,64},{192,96},{224,1... | collective-permute-start | bytes 49160 | tf_op jit(solution)/shard_map/ppermute | solution.py:259
  134.0 5.6 %collective-permute-start.12 = (f32[8,4,128]{2,1,0:T(4,128)S(1)}, f32[8,4,128]{2,1,0:T(4,128)S(1)}, u32[]{:S(2)}, u32[]{:S(2)}) collective-permute-start(f32[8,4,128]{2,1,0:T(4,128)S(1)} %bitcast.20), channel_id=1, source_target_pairs={{0,192},{32,224},{64,0},{96,32},{128,64},{160,96},{192,128},{224,1... | collective-permute-start | bytes 49160 | tf_op jit(solution)/shard_map/ppermute | solution.py:259
  138.0 3.7 %collective-permute-start.13 = (f32[8,4,128]{2,1,0:T(4,128)S(1)}, f32[8,4,128]{2,1,0:T(4,128)S(1)}, u32[]{:S(2)}, u32[]{:S(2)}) collective-permute-start(f32[8,4,128]{2,1,0:T(4,128)S(1)} %bitcast.21), channel_id=1, source_target_pairs={{0,224},{32,0},{64,32},{96,64},{128,96},{160,128},{192,160},{224,1... | collective-permute-start | bytes 49160 | tf_op jit(solution)/shard_map/ppermute | solution.py:259

commit v2 on v1

v2 whole, which is shorter than its diff:
```python
import math

import jax
import jax.numpy as jnp
from jax import lax
from jax.experimental import pallas as pl
from jax.experimental.pallas import tpu as pltpu
from jax.sharding import PartitionSpec as P

F = 32
BLK = 128
ACELL = 128
OCELL = 128
CAP = 4
ITERS = 8

ref_height = 10.0
karman = 0.4
buoyancy = 0.5
flux_scale = 40.0

GROUP = 64
FLUX_ROWS = 64
PARTS = 6
MIB = 1 << 20
VMEM = pltpu.VMEM
SMEM = pltpu.SMEM

ARCTAN = (
    0.9999999952,
    -0.3333319239,
    0.1999324926,
    -0.1416585733,
    0.1012280370,
    -0.0507783010,
)


def arctan_half(t):
    z = t * t
    total = jnp.full_like(z, ARCTAN[-1])
    for c in ARCTAN[-2::-1]:
        total = total * z + c
    return total * t


def flux_rows(mapped_u, mapped_v, mapped_t, mapped_q, surf_temp, surf_hum, hum_factor, log_mom):
    wind_u = 6.0 * mapped_u
    wind_v = 6.0 * mapped_v
    square_speed = wind_u * wind_u + wind_v * wind_v + 1.0
    wind_speed = jnp.sqrt(square_speed)
    temp_diff = mapped_t - surf_temp
    hum_diff = (mapped_q - surf_hum) * hum_factor
    log_heat = log_mom + math.log(10.0)
    gain = (ref_height * buoyancy) * (temp_diff + 0.2 * hum_diff) / square_speed
    from_mom = log_mom
    from_heat = log_heat
    for sweep in range(ITERS):
        stability = jnp.clip(gain * from_mom * from_mom / from_heat, -5.0, 1.0)
        unstable = jnp.minimum(stability, 0.0)
        square = jnp.sqrt(1.0 - 16.0 * unstable)
        root = jnp.sqrt(square)
        half_square = 0.5 + 0.5 * square
        half_root = 0.5 + 0.5 * root
        log_square = jnp.log(half_square)
        log_both = jnp.log(half_root * half_root * half_square)
        turn = arctan_half((root - 1.0) / (root + 1.0))
        stable = stability >= 0.0
        psi_stable = -5.0 * stability
        psi_mom = jnp.where(stable, psi_stable, log_both - 2.0 * turn)
        psi_heat = jnp.where(stable, psi_stable, 2.0 * log_square)
        from_mom = log_mom - psi_mom
        from_heat = log_heat - psi_heat
    fric_vel = karman * wind_speed / from_mom
    drag = flux_scale * fric_vel * fric_vel / wind_speed
    carry = -flux_scale * karman * fric_vel / from_heat
    return drag * wind_u, drag * wind_v, carry * temp_diff, carry * hum_diff


def serve_body(requests, fields, out):
    def owner(d, _):
        for c in range(CAP):
            out[d * CAP + c] = fields[requests[d, c]]
        return 0

    lax.fori_loop(0, out.shape[0] // CAP, owner, 0)


def serve(requests, fields):
    return pl.pallas_call(
        serve_body,
        out_shape=jax.ShapeDtypeStruct((requests.size,) + fields.shape[1:], fields.dtype),
        in_specs=[pl.BlockSpec(memory_space=SMEM), pl.BlockSpec(memory_space=VMEM)],
        out_specs=pl.BlockSpec(memory_space=VMEM),
        compiler_params=pltpu.CompilerParams(vmem_limit_bytes=8 * MIB),
        name="serve",
    )(requests, fields)


def prep_body(weights, ocean_cell, surf_temp, surf_hum, held, turned, hot, temp, hum, cells, sem, part_sem):
    small = [
        pltpu.make_async_copy(ocean_cell, cells, sem.at[0]),
        pltpu.make_async_copy(surf_temp, temp, sem.at[1]),
        pltpu.make_async_copy(surf_hum, hum, sem.at[2]),
    ]
    blocks = held.shape[0]
    share = blocks // PARTS
    large = [
        pltpu.make_async_copy(
            weights.at[pl.ds(p * share, share)], held.at[pl.ds(p * share, share)], part_sem.at[p]
        )
        for p in range(PARTS)
    ]
    for copy in small + large:
        copy.start()
    small[0].wait()
    target = lax.broadcasted_iota(jnp.int32, (OCELL, BLK), 0)

    def spread(g, _):
        first = pl.multiple_of(g * 16, 16)
        rows = cells[pl.ds(first, 16), :]
        for i in range(16):
            hot[first + i] = jnp.where(target == rows[i : i + 1], 1.0, 0.0).astype(jnp.bfloat16).T
        return 0

    lax.fori_loop(0, blocks // 16, spread, 0)
    for p in range(PARTS):
        large[p].wait()

        def turn(g, _):
            first = p * share + g * 16
            for i in range(16):
                turned[first + i] = held[first + i].T
            return 0

        lax.fori_loop(0, share // 16, turn, 0)
    small[1].wait()
    small[2].wait()


def prep(weights, ocean_cell, surf_temp, surf_hum):
    blocks = weights.shape[0]
    square = pltpu.VMEM((blocks, BLK, ACELL), jnp.bfloat16)
    flat = pltpu.VMEM(surf_temp.shape, jnp.float32)
    return pl.pallas_call(
        prep_body,
        out_shape=(square, square, square, flat, flat),
        in_specs=[pl.BlockSpec(memory_space=pltpu.HBM)] * 4,
        out_specs=(pl.BlockSpec(memory_space=VMEM),) * 5,
        scratch_shapes=[
            pltpu.VMEM(ocean_cell.shape, jnp.int32),
            pltpu.SemaphoreType.DMA((3,)),
            pltpu.SemaphoreType.DMA((PARTS,)),
        ],
        compiler_params=pltpu.CompilerParams(vmem_limit_bytes=4 * MIB),
        cost_estimate=pl.CostEstimate(
            flops=2 * weights.size, bytes_accessed=4 * weights.size, transcendentals=0
        ),
        name="prep",
    )(weights, ocean_cell, surf_temp, surf_hum)


def two_parts(value):
    high = value.astype(jnp.bfloat16)
    return high, (value - high.astype(jnp.float32)).astype(jnp.bfloat16)


def product(left, right):
    return jnp.dot(left, right, preferred_element_type=jnp.float32)


def sum_rows(picked, values, out, stride):
    entries = picked.shape[1]
    for c in range(4):
        high, low = two_parts(values[pl.ds(c, entries, stride=stride), :])
        out[pl.ds(c, picked.shape[0], stride=4), :] = product(picked, high) + product(picked, low)


def one_hot(index_row, count):
    rows = lax.broadcasted_iota(jnp.int32, (count, index_row.shape[1]), 0)
    return jnp.where(rows == index_row, 1.0, 0.0).astype(jnp.bfloat16)


def flux_body(
    use_slot,
    slot_row,
    table,
    turned,
    held,
    surf_temp,
    surf_hum,
    hum_factor,
    log_mom,
    cell_weight,
    rows,
    slot_sums,
    contrib,
):
    blocks = held.shape[0]

    def map_group(g, _):
        base = g * GROUP
        for i in range(0, GROUP, 2):
            k = base + i
            both = product(
                jnp.concatenate([table[use_slot[k]], table[use_slot[k + 1]]], axis=0),
                jnp.concatenate([turned[k], turned[k + 1]], axis=1),
            )
            rows[pl.ds(pl.multiple_of(k * F, F), F), :] = both[:F, :BLK]
            rows[pl.ds(pl.multiple_of(k * F + F, F), F), :] = both[F:, BLK:]
        return 0

    lax.fori_loop(0, blocks // GROUP, map_group, 0)

    def iterate(g, _):
        mine = pl.ds(pl.multiple_of(g * FLUX_ROWS, FLUX_ROWS), FLUX_ROWS)
        row = lambda f: pl.ds(g * (FLUX_ROWS * F) + f, FLUX_ROWS, stride=F)
        fluxes = flux_rows(
            *(rows[row(f), :] for f in range(4)),
            surf_temp[mine, :],
            surf_hum[mine, :],
            hum_factor[mine, :],
            log_mom[mine, :],
        )
        weight = cell_weight[mine, :]
        for f in range(4):
            rows[row(f), :] = weight * fluxes[f]
        return 0

    lax.fori_loop(0, blocks // FLUX_ROWS, iterate, 0)

    def contribute(g, _):
        base = g * GROUP
        for i in range(0, GROUP, 2):
            k = base + i
            left = jnp.concatenate(
                [
                    rows[pl.ds(pl.multiple_of(k * F, F), 8), :],
                    rows[pl.ds(pl.multiple_of(k * F + F, F), 8), :],
                ],
                axis=0,
            ).astype(jnp.bfloat16)
            both = product(left, jnp.concatenate([held[k], held[k + 1]], axis=1))
            contrib[pl.ds(pl.multiple_of(k * 8, 8), 8), :] = both[:8, :ACELL]
            contrib[pl.ds(pl.multiple_of(k * 8 + 8, 8), 8), :] = both[8:, ACELL:]
        return 0

    lax.fori_loop(0, blocks // GROUP, contribute, 0)
    sum_rows(one_hot(slot_row[...], table.shape[0]), contrib, slot_sums, 8)


def fluxes_of(use_slot, table, turned, held, temp, hum, cells):
    blocks = held.shape[0]
    here = pl.BlockSpec(memory_space=VMEM)
    pinned = [pltpu.with_memory_space_constraint(x, VMEM) for x in (turned, held, temp, hum)]
    return pl.pallas_call(
        flux_body,
        out_shape=(
            pltpu.VMEM((blocks * F, BLK), jnp.float32),
            jax.ShapeDtypeStruct((table.shape[0] * 4, ACELL), jnp.float32),
        ),
        in_specs=[pl.BlockSpec(memory_space=SMEM)] + [here] * 9,
        out_specs=(here, here),
        scratch_shapes=[pltpu.VMEM((blocks * 8, ACELL), jnp.float32)],
        compiler_params=pltpu.CompilerParams(vmem_limit_bytes=8 * MIB),
        name="fluxes",
    )(use_slot, use_slot.reshape(1, -1), table, *pinned, *cells)


def ocean_body(ocean_block, rows, hot, passive_weight, ocean_sums, partial):
    ocean_sums[...] = jnp.zeros_like(ocean_sums)
    is_flux = lax.broadcasted_iota(jnp.int32, (8, BLK), 0) < 4

    def group(g, _):
        base = g * GROUP
        for i in range(GROUP):
            k = base + i
            factor = passive_weight[pl.ds(k, 1), :]
            value = rows[pl.ds(pl.multiple_of(k * F, F), F), :]
            value = jnp.concatenate(
                [jnp.where(is_flux, value[:8], value[:8] * factor), value[8:] * factor], axis=0
            )
            both = product(jnp.concatenate(two_parts(value), axis=0), hot[k])
            partial[i * F : (i + 1) * F, :] = both[:F] + both[F:]
        for i in range(GROUP):
            target = ocean_block[base + i]
            ocean_sums[target] = ocean_sums[target] + partial[i * F : (i + 1) * F, :]
        return 0

    lax.fori_loop(0, rows.shape[0] // F // GROUP, group, 0)


def ocean_of(ocean_block, rows, hot, passive_weight, owners):
    here = pl.BlockSpec(memory_space=VMEM)
    pinned = [pltpu.with_memory_space_constraint(x, VMEM) for x in (rows, hot)]
    return pl.pallas_call(
        ocean_body,
        out_shape=jax.ShapeDtypeStruct((owners, F, OCELL), jnp.float32),
        in_specs=[pl.BlockSpec(memory_space=SMEM)] + [here] * 3,
        out_specs=here,
        scratch_shapes=[pltpu.VMEM((GROUP * F, OCELL), jnp.float32)],
        compiler_params=pltpu.CompilerParams(vmem_limit_bytes=8 * MIB),
        cost_estimate=pl.CostEstimate(
            flops=128 * rows.size, bytes_accessed=12 * rows.size, transcendentals=0
        ),
        name="ocean",
    )(ocean_block, *pinned, passive_weight)


def owner_body(request_row, returned, out):
    sum_rows(one_hot(request_row[...], out.shape[0] // 4), returned, out, 4)


def owner_sums_of(requests, returned, local_blocks):
    here = pl.BlockSpec(memory_space=VMEM)
    return pl.pallas_call(
        owner_body,
        out_shape=jax.ShapeDtypeStruct((local_blocks * 4, ACELL), jnp.float32),
        in_specs=[here, here],
        out_specs=here,
        compiler_params=pltpu.CompilerParams(vmem_limit_bytes=8 * MIB),
        name="owner_sums",
    )(requests.reshape(1, -1), returned)


def sum_over(x, axis):
    ranks = lax.axis_size(axis)
    bit = 1
    while bit < ranks:
        x = x + lax.ppermute(x, axis, [(i, i ^ bit) for i in range(ranks)])
        bit *= 2
    return x


def per_device(
    atm_fields,
    weights,
    surf_temp,
    surf_hum,
    roughness,
    cell_area,
    need_list,
    use_slot,
    ocean_block,
    ocean_cell,
    cell_count,
    ice_mask,
):
    owners = lax.axis_size("atm")
    local_blocks = atm_fields.shape[0]
    requests = lax.all_to_all(need_list[0], "atm", split_axis=0, concat_axis=0, tiled=True)
    table = lax.all_to_all(serve(requests, atm_fields), "atm", split_axis=0, concat_axis=0, tiled=True)
    held, turned, hot, temp, hum = prep(weights, ocean_cell, surf_temp, surf_hum)
    ice_frac = ice_mask.astype(jnp.float32)
    is_live = jnp.arange(BLK, dtype=jnp.int32)[None, :] < cell_count[:, None]
    cell_weight = jnp.where(is_live, cell_area, 0.0)
    cells = (1.0 - 0.6 * ice_frac, jnp.log(ref_height / roughness), cell_weight)
    passive_weight = cell_weight * (1.0 - 0.7 * ice_frac)
    rows, slot_sums = fluxes_of(use_slot, table, turned, held, temp, hum, cells)
    returned = lax.all_to_all(slot_sums, "atm", split_axis=0, concat_axis=0, tiled=True)
    ocean_sums = ocean_of(ocean_block, rows, hot, passive_weight, owners)
    ocean_parts = lax.all_to_all(ocean_sums, "atm", split_axis=0, concat_axis=0, tiled=True)
    owner_sums = owner_sums_of(requests, returned, local_blocks)
    atm_flux = sum_over(owner_sums, "ocn").reshape(local_blocks, 4, ACELL)
    ocean_flux = jnp.sum(ocean_parts, axis=0, keepdims=True)
    return (atm_flux, ocean_flux)


def solution(mesh):
    placed = (
        P("atm", None, None),
        P(("ocn", "atm"), None, None),
        P(("ocn", "atm"), None),
        P(("ocn", "atm"), None),
        P(("ocn", "atm"), None),
        P(("ocn", "atm"), None),
        P(("ocn", "atm"), None, None),
        P(("ocn", "atm")),
        P(("ocn", "atm")),
        P(("ocn", "atm"), None),
        P(("ocn", "atm")),
        P(("ocn", "atm"), None),
    )
    return jax.shard_map(
        per_device,
        mesh=mesh,
        in_specs=placed,
        out_specs=(P("atm", None, None), P(("ocn", "atm"), None, None)),
        check_vma=False,
    )
```

time: 144 us -> 138 us (0.958)
  local copies, waits for them, and re-layouts: 10.5 us -> 43.2 us
  blocking collectives: 25.8 us -> 13.6 us
  starting transfers between devices: 43 us -> 31.5 us
  Pallas kernels: 41 us -> 30.8 us
  waiting for transfers between devices: 19.3 us -> 15.1 us
    unnamed x14 -> x38, local copies, waits for them, and re-layouts: 9.76 us -> 41.1 us
    ppermute x14 -> x3, starting transfers between devices: 33 us -> 11.6 us  [sum_over(): x = x + lax.ppermute(x, axis, [(i, i ^ bit) for i in range(ranks)])]
    all_to_all x1, waiting for transfers between devices: 14.1 us -> 0.01 us  [per_device(): lax.all_to_all(serve(requests, atm_fields), 'atm', split_axis=0, concat_a...]
    all_to_all x1 -> x0, blocking collectives: 12.2 us -> none  [per_device(): lax.all_to_all(slot_sums, 'atm', split_axis=0, concat_axis=0, tiled=True)]
    pallas_call x3 -> x4, Pallas kernels: 38.9 us -> 28.7 us  [the longest x1 12 us: fluxes_of(): pl.pallas_call(flux_body, out_shape=(pltpu.VMEM((blocks * F, BLK), jnp.fl...]
    ppermute x14 -> x3, waiting for transfers between devices: 5.2 us -> 15.1 us  [sum_over(): x = x + lax.ppermute(x, axis, [(i, i ^ bit) for i in range(ranks)])]
    all_to_all x0 -> x1, starting transfers between devices: none -> 7.47 us  [per_device(): lax.all_to_all(slot_sums, 'atm', split_axis=0, concat_axis=0, tiled=True)]
    all_to_all x1, starting transfers between devices: 5 us -> 7.38 us  [per_device(): lax.all_to_all(ocean_sums, 'atm', split_axis=0, concat_axis=0, tiled=True)]
  transfers between devices with their start and end apart: 16 -> 6, of which waited for: 4 -> 3; matrix products, arithmetic and copies ran while one was open for 1% -> 2% of each run, Pallas kernels for 1% -> 12%
where the time goes in v2:
time: 138 us; the launch traced here: 137 us
  local copies, waits for them, and re-layouts  43.2 us (31%)
  starting transfers between devices  31.5 us (23%)
  Pallas kernels  30.8 us (22%)
  waiting for transfers between devices  15.1 us (11%)
  blocking collectives  13.6 us (10%)
  other arithmetic  2.16 us (2%)
    unnamed x38, local copies, waits for them, and re-layouts  41.1 us
    ppermute x3, waiting for transfers between devices, sum_over(): x = x + lax.ppermute(x, axis, [(i, i ^ bit) for i in range(ranks)])  15.1 us
    all_to_all x1, blocking collectives, per_device(): lax.all_to_all(need_list[0], 'atm', split_axis=0, concat_axis=0, tiled=True)  13.6 us
    pallas_call x1, Pallas kernels, fluxes_of(): pl.pallas_call(flux_body, out_shape=(pltpu.VMEM((blocks * F, BLK), jnp.fl...  12 us
    ppermute x3, starting transfers between devices, sum_over(): x = x + lax.ppermute(x, axis, [(i, i ^ bit) for i in range(ranks)])  11.6 us
    pallas_call x1, Pallas kernels, prep(): pl.pallas_call(prep_body, out_shape=(square, square, square, flat, flat),...  10.8 us
    all_to_all x1, starting transfers between devices, per_device(): lax.all_to_all(slot_sums, 'atm', split_axis=0, concat_axis=0, tiled=True)  7.47 us
    all_to_all x1, starting transfers between devices, per_device(): lax.all_to_all(ocean_sums, 'atm', split_axis=0, concat_axis=0, tiled=True)  7.38 us
  transfers between devices with their start and end apart: 6, of which 3 were waited for; matrix products, arithmetic and copies ran while one was open for 2% of the time, Pallas kernels for 12%

profile of v2, /device:TPU:2, one launch (start us, length us, event | category | flops | bytes accessed | tf_op | source)
XLA Modules:
  0.0 137.2 jit_solution(3890821430971071061)
XLA Ops:
  0.6 0.0 copy-start.13
  0.6 0.0 copy-start.18
  0.7 0.8 copy.18
  1.4 13.6 %all_to_all.32 = s32[32,1,4]{2,1,0:T(1,128)S(1)} all-to-all(s32[32,1,4]{2,1,0:T(1,128)S(1)} %copy.18), channel_id=1, replica_groups=mesh['ocn'=8,'atm'=32] {'atm'}, dimensions={0} | all-to-all | bytes 1024 | tf_op jit(solution)/shard_map/all_to_all | solution.py:351
  15.0 1.0 copy-done.9
  16.0 2.1 %serve.1 = bf16[128,32,128]{2,1,0:T(8,128)(2,1)} custom-call(s32[32,4]{1,0:T(8,128)S(1)} %bitcast.7, bf16[64,32,128]{2,1,0:T(8,128)(2,1)S(1)} %copy-done.9), custom_call_target="tpu_custom_call" | custom-call | tf_op jit(solution)/shard_map/serve/pallas_call | solution.py:90
  18.1 5.0 %all-to-all-start.1 = ((bf16[128,32,128]{2,1,0:T(8,128)(2,1)}), bf16[128,32,128]{2,1,0:T(8,128)(2,1)S(1)}, u32[]{:S(2)}, u32[]{:S(2)}) async-start(bf16[128,32,128]{2,1,0:T(8,128)(2,1)} %serve.1), calls=%async_computation.1 | async-start | bytes 2097152 | tf_op jit(solution)/shard_map/all_to_all | solution.py:352
  23.2 0.7 reshape.21.slot_row
  23.9 4.6 %copy-done = bf16[384,128,128]{2,1,0:T(8,128)(2,1)S(1)} copy-done((bf16[384,128,128]{2,1,0:T(8,128)(2,1)S(1)}, bf16[384,128,128]{2,1,0:T(8,128)(2,1)}, u32[]{:S(2)}) %copy-start) | copy-done | bytes 12582936
  28.4 0.9 copy-done.10
  29.4 0.9 copy-done.11
  30.3 0.9 copy-done.12
  31.2 10.8 %prep.1 = (bf16[384,128,128]{2,1,0:T(8,128)(2,1)S(1)}, bf16[384,128,128]{2,1,0:T(8,128)(2,1)S(1)}, bf16[384,128,128]{2,1,0:T(8,128)(2,1)S(1)}, f32[384,128]{1,0:T(8,128)S(1)}, f32[384,128]{1,0:T(8,128)S(1)}) custom-call(bf16[384,128,128]{2,1,0:T(8,128)(2,1)S(1)} %copy-done, s32[384,128]{1,0:T(8,128)S(1)} %copy-done.10, f32[384,128]{1,0:T(8,128)S(1)} %copy-done.11, ...), custom_call_target="tpu_custom_call" | custom-call | flops 12582912 | bytes 25165824 | tf_op jit(solution)/shard_map/prep/pallas_call | solution.py:145
  42.1 0.0 copy-start.1
  42.1 4.5 %copy-done.1 = bf16[384,128,128]{2,1,0:T(8,128)(2,1)} copy-done((bf16[384,128,128]{2,1,0:T(8,128)(2,1)}, bf16[384,128,128]{2,1,0:T(8,128)(2,1)S(1)}, u32[]{:S(2)}) %copy-start.1) | copy-done | bytes 12582936
  46.6 4.6 %copy-done.3 = bf16[384,128,128]{2,1,0:T(8,128)(2,1)} copy-done((bf16[384,128,128]{2,1,0:T(8,128)(2,1)}, bf16[384,128,128]{2,1,0:T(8,128)(2,1)S(1)}, u32[]{:S(2)}) %copy-start.3) | copy-done | bytes 12582936
  51.2 4.5 %copy-done.5 = bf16[384,128,128]{2,1,0:T(8,128)(2,1)} copy-done((bf16[384,128,128]{2,1,0:T(8,128)(2,1)}, bf16[384,128,128]{2,1,0:T(8,128)(2,1)S(1)}, u32[]{:S(2)}) %copy-start.5) | copy-done | bytes 12582936
  55.7 0.0 copy-done.18
  55.7 0.0 copy-done.15
  55.7 0.0 copy-done.16
  55.7 0.0 copy-done.17
  55.7 0.1 subtract_multiply_fusion
  55.8 0.0 all-to-all-done.1.table
  55.9 4.6 %copy-done.4 = bf16[384,128,128]{2,1,0:T(8,128)(2,1)S(1)} copy-done((bf16[384,128,128]{2,1,0:T(8,128)(2,1)S(1)}, bf16[384,128,128]{2,1,0:T(8,128)(2,1)}, u32[]{:S(2)}) %copy-start.4) | copy-done | bytes 12582936
  60.4 4.6 %copy-done.6 = bf16[384,128,128]{2,1,0:T(8,128)(2,1)S(1)} copy-done((bf16[384,128,128]{2,1,0:T(8,128)(2,1)S(1)}, bf16[384,128,128]{2,1,0:T(8,128)(2,1)}, u32[]{:S(2)}) %copy-start.6) | copy-done | bytes 12582936
  65.0 12.0 %fluxes.1 = (f32[12288,128]{1,0:T(8,128)S(1)}, f32[512,128]{1,0:T(8,128)}) custom-call(s32[384]{0:T(512)S(1)} %copy-done.13, s32[1,384]{1,0:T(1,128)S(1)} %reshape.21.slot_row, bf16[128,32,128]{2,1,0:T(8,128)(2,1)S(1)} %all-to-all-done.1.table, bf16[384,128,128]{2,1,0:T(8,128)(2,1)S(1)} %copy-done.6, bf16[384,128,128]{2,1,0:T(8,128)(2,1)S(1)} %copy-done.4, ...), custom_call_target="tpu_custom_call" | custom-call | tf_op jit(solution)/shard_map/fluxes/pallas_call | solution.py:256
  77.1 2.6 %copy-done.7 = f32[12288,128]{1,0:T(8,128)} copy-done((f32[12288,128]{1,0:T(8,128)}, f32[12288,128]{1,0:T(8,128)S(1)}, u32[]{:S(2)}) %copy-start.7) | copy-done | bytes 6291480
  79.6 7.5 %all-to-all-start.2 = ((f32[32,16,128]{2,1,0:T(8,128)}), f32[32,16,128]{2,1,0:T(8,128)S(1)}, u32[]{:S(2)}, u32[]{:S(2)}) async-start(f32[32,16,128]{2,1,0:T(8,128)} %bitcast.2), calls=%async_computation.2 | async-start | bytes 524288 | tf_op jit(solution)/shard_map/all_to_all | solution.py:360
  87.1 0.0 copy-done.14
  87.1 0.0 copy-start.2
  87.2 4.6 %copy-done.2 = bf16[384,128,128]{2,1,0:T(8,128)(2,1)S(1)} copy-done((bf16[384,128,128]{2,1,0:T(8,128)(2,1)S(1)}, bf16[384,128,128]{2,1,0:T(8,128)(2,1)}, u32[]{:S(2)}) %copy-start.2) | copy-done | bytes 12582936
  91.7 2.8 %copy-done.8 = f32[12288,128]{1,0:T(8,128)S(1)} copy-done((f32[12288,128]{1,0:T(8,128)S(1)}, f32[12288,128]{1,0:T(8,128)}, u32[]{:S(2)}) %copy-start.8) | copy-done | bytes 6291480
  94.5 5.6 %ocean.1 = f32[32,32,128]{2,1,0:T(8,128)} custom-call(s32[384]{0:T(512)S(1)} %copy-done.14, f32[12288,128]{1,0:T(8,128)S(1)} %copy-done.8, bf16[384,128,128]{2,1,0:T(8,128)(2,1)S(1)} %copy-done.2, f32[384,128]{1,0:T(8,128)S(1)} %get-tuple-element.16.passive_weight), custom_call_target="tpu_custom_call" | custom-call | flops 201326592 | bytes 18874368 | tf_op jit(solution)/shard_map/ocean/pallas_call | solution.py:296
  100.1 0.0 all-to-all-done.2
  100.1 7.4 %all-to-all-start.3 = ((f32[32,32,128]{2,1,0:T(8,128)}), f32[32,32,128]{2,1,0:T(8,128)S(1)}, u32[]{:S(2)}, u32[]{:S(2)}) async-start(f32[32,32,128]{2,1,0:T(8,128)} %ocean.1), calls=%async_computation.3 | async-start | bytes 1048576 | tf_op jit(solution)/shard_map/all_to_all | solution.py:362
  107.5 0.5 broadcast.10
  108.0 0.7 reduce.3
  108.7 0.1 reshape.20.request_row
  108.8 0.2 owner_sums.1
  109.0 2.0 %collective-permute-start = (f32[256,128]{1,0:T(8,128)S(1)}, f32[256,128]{1,0:T(8,128)S(1)}, u32[]{:S(2)}, u32[]{:S(2)}) collective-permute-start(f32[256,128]{1,0:T(8,128)S(1)} %owner_sums.1), channel_id=1, source_target_pairs={{0,32},{32,0},{64,96},{96,64},{128,160},{160,128},{192,224},{224,1... | collective-permute-start | bytes 393224 | tf_op jit(solution)/shard_map/ppermute | solution.py:330
  111.0 3.8 %collective-permute-done = f32[256,128]{1,0:T(8,128)S(1)} collective-permute-done((f32[256,128]{1,0:T(8,128)S(1)}, f32[256,128]{1,0:T(8,128)S(1)}, u32[]{:S(2)}, u32[]{:S(2)}) %collective-permute-start) | collective-permute-done | bytes 131104 | tf_op jit(solution)/shard_map/ppermute | solution.py:330
  114.9 3.3 %collective-permute-start.1 = (f32[256,128]{1,0:T(8,128)S(1)}, f32[256,128]{1,0:T(8,128)S(1)}, u32[]{:S(2)}, u32[]{:S(2)}) collective-permute-start(f32[256,128]{1,0:T(8,128)S(1)} %add.9), channel_id=1, source_target_pairs={{0,64},{32,96},{64,0},{96,32},{128,192},{160,224},{192,128},{224,1... | collective-permute-start | bytes 393224 | tf_op jit(solution)/shard_map/ppermute | solution.py:330
  118.2 6.0 %collective-permute-done.1 = f32[256,128]{1,0:T(8,128)S(1)} collective-permute-done((f32[256,128]{1,0:T(8,128)S(1)}, f32[256,128]{1,0:T(8,128)S(1)}, u32[]{:S(2)}, u32[]{:S(2)}) %collective-permute-start.1) | collective-permute-done | bytes 131104 | tf_op jit(solution)/shard_map/ppermute | solution.py:330
  124.2 6.3 %collective-permute-start.2 = (f32[256,128]{1,0:T(8,128)S(1)}, f32[256,128]{1,0:T(8,128)S(1)}, u32[]{:S(2)}, u32[]{:S(2)}) collective-permute-start(f32[256,128]{1,0:T(8,128)S(1)} %add.10), channel_id=1, source_target_pairs={{0,128},{32,160},{64,192},{96,224},{128,0},{160,32},{192,64},{224,... | collective-permute-start | bytes 393224 | tf_op jit(solution)/shard_map/ppermute | solution.py:330
  130.5 0.0 all-to-all-done.3
  130.5 0.7 reduce_sum.9
  131.1 5.3 %collective-permute-done.2 = f32[256,128]{1,0:T(8,128)S(1)} collective-permute-done((f32[256,128]{1,0:T(8,128)S(1)}, f32[256,128]{1,0:T(8,128)S(1)}, u32[]{:S(2)}, u32[]{:S(2)}) %collective-permute-start.2) | collective-permute-done | bytes 131104 | tf_op jit(solution)/shard_map/ppermute | solution.py:330
  136.5 0.7 add.11
  (18 shorter events, 0.1 us)
Async XLA Ops:
  0.6 55.2 %copy-start.13 = (s32[384]{0:T(512)S(1)}, s32[384]{0:T(512)}, u32[]{:S(2)}) copy-start(s32[384]{0:T(512)} %use_slot.1) | copy-start | bytes 4612
  0.6 55.1 %copy-start.18 = (s32[384]{0:T(512)S(1)}, s32[384]{0:T(512)}, u32[]{:S(2)}) copy-start(s32[384]{0:T(512)} %param.22) | copy-start | bytes 4612
  15.0 1.0 copy-start.9
  16.0 39.7 %copy-start.15 = (s32[384,128]{1,0:T(8,128)S(1)}, s32[384,128]{1,0:T(8,128)}, u32[]{:S(2)}) copy-start(s32[384,128]{1,0:T(8,128)} %param.23) | copy-start | bytes 589828
  16.0 39.7 %copy-start.16 = (f32[384,128]{1,0:T(8,128)S(1)}, f32[384,128]{1,0:T(8,128)}, u32[]{:S(2)}) copy-start(f32[384,128]{1,0:T(8,128)} %param.17) | copy-start | bytes 589828
  16.0 39.7 %copy-start.17 = (f32[384,128]{1,0:T(8,128)S(1)}, f32[384,128]{1,0:T(8,128)}, u32[]{:S(2)}) copy-start(f32[384,128]{1,0:T(8,128)} %param.16) | copy-start | bytes 589828
  18.1 37.7 %all-to-all-start.1 = ((bf16[128,32,128]{2,1,0:T(8,128)(2,1)}), bf16[128,32,128]{2,1,0:T(8,128)(2,1)S(1)}, u32[]{:S(2)}, u32[]{:S(2)}) async-start(bf16[128,32,128]{2,1,0:T(8,128)(2,1)} %serve.1), calls=%async_computation.1 | async-start | bytes 2097152 | tf_op jit(solution)/shard_map/all_to_all | solution.py:352
  23.9 4.6 %copy-start = (bf16[384,128,128]{2,1,0:T(8,128)(2,1)S(1)}, bf16[384,128,128]{2,1,0:T(8,128)(2,1)}, u32[]{:S(2)}) copy-start(bf16[384,128,128]{2,1,0:T(8,128)(2,1)} %weights.1) | copy-start | bytes 37748740
  28.4 0.9 copy-start.10
  29.4 0.9 copy-start.11
  30.3 0.9 copy-start.12
  42.1 4.5 %copy-start.1 = (bf16[384,128,128]{2,1,0:T(8,128)(2,1)}, bf16[384,128,128]{2,1,0:T(8,128)(2,1)S(1)}, u32[]{:S(2)}) copy-start(bf16[384,128,128]{2,1,0:T(8,128)(2,1)S(1)} %get-tuple-element.15.hot) | copy-start | bytes 37748740
  46.6 4.6 %copy-start.3 = (bf16[384,128,128]{2,1,0:T(8,128)(2,1)}, bf16[384,128,128]{2,1,0:T(8,128)(2,1)S(1)}, u32[]{:S(2)}) copy-start(bf16[384,128,128]{2,1,0:T(8,128)(2,1)S(1)} %get-tuple-element.10.held) | copy-start | bytes 37748740
  51.2 4.5 %copy-start.5 = (bf16[384,128,128]{2,1,0:T(8,128)(2,1)}, bf16[384,128,128]{2,1,0:T(8,128)(2,1)S(1)}, u32[]{:S(2)}) copy-start(bf16[384,128,128]{2,1,0:T(8,128)(2,1)S(1)} %get-tuple-element.9.turned) | copy-start | bytes 37748740
  55.9 4.6 %copy-start.4 = (bf16[384,128,128]{2,1,0:T(8,128)(2,1)S(1)}, bf16[384,128,128]{2,1,0:T(8,128)(2,1)}, u32[]{:S(2)}) copy-start(bf16[384,128,128]{2,1,0:T(8,128)(2,1)} %copy-done.3) | copy-start | bytes 37748740
  60.4 4.6 %copy-start.6 = (bf16[384,128,128]{2,1,0:T(8,128)(2,1)S(1)}, bf16[384,128,128]{2,1,0:T(8,128)(2,1)}, u32[]{:S(2)}) copy-start(bf16[384,128,128]{2,1,0:T(8,128)(2,1)} %copy-done.5) | copy-start | bytes 37748740
  65.0 22.1 %copy-start.14 = (s32[384]{0:T(512)S(1)}, s32[384]{0:T(512)}, u32[]{:S(2)}) copy-start(s32[384]{0:T(512)} %ocean_block.1) | copy-start | bytes 4612
  77.1 2.6 %copy-start.7 = (f32[12288,128]{1,0:T(8,128)}, f32[12288,128]{1,0:T(8,128)S(1)}, u32[]{:S(2)}) copy-start(f32[12288,128]{1,0:T(8,128)S(1)} %get-tuple-element.14.rows) | copy-start | bytes 18874372
  79.6 20.5 %all-to-all-start.2 = ((f32[32,16,128]{2,1,0:T(8,128)}), f32[32,16,128]{2,1,0:T(8,128)S(1)}, u32[]{:S(2)}, u32[]{:S(2)}) async-start(f32[32,16,128]{2,1,0:T(8,128)} %bitcast.2), calls=%async_computation.2 | async-start | bytes 524288 | tf_op jit(solution)/shard_map/all_to_all | solution.py:360
  87.1 4.6 %copy-start.2 = (bf16[384,128,128]{2,1,0:T(8,128)(2,1)S(1)}, bf16[384,128,128]{2,1,0:T(8,128)(2,1)}, u32[]{:S(2)}) copy-start(bf16[384,128,128]{2,1,0:T(8,128)(2,1)} %copy-done.1) | copy-start | bytes 37748740
  91.7 2.8 %copy-start.8 = (f32[12288,128]{1,0:T(8,128)S(1)}, f32[12288,128]{1,0:T(8,128)}, u32[]{:S(2)}) copy-start(f32[12288,128]{1,0:T(8,128)} %copy-done.7) | copy-start | bytes 18874372
  100.1 30.4 %all-to-all-start.3 = ((f32[32,32,128]{2,1,0:T(8,128)}), f32[32,32,128]{2,1,0:T(8,128)S(1)}, u32[]{:S(2)}, u32[]{:S(2)}) async-start(f32[32,32,128]{2,1,0:T(8,128)} %ocean.1), calls=%async_computation.3 | async-start | bytes 1048576 | tf_op jit(solution)/shard_map/all_to_all | solution.py:362
  109.0 5.8 %collective-permute-start = (f32[256,128]{1,0:T(8,128)S(1)}, f32[256,128]{1,0:T(8,128)S(1)}, u32[]{:S(2)}, u32[]{:S(2)}) collective-permute-start(f32[256,128]{1,0:T(8,128)S(1)} %owner_sums.1), channel_id=1, source_target_pairs={{0,32},{32,0},{64,96},{96,64},{128,160},{160,128},{192,224},{224,1... | collective-permute-start | bytes 393224 | tf_op jit(solution)/shard_map/ppermute | solution.py:330
  114.9 9.3 %collective-permute-start.1 = (f32[256,128]{1,0:T(8,128)S(1)}, f32[256,128]{1,0:T(8,128)S(1)}, u32[]{:S(2)}, u32[]{:S(2)}) collective-permute-start(f32[256,128]{1,0:T(8,128)S(1)} %add.9), channel_id=1, source_target_pairs={{0,64},{32,96},{64,0},{96,32},{128,192},{160,224},{192,128},{224,1... | collective-permute-start | bytes 393224 | tf_op jit(solution)/shard_map/ppermute | solution.py:330
  124.2 12.3 %collective-permute-start.2 = (f32[256,128]{1,0:T(8,128)S(1)}, f32[256,128]{1,0:T(8,128)S(1)}, u32[]{:S(2)}, u32[]{:S(2)}) collective-permute-start(f32[256,128]{1,0:T(8,128)S(1)} %add.10), channel_id=1, source_target_pairs={{0,128},{32,160},{64,192},{96,224},{128,0},{160,32},{192,64},{224,... | collective-permute-start | bytes 393224 | tf_op jit(solution)/shard_map/ppermute | solution.py:330

commit v3 on v2

v3 whole, which is shorter than its diff:
```python
import math

import jax
import jax.numpy as jnp
from jax import lax
from jax.experimental import pallas as pl
from jax.experimental.pallas import tpu as pltpu
from jax.sharding import PartitionSpec as P

F = 32
BLK = 128
ACELL = 128
OCELL = 128
CAP = 4
ITERS = 8

ref_height = 10.0
karman = 0.4
buoyancy = 0.5
flux_scale = 40.0

GROUP = 64
MIB = 1 << 20
VMEM = pltpu.VMEM
SMEM = pltpu.SMEM

ARCTAN = (
    0.9999999952,
    -0.3333319239,
    0.1999324926,
    -0.1416585733,
    0.1012280370,
    -0.0507783010,
)


def arctan_half(t):
    z = t * t
    total = jnp.full_like(z, ARCTAN[-1])
    for c in ARCTAN[-2::-1]:
        total = total * z + c
    return total * t


def flux_rows(mapped_u, mapped_v, mapped_t, mapped_q, surf_temp, surf_hum, hum_factor, log_mom):
    wind_u = 6.0 * mapped_u
    wind_v = 6.0 * mapped_v
    square_speed = wind_u * wind_u + wind_v * wind_v + 1.0
    wind_speed = jnp.sqrt(square_speed)
    temp_diff = mapped_t - surf_temp
    hum_diff = (mapped_q - surf_hum) * hum_factor
    log_heat = log_mom + math.log(10.0)
    gain = (ref_height * buoyancy) * (temp_diff + 0.2 * hum_diff) / square_speed
    from_mom = log_mom
    from_heat = log_heat
    for sweep in range(ITERS):
        stability = jnp.clip(gain * from_mom * from_mom / from_heat, -5.0, 1.0)
        unstable = jnp.minimum(stability, 0.0)
        square = jnp.sqrt(1.0 - 16.0 * unstable)
        root = jnp.sqrt(square)
        half_square = 0.5 + 0.5 * square
        half_root = 0.5 + 0.5 * root
        log_square = jnp.log(half_square)
        log_both = jnp.log(half_root * half_root * half_square)
        turn = arctan_half((root - 1.0) / (root + 1.0))
        stable = stability >= 0.0
        psi_stable = -5.0 * stability
        psi_mom = jnp.where(stable, psi_stable, log_both - 2.0 * turn)
        psi_heat = jnp.where(stable, psi_stable, 2.0 * log_square)
        from_mom = log_mom - psi_mom
        from_heat = log_heat - psi_heat
    fric_vel = karman * wind_speed / from_mom
    drag = flux_scale * fric_vel * fric_vel / wind_speed
    carry = -flux_scale * karman * fric_vel / from_heat
    return drag * wind_u, drag * wind_v, carry * temp_diff, carry * hum_diff


def serve_body(requests, fields, out):
    def owner(d, _):
        for c in range(CAP):
            out[d * CAP + c] = fields[requests[d, c]]
        return 0

    lax.fori_loop(0, out.shape[0] // CAP, owner, 0)


def serve(requests, fields):
    return pl.pallas_call(
        serve_body,
        out_shape=jax.ShapeDtypeStruct((requests.size,) + fields.shape[1:], fields.dtype),
        in_specs=[pl.BlockSpec(memory_space=SMEM), pl.BlockSpec(memory_space=VMEM)],
        out_specs=pl.BlockSpec(memory_space=VMEM),
        compiler_params=pltpu.CompilerParams(vmem_limit_bytes=8 * MIB),
        name="serve",
    )(requests, fields)


def prep_body(ocean_cell, surf_temp, surf_hum, requests, hot, temp, hum, request_row):
    request_row[...] = requests[...]
    temp[...] = surf_temp[...]
    hum[...] = surf_hum[...]
    target = lax.broadcasted_iota(jnp.int32, (OCELL, BLK), 0)
    for i in range(hot.shape[0]):
        hot[i] = jnp.where(target == ocean_cell[i : i + 1, :], 1.0, 0.0).astype(jnp.bfloat16).T


def prep(ocean_cell, surf_temp, surf_hum, requests):
    blocks = ocean_cell.shape[0]
    part = pl.BlockSpec((GROUP, BLK), lambda s: (s, 0))
    flat = jax.ShapeDtypeStruct((blocks, BLK), jnp.float32)
    line = pl.BlockSpec((1, requests.size), lambda s: (0, 0))
    return pl.pallas_call(
        prep_body,
        out_shape=(pltpu.HBM((blocks, BLK, OCELL), jnp.bfloat16), flat, flat, jax.ShapeDtypeStruct((1, requests.size), jnp.int32)),
        grid=(blocks // GROUP,),
        in_specs=[part] * 3 + [line],
        out_specs=(pl.BlockSpec((GROUP, BLK, OCELL), lambda s: (s, 0, 0)), part, part, line),
        compiler_params=pltpu.CompilerParams(vmem_limit_bytes=16 * MIB),
        cost_estimate=pl.CostEstimate(
            flops=2 * blocks * BLK * OCELL,
            bytes_accessed=2 * blocks * BLK * OCELL,
            transcendentals=0,
        ),
        name="prep",
    )(ocean_cell, surf_temp, surf_hum, requests.reshape(1, -1))


def two_parts(value):
    high = value.astype(jnp.bfloat16)
    return high, (value - high.astype(jnp.float32)).astype(jnp.bfloat16)


def product(left, right):
    return jnp.dot(left, right, preferred_element_type=jnp.float32)


def sum_rows(picked, values, out, stride):
    entries = picked.shape[1]
    for c in range(4):
        high, low = two_parts(values[pl.ds(c, entries, stride=stride), :])
        out[pl.ds(c, picked.shape[0], stride=4), :] = product(picked, high) + product(picked, low)


def one_hot(index_row, count):
    rows = lax.broadcasted_iota(jnp.int32, (count, index_row.shape[1]), 0)
    return jnp.where(rows == index_row, 1.0, 0.0).astype(jnp.bfloat16)


def flux_body(
    use_slot,
    slot_row,
    table,
    weights,
    surf_temp,
    surf_hum,
    hum_factor,
    log_mom,
    cell_weight,
    rows_out,
    slot_sums,
    held,
    rows,
    contrib,
    in_sem,
    out_sem,
):
    blocks = held.shape[0]
    parts = blocks // GROUP

    def fetch(p):
        share = pl.ds(pl.multiple_of(p * GROUP, GROUP), GROUP)
        return pltpu.make_async_copy(weights.at[share], held.at[share], in_sem.at[p])

    def put(p):
        share = pl.ds(pl.multiple_of(p * (GROUP * F), GROUP * F), GROUP * F)
        return pltpu.make_async_copy(rows.at[share], rows_out.at[share], out_sem.at[p])

    for p in range(parts):
        fetch(p).start()

    def part(p, _):
        base = p * GROUP
        fetch(p).wait()
        for i in range(0, GROUP, 2):
            k = base + i
            both = lax.dot_general(
                jnp.concatenate([table[use_slot[k]], table[use_slot[k + 1]]], axis=0),
                held[pl.ds(k, 2)].reshape(2 * BLK, ACELL),
                (((1,), (1,)), ((), ())),
                preferred_element_type=jnp.float32,
            )
            rows[pl.ds(pl.multiple_of(k * F, F), F), :] = both[:F, :BLK]
            rows[pl.ds(pl.multiple_of(k * F + F, F), F), :] = both[F:, BLK:]
        mine = pl.ds(pl.multiple_of(base, GROUP), GROUP)
        row = lambda f: pl.ds(base * F + f, GROUP, stride=F)
        fluxes = flux_rows(
            *(rows[row(f), :] for f in range(4)),
            surf_temp[mine, :],
            surf_hum[mine, :],
            hum_factor[mine, :],
            log_mom[mine, :],
        )
        weight = cell_weight[mine, :]
        for f in range(4):
            rows[row(f), :] = weight * fluxes[f]
        put(p).start()
        for i in range(0, GROUP, 2):
            k = base + i
            left = jnp.concatenate(
                [
                    rows[pl.ds(pl.multiple_of(k * F, F), 8), :],
                    rows[pl.ds(pl.multiple_of(k * F + F, F), 8), :],
                ],
                axis=0,
            ).astype(jnp.bfloat16)
            both = product(left, jnp.concatenate([held[k], held[k + 1]], axis=1))
            contrib[pl.ds(pl.multiple_of(k * 8, 8), 8), :] = both[:8, :ACELL]
            contrib[pl.ds(pl.multiple_of(k * 8 + 8, 8), 8), :] = both[8:, ACELL:]
        return 0

    lax.fori_loop(0, parts, part, 0)
    sum_rows(one_hot(slot_row[...], table.shape[0]), contrib, slot_sums, 8)
    for p in range(parts):
        put(p).wait()


def fluxes_of(use_slot, table, weights, cells):
    blocks = weights.shape[0]
    here = pl.BlockSpec(memory_space=VMEM)
    far = pl.BlockSpec(memory_space=pltpu.HBM)
    return pl.pallas_call(
        flux_body,
        out_shape=(
            pltpu.HBM((blocks * F, BLK), jnp.float32),
            jax.ShapeDtypeStruct((table.shape[0] * 4, ACELL), jnp.float32),
        ),
        in_specs=[pl.BlockSpec(memory_space=SMEM), here, here, far] + [here] * 5,
        out_specs=(far, here),
        scratch_shapes=[
            pltpu.VMEM(weights.shape, weights.dtype),
            pltpu.VMEM((blocks * F, BLK), jnp.float32),
            pltpu.VMEM((blocks * 8, ACELL), jnp.float32),
            pltpu.SemaphoreType.DMA((blocks // GROUP,)),
            pltpu.SemaphoreType.DMA((blocks // GROUP,)),
        ],
        compiler_params=pltpu.CompilerParams(vmem_limit_bytes=30 * MIB),
        name="fluxes",
    )(
        use_slot,
        use_slot.reshape(1, -1),
        table,
        pltpu.with_memory_space_constraint(weights, pltpu.HBM),
        *cells,
    )


def ocean_body(ocean_block, rows, hot, passive_weight, ocean_sums, partial):
    step = pl.program_id(0)

    @pl.when(step == 0)
    def _():
        ocean_sums[...] = jnp.zeros_like(ocean_sums)

    is_flux = lax.broadcasted_iota(jnp.int32, (8, BLK), 0) < 4
    for i in range(GROUP):
        factor = passive_weight[i : i + 1, :]
        value = rows[i * F : (i + 1) * F, :]
        value = jnp.concatenate(
            [jnp.where(is_flux, value[:8], value[:8] * factor), value[8:] * factor], axis=0
        )
        both = product(jnp.concatenate(two_parts(value), axis=0), hot[i])
        partial[i * F : (i + 1) * F, :] = both[:F] + both[F:]
    for i in range(GROUP):
        target = ocean_block[step * GROUP + i]
        ocean_sums[target] = ocean_sums[target] + partial[i * F : (i + 1) * F, :]


def ocean_of(ocean_block, rows, hot, passive_weight, owners):
    blocks = hot.shape[0]
    return pl.pallas_call(
        ocean_body,
        out_shape=jax.ShapeDtypeStruct((owners, F, OCELL), jnp.float32),
        grid_spec=pltpu.PrefetchScalarGridSpec(
            num_scalar_prefetch=1,
            grid=(blocks // GROUP,),
            in_specs=[
                pl.BlockSpec((GROUP * F, BLK), lambda s, _: (s, 0)),
                pl.BlockSpec((GROUP, BLK, OCELL), lambda s, _: (s, 0, 0)),
                pl.BlockSpec((GROUP, BLK), lambda s, _: (s, 0)),
            ],
            out_specs=pl.BlockSpec((owners, F, OCELL), lambda s, _: (0, 0, 0)),
            scratch_shapes=[pltpu.VMEM((GROUP * F, OCELL), jnp.float32)],
        ),
        compiler_params=pltpu.CompilerParams(vmem_limit_bytes=16 * MIB),
        cost_estimate=pl.CostEstimate(
            flops=128 * rows.size, bytes_accessed=12 * rows.size, transcendentals=0
        ),
        name="ocean",
    )(
        ocean_block,
        pltpu.with_memory_space_constraint(rows, pltpu.HBM),
        pltpu.with_memory_space_constraint(hot, pltpu.HBM),
        passive_weight,
    )


def owner_body(request_row, returned, out):
    sum_rows(one_hot(request_row[...], out.shape[0] // 4), returned, out, 4)


def owner_sums_of(request_row, returned, local_blocks):
    here = pl.BlockSpec(memory_space=VMEM)
    return pl.pallas_call(
        owner_body,
        out_shape=jax.ShapeDtypeStruct((local_blocks * 4, ACELL), jnp.float32),
        in_specs=[here, here],
        out_specs=here,
        compiler_params=pltpu.CompilerParams(vmem_limit_bytes=8 * MIB),
        name="owner_sums",
    )(request_row, returned)


def sum_over(x, axis):
    ranks = lax.axis_size(axis)
    bit = 1
    while bit < ranks:
        x = x + lax.ppermute(x, axis, [(i, i ^ bit) for i in range(ranks)])
        bit *= 2
    return x


def per_device(
    atm_fields,
    weights,
    surf_temp,
    surf_hum,
    roughness,
    cell_area,
    need_list,
    use_slot,
    ocean_block,
    ocean_cell,
    cell_count,
    ice_mask,
):
    owners = lax.axis_size("atm")
    local_blocks = atm_fields.shape[0]
    requests = lax.all_to_all(need_list[0], "atm", split_axis=0, concat_axis=0, tiled=True)
    table = lax.all_to_all(serve(requests, atm_fields), "atm", split_axis=0, concat_axis=0, tiled=True)
    hot, surf_temp, surf_hum, request_row = prep(ocean_cell, surf_temp, surf_hum, requests)
    ice_frac = ice_mask.astype(jnp.float32)
    is_live = jnp.arange(BLK, dtype=jnp.int32)[None, :] < cell_count[:, None]
    cell_weight = jnp.where(is_live, cell_area, 0.0)
    log_mom = jnp.log(ref_height / roughness)
    cells = (surf_temp, surf_hum, 1.0 - 0.6 * ice_frac, log_mom, cell_weight)
    passive_weight = cell_weight * (1.0 - 0.7 * ice_frac)
    rows, slot_sums = fluxes_of(use_slot, table, weights, cells)
    returned = lax.all_to_all(slot_sums, "atm", split_axis=0, concat_axis=0, tiled=True)
    ocean_sums = ocean_of(ocean_block, rows, hot, passive_weight, owners)
    ocean_parts = lax.all_to_all(ocean_sums, "atm", split_axis=0, concat_axis=0, tiled=True)
    owner_sums = owner_sums_of(request_row, returned, local_blocks)
    atm_flux = sum_over(owner_sums, "ocn").reshape(local_blocks, 4, ACELL)
    ocean_flux = jnp.sum(ocean_parts, axis=0, keepdims=True)
    return (atm_flux, ocean_flux)


def solution(mesh):
    placed = (
        P("atm", None, None),
        P(("ocn", "atm"), None, None),
        P(("ocn", "atm"), None),
        P(("ocn", "atm"), None),
        P(("ocn", "atm"), None),
        P(("ocn", "atm"), None),
        P(("ocn", "atm"), None, None),
        P(("ocn", "atm")),
        P(("ocn", "atm")),
        P(("ocn", "atm"), None),
        P(("ocn", "atm")),
        P(("ocn", "atm"), None),
    )
    return jax.shard_map(
        per_device,
        mesh=mesh,
        in_specs=placed,
        out_specs=(P("atm", None, None), P(("ocn", "atm"), None, None)),
        check_vma=False,
    )
```

time: 138 us -> 105 us (0.76)
  local copies, waits for them, and re-layouts: 43.2 us -> 6.57 us
  waiting for transfers between devices: 15.1 us -> 18.9 us
  starting transfers between devices: 31.5 us -> 29.1 us
  Pallas kernels: 30.8 us -> 32.4 us
    unnamed x38 -> x12, local copies, waits for them, and re-layouts: 41.1 us -> 4.5 us
    pallas_call x1, Pallas kernels: 5.62 us -> 10.6 us  [ocean_of(): pl.pallas_call(ocean_body, out_shape=jax.ShapeDtypeStruct((owners, F, OCE...]
    all_to_all x1, waiting for transfers between devices: 0.01 us -> 3.76 us  [per_device(): lax.all_to_all(serve(requests, atm_fields), 'atm', split_axis=0, concat_a...]
    pallas_call x2, Pallas kernels: 22.9 us -> 19.4 us  [the longest x1 12.9 us: fluxes_of(): pl.pallas_call(flux_body, out_shape=(pltpu.HBM((blocks * F, BLK), jnp.flo...]
    all_to_all x1, starting transfers between devices: 7.47 us -> 5 us  [per_device(): lax.all_to_all(slot_sums, 'atm', split_axis=0, concat_axis=0, tiled=True)]
  transfers between devices with their start and end apart: 6 -> 6, of which waited for: 3 -> 4; matrix products, arithmetic and copies ran while one was open for 2% -> 4% of each run, Pallas kernels for 12% -> 16%
where the time goes in v3:
time: 105 us
  Pallas kernels  32.4 us (31%)
  starting transfers between devices  29.1 us (28%)
  waiting for transfers between devices  18.9 us (18%)
  blocking collectives  13.6 us (13%)
  local copies, waits for them, and re-layouts  6.57 us (6%)
  other arithmetic  3.29 us (3%)
    ppermute x3, waiting for transfers between devices, sum_over(): x = x + lax.ppermute(x, axis, [(i, i ^ bit) for i in range(ranks)])  15.2 us
    all_to_all x1, blocking collectives, per_device(): lax.all_to_all(need_list[0], 'atm', split_axis=0, concat_axis=0, tiled=True)  13.6 us
    pallas_call x1, Pallas kernels, fluxes_of(): pl.pallas_call(flux_body, out_shape=(pltpu.HBM((blocks * F, BLK), jnp.flo...  12.9 us
    ppermute x3, starting transfers between devices, sum_over(): x = x + lax.ppermute(x, axis, [(i, i ^ bit) for i in range(ranks)])  11.6 us
    pallas_call x1, Pallas kernels, ocean_of(): pl.pallas_call(ocean_body, out_shape=jax.ShapeDtypeStruct((owners, F, OCE...  10.6 us
    all_to_all x1, starting transfers between devices, per_device(): lax.all_to_all(ocean_sums, 'atm', split_axis=0, concat_axis=0, tiled=True)  7.49 us
    pallas_call x1, Pallas kernels, prep(): pl.pallas_call(prep_body, out_shape=(pltpu.HBM((blocks, BLK, OCELL), jnp....  6.42 us
    all_to_all x1, starting transfers between devices, per_device(): lax.all_to_all(serve(requests, atm_fields), 'atm', split_axis=0, concat_a...  5.03 us
  transfers between devices with their start and end apart: 6, of which 4 were waited for; matrix products, arithmetic and copies ran while one was open for 4% of the time, Pallas kernels for 16%

profile of v3, /device:TPU:2, one launch (start us, length us, event | category | flops | bytes accessed | tf_op | source)
XLA Modules:
  0.0 104.5 jit_solution(5730107485293088159)
XLA Ops:
  0.6 0.0 copy-start.5
  0.6 0.8 copy.18
  1.4 13.6 %all_to_all.32 = s32[32,1,4]{2,1,0:T(1,128)S(1)} all-to-all(s32[32,1,4]{2,1,0:T(1,128)S(1)} %copy.18), channel_id=1, replica_groups=mesh['ocn'=8,'atm'=32] {'atm'}, dimensions={0} | all-to-all | bytes 1024 | tf_op jit(solution)/shard_map/all_to_all | solution.py:348
  15.0 0.0 copy-start
  15.0 1.0 copy-done
  16.0 2.2 %serve.1 = bf16[128,32,128]{2,1,0:T(8,128)(2,1)} custom-call(s32[32,4]{1,0:T(8,128)S(1)} %bitcast.7, bf16[64,32,128]{2,1,0:T(8,128)(2,1)S(1)} %copy-done), custom_call_target="tpu_custom_call" | custom-call | tf_op jit(solution)/shard_map/serve/pallas_call | solution.py:88
  18.2 5.0 %all-to-all-start.1 = ((bf16[128,32,128]{2,1,0:T(8,128)(2,1)}), bf16[128,32,128]{2,1,0:T(8,128)(2,1)S(1)}, u32[]{:S(2)}, u32[]{:S(2)}) async-start(bf16[128,32,128]{2,1,0:T(8,128)(2,1)} %serve.1), calls=%async_computation.1 | async-start | bytes 2097152 | tf_op jit(solution)/shard_map/all_to_all | solution.py:349
  23.2 0.7 reshape.21.slot_row
  23.9 1.2 %subtract_multiply_fusion = (f32[384,128]{1,0:T(8,128)S(1)}, f32[384,128]{1,0:T(8,128)S(1)}, f32[384,128]{1,0:T(8,128)S(1)}, f32[384,128]{1,0:T(8,128)S(1)}) fusion(s32[384,128]{1,0:T(8,128)} %param.23, f32[384,128]{1,0:T(8,128)} %param.17, s32[384]{0:T(512)} %param.22, f32[384,128]{1,0:T(8,128)} %param.16), kind=kLoop, calls=%fused_computation | loop fusion | flops 442368 | bytes 1377792 | tf_op jit(solution)/shard_map/mul | solution.py:356
  25.2 0.5 broadcast.10
  25.7 0.7 reduce.3
  26.4 0.1 reshape.20.requests
  26.5 0.0 copy-start.1
  26.5 0.9 copy-done.1
  27.4 0.0 copy-start.2
  27.4 0.9 copy-done.2
  28.3 0.0 copy-start.3
  28.3 0.9 copy-done.3
  29.3 6.4 %prep.1 = (bf16[384,128,128]{2,1,0:T(8,128)(2,1)}, f32[384,128]{1,0:T(8,128)S(1)}, f32[384,128]{1,0:T(8,128)S(1)}, s32[1,128]{1,0:T(1,128)S(1)}) custom-call(s32[384,128]{1,0:T(8,128)S(1)} %copy-done.1, f32[384,128]{1,0:T(8,128)S(1)} %copy-done.2, f32[384,128]{1,0:T(8,128)S(1)} %copy-done.3, s32[1,128]{1,0:T(1,128)S(1)} %reshape.20.requests), custom_call_target="tpu_custom_call" | custom-call | flops 12582912 | bytes 12582912 | tf_op jit(solution)/shard_map/prep/pallas_call | solution.py:112
  35.7 3.8 %all-to-all-done.1.table = bf16[128,32,128]{2,1,0:T(8,128)(2,1)S(1)} async-done(((bf16[128,32,128]{2,1,0:T(8,128)(2,1)}), bf16[128,32,128]{2,1,0:T(8,128)(2,1)S(1)}, u32[]{:S(2)}, u32[]{:S(2)}) %all-to-all-start.1) | async-done | bytes 1048608 | tf_op jit(solution)/shard_map/all_to_all | solution.py:349
  39.4 0.0 copy-start.4
  39.4 0.7 copy-done.4
  40.1 12.9 %fluxes.1 = (f32[12288,128]{1,0:T(8,128)}, f32[512,128]{1,0:T(8,128)}) custom-call(s32[384]{0:T(512)S(1)} %copy-done.4, s32[1,384]{1,0:T(1,128)S(1)} %reshape.21.slot_row, bf16[128,32,128]{2,1,0:T(8,128)(2,1)S(1)} %all-to-all-done.1.table, bf16[384,128,128]{2,1,0:T(8,128)(2,1)} %weights.1, f32[384,128]{1,0:T(8,128)S(1)} %get-tuple-element.9.surf_temp, ...), custom_call_target="tpu_custom_call" | custom-call | tf_op jit(solution)/shard_map/fluxes/pallas_call | solution.py:231
  53.1 5.0 %all-to-all-start.2 = ((f32[32,16,128]{2,1,0:T(8,128)}), f32[32,16,128]{2,1,0:T(8,128)S(1)}, u32[]{:S(2)}, u32[]{:S(2)}) async-start(f32[32,16,128]{2,1,0:T(8,128)} %bitcast.2), calls=%async_computation.2 | async-start | bytes 524288 | tf_op jit(solution)/shard_map/all_to_all | solution.py:358
  58.1 0.0 copy-done.5
  58.1 10.6 %ocean.1 = f32[32,32,128]{2,1,0:T(8,128)} custom-call(s32[384]{0:T(512)S(1)} %copy-done.5, f32[12288,128]{1,0:T(8,128)} %get-tuple-element.12.rows, bf16[384,128,128]{2,1,0:T(8,128)(2,1)} %get-tuple-element.13.hot, f32[384,128]{1,0:T(8,128)S(1)} %get-tuple-element.14.passive_weight), custom_call_target="tpu_custom_call" | custom-call | flops 201326592 | bytes 18874368 | tf_op jit(solution)/shard_map/ocean/pallas_call | solution.py:280
  68.7 0.0 all-to-all-done.2
  68.7 7.5 %all-to-all-start.3 = ((f32[32,32,128]{2,1,0:T(8,128)}), f32[32,32,128]{2,1,0:T(8,128)S(1)}, u32[]{:S(2)}, u32[]{:S(2)}) async-start(f32[32,32,128]{2,1,0:T(8,128)} %ocean.1), calls=%async_computation.3 | async-start | bytes 1048576 | tf_op jit(solution)/shard_map/all_to_all | solution.py:360
  76.2 0.2 owner_sums.1
  76.4 2.0 %collective-permute-start = (f32[256,128]{1,0:T(8,128)S(1)}, f32[256,128]{1,0:T(8,128)S(1)}, u32[]{:S(2)}, u32[]{:S(2)}) collective-permute-start(f32[256,128]{1,0:T(8,128)S(1)} %owner_sums.1), channel_id=1, source_target_pairs={{0,32},{32,0},{64,96},{96,64},{128,160},{160,128},{192,224},{224,1... | collective-permute-start | bytes 393224 | tf_op jit(solution)/shard_map/ppermute | solution.py:327
  78.4 3.8 %collective-permute-done = f32[256,128]{1,0:T(8,128)S(1)} collective-permute-done((f32[256,128]{1,0:T(8,128)S(1)}, f32[256,128]{1,0:T(8,128)S(1)}, u32[]{:S(2)}, u32[]{:S(2)}) %collective-permute-start) | collective-permute-done | bytes 131104 | tf_op jit(solution)/shard_map/ppermute | solution.py:327
  82.2 3.4 %collective-permute-start.1 = (f32[256,128]{1,0:T(8,128)S(1)}, f32[256,128]{1,0:T(8,128)S(1)}, u32[]{:S(2)}, u32[]{:S(2)}) collective-permute-start(f32[256,128]{1,0:T(8,128)S(1)} %add.9), channel_id=1, source_target_pairs={{0,64},{32,96},{64,0},{96,32},{128,192},{160,224},{192,128},{224,1... | collective-permute-start | bytes 393224 | tf_op jit(solution)/shard_map/ppermute | solution.py:327
  85.6 6.0 %collective-permute-done.1 = f32[256,128]{1,0:T(8,128)S(1)} collective-permute-done((f32[256,128]{1,0:T(8,128)S(1)}, f32[256,128]{1,0:T(8,128)S(1)}, u32[]{:S(2)}, u32[]{:S(2)}) %collective-permute-start.1) | collective-permute-done | bytes 131104 | tf_op jit(solution)/shard_map/ppermute | solution.py:327
  91.6 6.3 %collective-permute-start.2 = (f32[256,128]{1,0:T(8,128)S(1)}, f32[256,128]{1,0:T(8,128)S(1)}, u32[]{:S(2)}, u32[]{:S(2)}) collective-permute-start(f32[256,128]{1,0:T(8,128)S(1)} %add.10), channel_id=1, source_target_pairs={{0,128},{32,160},{64,192},{96,224},{128,0},{160,32},{192,64},{224,... | collective-permute-start | bytes 393224 | tf_op jit(solution)/shard_map/ppermute | solution.py:327
  97.8 0.0 all-to-all-done.3
  97.9 0.7 reduce_sum.9
  98.5 5.4 %collective-permute-done.2 = f32[256,128]{1,0:T(8,128)S(1)} collective-permute-done((f32[256,128]{1,0:T(8,128)S(1)}, f32[256,128]{1,0:T(8,128)S(1)}, u32[]{:S(2)}, u32[]{:S(2)}) %collective-permute-start.2) | collective-permute-done | bytes 131104 | tf_op jit(solution)/shard_map/ppermute | solution.py:327
  103.9 0.7 add.11
  (2 shorter events, 0.0 us)
Async XLA Ops:
  0.6 57.4 %copy-start.5 = (s32[384]{0:T(512)S(1)}, s32[384]{0:T(512)}, u32[]{:S(2)}) copy-start(s32[384]{0:T(512)} %ocean_block.1) | copy-start | bytes 4612
  15.0 1.0 copy-start
  18.2 21.3 %all-to-all-start.1 = ((bf16[128,32,128]{2,1,0:T(8,128)(2,1)}), bf16[128,32,128]{2,1,0:T(8,128)(2,1)S(1)}, u32[]{:S(2)}, u32[]{:S(2)}) async-start(bf16[128,32,128]{2,1,0:T(8,128)(2,1)} %serve.1), calls=%async_computation.1 | async-start | bytes 2097152 | tf_op jit(solution)/shard_map/all_to_all | solution.py:349
  26.5 0.9 copy-start.1
  27.4 0.9 copy-start.2
  28.3 0.9 copy-start.3
  39.4 0.7 copy-start.4
  53.1 15.6 %all-to-all-start.2 = ((f32[32,16,128]{2,1,0:T(8,128)}), f32[32,16,128]{2,1,0:T(8,128)S(1)}, u32[]{:S(2)}, u32[]{:S(2)}) async-start(f32[32,16,128]{2,1,0:T(8,128)} %bitcast.2), calls=%async_computation.2 | async-start | bytes 524288 | tf_op jit(solution)/shard_map/all_to_all | solution.py:358
  68.7 29.2 %all-to-all-start.3 = ((f32[32,32,128]{2,1,0:T(8,128)}), f32[32,32,128]{2,1,0:T(8,128)S(1)}, u32[]{:S(2)}, u32[]{:S(2)}) async-start(f32[32,32,128]{2,1,0:T(8,128)} %ocean.1), calls=%async_computation.3 | async-start | bytes 1048576 | tf_op jit(solution)/shard_map/all_to_all | solution.py:360
  76.4 5.8 %collective-permute-start = (f32[256,128]{1,0:T(8,128)S(1)}, f32[256,128]{1,0:T(8,128)S(1)}, u32[]{:S(2)}, u32[]{:S(2)}) collective-permute-start(f32[256,128]{1,0:T(8,128)S(1)} %owner_sums.1), channel_id=1, source_target_pairs={{0,32},{32,0},{64,96},{96,64},{128,160},{160,128},{192,224},{224,1... | collective-permute-start | bytes 393224 | tf_op jit(solution)/shard_map/ppermute | solution.py:327
  82.2 9.3 %collective-permute-start.1 = (f32[256,128]{1,0:T(8,128)S(1)}, f32[256,128]{1,0:T(8,128)S(1)}, u32[]{:S(2)}, u32[]{:S(2)}) collective-permute-start(f32[256,128]{1,0:T(8,128)S(1)} %add.9), channel_id=1, source_target_pairs={{0,64},{32,96},{64,0},{96,32},{128,192},{160,224},{192,128},{224,1... | collective-permute-start | bytes 393224 | tf_op jit(solution)/shard_map/ppermute | solution.py:327
  91.6 12.3 %collective-permute-start.2 = (f32[256,128]{1,0:T(8,128)S(1)}, f32[256,128]{1,0:T(8,128)S(1)}, u32[]{:S(2)}, u32[]{:S(2)}) collective-permute-start(f32[256,128]{1,0:T(8,128)S(1)} %add.10), channel_id=1, source_target_pairs={{0,128},{32,160},{64,192},{96,224},{128,0},{160,32},{192,64},{224,... | collective-permute-start | bytes 393224 | tf_op jit(solution)/shard_map/ppermute | solution.py:327

commit v4 on v3

v4 whole, which is shorter than its diff:
```python
import math

import jax
import jax.numpy as jnp
from jax import lax
from jax.experimental import pallas as pl
from jax.experimental.pallas import tpu as pltpu
from jax.sharding import PartitionSpec as P

F = 32
BLK = 128
ACELL = 128
OCELL = 128
CAP = 4
ITERS = 8

ref_height = 10.0
karman = 0.4
buoyancy = 0.5
flux_scale = 40.0

GROUP = 64
SLOT_ROWS = CAP * 4
OWNER_ROWS = SLOT_ROWS + F
MIB = 1 << 20
VMEM = pltpu.VMEM
SMEM = pltpu.SMEM

ARCTAN = (
    0.9999999952,
    -0.3333319239,
    0.1999324926,
    -0.1416585733,
    0.1012280370,
    -0.0507783010,
)


def arctan_half(t):
    z = t * t
    total = jnp.full_like(z, ARCTAN[-1])
    for c in ARCTAN[-2::-1]:
        total = total * z + c
    return total * t


def flux_rows(mapped_u, mapped_v, mapped_t, mapped_q, surf_temp, surf_hum, hum_factor, log_mom):
    wind_u = 6.0 * mapped_u
    wind_v = 6.0 * mapped_v
    square_speed = wind_u * wind_u + wind_v * wind_v + 1.0
    wind_speed = jnp.sqrt(square_speed)
    temp_diff = mapped_t - surf_temp
    hum_diff = (mapped_q - surf_hum) * hum_factor
    log_heat = log_mom + math.log(10.0)
    gain = (ref_height * buoyancy) * (temp_diff + 0.2 * hum_diff) / square_speed
    from_mom = log_mom
    from_heat = log_heat
    for sweep in range(ITERS):
        stability = jnp.clip(gain * from_mom * from_mom / from_heat, -5.0, 1.0)
        unstable = jnp.minimum(stability, 0.0)
        square = jnp.sqrt(1.0 - 16.0 * unstable)
        root = jnp.sqrt(square)
        half_square = 0.5 + 0.5 * square
        half_root = 0.5 + 0.5 * root
        log_square = jnp.log(half_square)
        log_both = jnp.log(half_root * half_root * half_square)
        turn = arctan_half((root - 1.0) / (root + 1.0))
        stable = stability >= 0.0
        psi_stable = -5.0 * stability
        psi_mom = jnp.where(stable, psi_stable, log_both - 2.0 * turn)
        psi_heat = jnp.where(stable, psi_stable, 2.0 * log_square)
        from_mom = log_mom - psi_mom
        from_heat = log_heat - psi_heat
    fric_vel = karman * wind_speed / from_mom
    drag = flux_scale * fric_vel * fric_vel / wind_speed
    carry = -flux_scale * karman * fric_vel / from_heat
    return drag * wind_u, drag * wind_v, carry * temp_diff, carry * hum_diff


def serve_body(requests, fields, out):
    def owner(d, _):
        for c in range(CAP):
            out[d * CAP + c] = fields[requests[d, c]]
        return 0

    lax.fori_loop(0, out.shape[0] // CAP, owner, 0)


def serve(requests, fields):
    return pl.pallas_call(
        serve_body,
        out_shape=jax.ShapeDtypeStruct((requests.size,) + fields.shape[1:], fields.dtype),
        in_specs=[pl.BlockSpec(memory_space=SMEM), pl.BlockSpec(memory_space=VMEM)],
        out_specs=pl.BlockSpec(memory_space=VMEM),
        compiler_params=pltpu.CompilerParams(vmem_limit_bytes=8 * MIB),
        name="serve",
    )(requests, fields)


def prep_body(ocean_cell, surf_temp, surf_hum, requests, hot, temp, hum, request_row):
    request_row[...] = requests[...]
    temp[...] = surf_temp[...]
    hum[...] = surf_hum[...]
    target = lax.broadcasted_iota(jnp.int32, (OCELL, BLK), 0)
    for i in range(hot.shape[0]):
        hot[i] = jnp.where(target == ocean_cell[i : i + 1, :], 1.0, 0.0).astype(jnp.bfloat16).T


def prep(ocean_cell, surf_temp, surf_hum, requests):
    blocks = ocean_cell.shape[0]
    part = pl.BlockSpec((GROUP, BLK), lambda s: (s, 0))
    flat = jax.ShapeDtypeStruct((blocks, BLK), jnp.float32)
    line = pl.BlockSpec((1, requests.size), lambda s: (0, 0))
    return pl.pallas_call(
        prep_body,
        out_shape=(pltpu.HBM((blocks, BLK, OCELL), jnp.bfloat16), flat, flat, jax.ShapeDtypeStruct((1, requests.size), jnp.int32)),
        grid=(blocks // GROUP,),
        in_specs=[part] * 3 + [line],
        out_specs=(pl.BlockSpec((GROUP, BLK, OCELL), lambda s: (s, 0, 0)), part, part, line),
        compiler_params=pltpu.CompilerParams(vmem_limit_bytes=16 * MIB),
        cost_estimate=pl.CostEstimate(
            flops=2 * blocks * BLK * OCELL,
            bytes_accessed=2 * blocks * BLK * OCELL,
            transcendentals=0,
        ),
        name="prep",
    )(ocean_cell, surf_temp, surf_hum, requests.T.reshape(1, -1))


def two_parts(value):
    high = value.astype(jnp.bfloat16)
    return high, (value - high.astype(jnp.float32)).astype(jnp.bfloat16)


def product(left, right):
    return jnp.dot(left, right, preferred_element_type=jnp.float32)


def one_hot(of_row, index_row):
    return jnp.where(of_row == index_row, 1.0, 0.0).astype(jnp.bfloat16)


def picked_sum(picked, values):
    high, low = two_parts(values)
    return product(picked, high) + product(picked, low)


def couple_body(
    use_slot,
    ocean_block,
    slot_row,
    table,
    weights,
    hot_far,
    surf_temp,
    surf_hum,
    hum_factor,
    log_mom,
    cell_weight,
    passive_weight,
    out,
    held,
    hot,
    rows_even,
    rows_odd,
    partial,
    contrib,
    sem,
):
    blocks = held.shape[0]
    parts = blocks // GROUP
    owners = out.shape[0] // OWNER_ROWS

    def fetch(p):
        share = pl.ds(pl.multiple_of(p * GROUP, GROUP), GROUP)
        return (
            pltpu.make_async_copy(weights.at[share], held.at[share], sem.at[p]),
            pltpu.make_async_copy(hot_far.at[share], hot.at[share], sem.at[parts + p]),
        )

    for p in range(parts):
        for copy in fetch(p):
            copy.start()
    out[...] = jnp.zeros_like(out)
    is_flux = lax.broadcasted_iota(jnp.int32, (8, BLK), 0) < 4

    def map_part(p, rows):
        base = p * GROUP
        for i in range(0, GROUP, 2):
            k = base + i
            both = lax.dot_general(
                jnp.concatenate([table[use_slot[0, k]], table[use_slot[0, k + 1]]], axis=0),
                held[pl.ds(k, 2)].reshape(2 * BLK, ACELL),
                (((1,), (1,)), ((), ())),
                preferred_element_type=jnp.float32,
            )
            rows[i * F : (i + 1) * F, :] = both[:F, :BLK]
            rows[(i + 1) * F : (i + 2) * F, :] = both[F:, BLK:]

    def flux_part(p, rows):
        mine = pl.ds(pl.multiple_of(p * GROUP, GROUP), GROUP)
        fluxes = flux_rows(
            *(rows[pl.ds(f, GROUP, stride=F), :] for f in range(4)),
            surf_temp[mine, :],
            surf_hum[mine, :],
            hum_factor[mine, :],
            log_mom[mine, :],
        )
        weight = cell_weight[mine, :]
        for f in range(4):
            rows[pl.ds(f, GROUP, stride=F), :] = weight * fluxes[f]

    def sum_part(p, rows):
        base = p * GROUP
        for i in range(0, GROUP, 2):
            k = base + i
            left = jnp.concatenate(
                [rows[i * F : i * F + 8, :], rows[(i + 1) * F : (i + 1) * F + 8, :]], axis=0
            ).astype(jnp.bfloat16)
            both = product(left, jnp.concatenate([held[k], held[k + 1]], axis=1))
            contrib[pl.ds(pl.multiple_of(k * 8, 8), 8), :] = both[:8, :ACELL]
            contrib[pl.ds(pl.multiple_of(k * 8 + 8, 8), 8), :] = both[8:, ACELL:]
        for i in range(GROUP):
            k = base + i
            factor = passive_weight[pl.ds(k, 1), :]
            value = rows[i * F : (i + 1) * F, :]
            value = jnp.concatenate(
                [jnp.where(is_flux, value[:8], value[:8] * factor), value[8:] * factor], axis=0
            )
            both = product(jnp.concatenate(two_parts(value), axis=0), hot[k])
            partial[i * F : (i + 1) * F, :] = both[:F] + both[F:]
        for i in range(GROUP):
            target = pl.ds(
                pl.multiple_of(ocean_block[0, base + i] * OWNER_ROWS + SLOT_ROWS, SLOT_ROWS), F
            )
            out[target, :] = out[target, :] + partial[i * F : (i + 1) * F, :]

    def arrive(p, which):
        fetch(p)[which].wait()

    def step(p, _):
        arrive(p, 0)
        map_part(p, rows_even)
        flux_part(p, rows_even)
        arrive(p, 1)
        sum_part(p, rows_even)
        return 0

    lax.fori_loop(0, parts, step, 0)

    order = lax.broadcasted_iota(jnp.int32, (owners * CAP, blocks), 0)
    slot_of = lax.rem(order, owners) * CAP + order // owners
    picked = one_hot(slot_of, slot_row[...])
    for c in range(4):
        sums = picked_sum(picked, contrib[pl.ds(c, blocks, stride=8), :])
        for column in range(CAP):
            out[pl.ds(column * 4 + c, owners, stride=OWNER_ROWS), :] = sums[
                column * owners : (column + 1) * owners
            ]


def couple(slot_row, block_row, table, weights, hot, cells, owners):
    blocks = weights.shape[0]
    here = pl.BlockSpec(memory_space=VMEM)
    far = pl.BlockSpec(memory_space=pltpu.HBM)
    line = pl.BlockSpec(memory_space=SMEM)
    return pl.pallas_call(
        couple_body,
        out_shape=jax.ShapeDtypeStruct((owners * OWNER_ROWS, ACELL), jnp.float32),
        in_specs=[line, line, here, here, far, far] + [here] * 6,
        out_specs=here,
        scratch_shapes=[
            pltpu.VMEM(weights.shape, weights.dtype),
            pltpu.VMEM(hot.shape, hot.dtype),
            pltpu.VMEM((GROUP * F, BLK), jnp.float32),
            pltpu.VMEM((GROUP * F, BLK), jnp.float32),
            pltpu.VMEM((GROUP * F, OCELL), jnp.float32),
            pltpu.VMEM((blocks * 8, ACELL), jnp.float32),
            pltpu.SemaphoreType.DMA((2 * (blocks // GROUP),)),
        ],
        compiler_params=pltpu.CompilerParams(vmem_limit_bytes=44 * MIB),
        name="couple",
    )(
        slot_row,
        block_row,
        slot_row,
        table,
        pltpu.with_memory_space_constraint(weights, pltpu.HBM),
        pltpu.with_memory_space_constraint(hot, pltpu.HBM),
        *cells,
    )


def owner_body(request_row, returned, owner_sums, ocean_flux):
    sources = returned.shape[0] // OWNER_ROWS
    shape = (owner_sums.shape[0] // 4, request_row.shape[1])
    picked = one_hot(lax.broadcasted_iota(jnp.int32, shape, 0), request_row[...])
    for c in range(4):
        values = jnp.concatenate(
            [
                returned[pl.ds(column * 4 + c, sources, stride=OWNER_ROWS), :]
                for column in range(CAP)
            ],
            axis=0,
        )
        owner_sums[pl.ds(c, shape[0], stride=4), :] = picked_sum(picked, values)
    total = returned[SLOT_ROWS:OWNER_ROWS, :]
    for source in range(1, sources):
        first = source * OWNER_ROWS
        total = total + returned[first + SLOT_ROWS : first + OWNER_ROWS, :]
    ocean_flux[0] = total


def owner_sums_of(request_row, returned, local_blocks):
    here = pl.BlockSpec(memory_space=VMEM)
    return pl.pallas_call(
        owner_body,
        out_shape=(
            jax.ShapeDtypeStruct((local_blocks * 4, ACELL), jnp.float32),
            jax.ShapeDtypeStruct((1, F, OCELL), jnp.float32),
        ),
        in_specs=[here, here],
        out_specs=(here, here),
        compiler_params=pltpu.CompilerParams(vmem_limit_bytes=8 * MIB),
        name="owner_sums",
    )(request_row, returned)


def sum_over(x, axis):
    ranks = lax.axis_size(axis)
    bit = 1
    while bit < ranks:
        mask = ranks - 1 if 2 * bit == ranks else bit
        x = x + lax.ppermute(x, axis, [(i, i ^ mask) for i in range(ranks)])
        bit *= 2
    return x


def per_device(
    atm_fields,
    weights,
    surf_temp,
    surf_hum,
    roughness,
    cell_area,
    need_list,
    use_slot,
    ocean_block,
    ocean_cell,
    cell_count,
    ice_mask,
):
    owners = lax.axis_size("atm")
    local_blocks = atm_fields.shape[0]
    requests = lax.all_to_all(need_list[0], "atm", split_axis=0, concat_axis=0, tiled=True)
    table = lax.all_to_all(serve(requests, atm_fields), "atm", split_axis=0, concat_axis=0, tiled=True)
    hot, surf_temp, surf_hum, request_row = prep(ocean_cell, surf_temp, surf_hum, requests)
    ice_frac = ice_mask.astype(jnp.float32)
    is_live = jnp.arange(BLK, dtype=jnp.int32)[None, :] < cell_count[:, None]
    cell_weight = jnp.where(is_live, cell_area, 0.0)
    log_mom = jnp.log(ref_height / roughness)
    passive_weight = cell_weight * (1.0 - 0.7 * ice_frac)
    cells = (surf_temp, surf_hum, 1.0 - 0.6 * ice_frac, log_mom, cell_weight, passive_weight)
    lines = (use_slot.reshape(1, -1), ocean_block.reshape(1, -1))
    sums = couple(*lines, table, weights, hot, cells, owners)
    returned = lax.all_to_all(sums, "atm", split_axis=0, concat_axis=0, tiled=True)
    owner_sums, ocean_flux = owner_sums_of(request_row, returned, local_blocks)
    atm_flux = sum_over(owner_sums, "ocn").reshape(local_blocks, 4, ACELL)
    return (atm_flux, ocean_flux)


def solution(mesh):
    placed = (
        P("atm", None, None),
        P(("ocn", "atm"), None, None),
        P(("ocn", "atm"), None),
        P(("ocn", "atm"), None),
        P(("ocn", "atm"), None),
        P(("ocn", "atm"), None),
        P(("ocn", "atm"), None, None),
        P(("ocn", "atm")),
        P(("ocn", "atm")),
        P(("ocn", "atm"), None),
        P(("ocn", "atm")),
        P(("ocn", "atm"), None),
    )
    return jax.shard_map(
        per_device,
        mesh=mesh,
        in_specs=placed,
        out_specs=(P("atm", None, None), P(("ocn", "atm"), None, None)),
        check_vma=False,
    )
```

time: 105 us -> 103 us (0.981)
  blocking collectives: 13.6 us -> 31.4 us
  starting transfers between devices: 29.1 us -> 15.3 us
  Pallas kernels: 32.4 us -> 26 us
  other arithmetic: 3.29 us -> 1.95 us
  waiting for transfers between devices: 18.9 us -> 20 us
    all_to_all x0 -> x1, blocking collectives: none -> 17.8 us  [per_device(): lax.all_to_all(sums, 'atm', split_axis=0, concat_axis=0, tiled=True)]
    all_to_all x2 -> x0, starting transfers between devices: 12.5 us -> none  [the longest x1 7.49 us: per_device(): lax.all_to_all(ocean_sums, 'atm', split_axis=0, concat_axis=0, tiled=True)]
    pallas_call x3 -> x2, Pallas kernels: 23.8 us -> 17.4 us  [the longest x1 16.7 us: couple(): pl.pallas_call(couple_body, out_shape=jax.ShapeDtypeStruct((owners * OWNE...]
    ppermute x3, starting transfers between devices: 11.6 us -> 10.2 us  [sum_over(): x = x + lax.ppermute(x, axis, [(i, i ^ mask) for i in range(ranks)])]
    unnamed x12 -> x8, local copies, waits for them, and re-layouts: 4.5 us -> 3.83 us
  transfers between devices with their start and end apart: 6 -> 4, of which waited for: 4 -> 4; matrix products, arithmetic and copies ran while one was open for 4% -> 3% of each run, Pallas kernels for 16% -> 6%
where the time goes in v4:
time: 103 us; the launch traced here: 101 us
  blocking collectives  31.4 us (30%)
  Pallas kernels  26 us (25%)
  waiting for transfers between devices  20 us (19%)
  starting transfers between devices  15.3 us (15%)
  local copies, waits for them, and re-layouts  6.21 us (6%)
  other arithmetic  1.95 us (2%)
    all_to_all x1, blocking collectives, per_device(): lax.all_to_all(sums, 'atm', split_axis=0, concat_axis=0, tiled=True)  17.8 us
    pallas_call x1, Pallas kernels, couple(): pl.pallas_call(couple_body, out_shape=jax.ShapeDtypeStruct((owners * OWNE...  16.7 us
    ppermute x3, waiting for transfers between devices, sum_over(): x = x + lax.ppermute(x, axis, [(i, i ^ mask) for i in range(ranks)])  15.7 us
    all_to_all x1, blocking collectives, per_device(): lax.all_to_all(need_list[0], 'atm', split_axis=0, concat_axis=0, tiled=True)  13.6 us
    ppermute x3, starting transfers between devices, sum_over(): x = x + lax.ppermute(x, axis, [(i, i ^ mask) for i in range(ranks)])  10.2 us
    pallas_call x1, Pallas kernels, prep(): pl.pallas_call(prep_body, out_shape=(pltpu.HBM((blocks, BLK, OCELL), jnp....  6.43 us
    all_to_all x1, starting transfers between devices, per_device(): lax.all_to_all(serve(requests, atm_fields), 'atm', split_axis=0, concat_a...  5.03 us
    all_to_all x1, waiting for transfers between devices, per_device(): lax.all_to_all(serve(requests, atm_fields), 'atm', split_axis=0, concat_a...  4.29 us
  transfers between devices with their start and end apart: 4, of which 4 were waited for; matrix products, arithmetic and copies ran while one was open for 3% of the time, Pallas kernels for 6%

profile of v4, /device:TPU:2, one launch (start us, length us, event | category | flops | bytes accessed | tf_op | source)
XLA Modules:
  0.0 101.5 jit_solution(5622739818968437245)
XLA Ops:
  0.6 0.8 copy.15
  1.4 13.6 %all_to_all.27 = s32[32,1,4]{2,1,0:T(1,128)S(1)} all-to-all(s32[32,1,4]{2,1,0:T(1,128)S(1)} %copy.15), channel_id=1, replica_groups=mesh['ocn'=8,'atm'=32] {'atm'}, dimensions={0} | all-to-all | bytes 1024 | tf_op jit(solution)/shard_map/all_to_all | solution.py:355
  14.9 0.1 copy.16
  15.0 0.1 copy.17.requests
  15.1 0.0 copy-start
  15.1 1.0 %copy-done = bf16[64,32,128]{2,1,0:T(8,128)(2,1)S(1)} copy-done((bf16[64,32,128]{2,1,0:T(8,128)(2,1)S(1)}, bf16[64,32,128]{2,1,0:T(8,128)(2,1)}, u32[]{:S(2)}) %copy-start) | copy-done | bytes 524312
  16.2 2.2 %serve.1 = bf16[128,32,128]{2,1,0:T(8,128)(2,1)} custom-call(s32[32,4]{1,0:T(8,128)S(1)} %copy.17.requests, bf16[64,32,128]{2,1,0:T(8,128)(2,1)S(1)} %copy-done), custom_call_target="tpu_custom_call" | custom-call | tf_op jit(solution)/shard_map/serve/pallas_call | solution.py:90
  18.3 5.0 %all-to-all-start.1 = ((bf16[128,32,128]{2,1,0:T(8,128)(2,1)}), bf16[128,32,128]{2,1,0:T(8,128)(2,1)S(1)}, u32[]{:S(2)}, u32[]{:S(2)}) async-start(bf16[128,32,128]{2,1,0:T(8,128)(2,1)} %serve.1), calls=%async_computation.1 | async-start | bytes 2097152 | tf_op jit(solution)/shard_map/all_to_all | solution.py:356
  23.4 0.7 reshape.23.use_slot.slot_row
  24.1 0.7 reshape.24.ocean_block
  24.7 1.2 %subtract_multiply_fusion = (f32[384,128]{1,0:T(8,128)S(1)}, f32[384,128]{1,0:T(8,128)S(1)}, f32[384,128]{1,0:T(8,128)S(1)}, f32[384,128]{1,0:T(8,128)S(1)}) fusion(s32[384,128]{1,0:T(8,128)} %param.23, f32[384,128]{1,0:T(8,128)} %param.17, s32[384]{0:T(512)} %param.22, f32[384,128]{1,0:T(8,128)} %param.16), kind=kLoop, calls=%fused_computation | loop fusion | flops 442368 | bytes 1377792 | tf_op jit(solution)/shard_map/mul | solution.py:362
  26.0 0.1 reshape.22.requests
  26.1 0.0 copy-start.1
  26.1 0.9 copy-done.1
  27.0 0.0 copy-start.2
  27.0 0.9 copy-done.2
  27.9 0.0 copy-start.3
  27.9 0.9 copy-done.3
  28.9 6.4 %prep.1 = (bf16[384,128,128]{2,1,0:T(8,128)(2,1)}, f32[384,128]{1,0:T(8,128)S(1)}, f32[384,128]{1,0:T(8,128)S(1)}, s32[1,128]{1,0:T(1,128)S(1)}) custom-call(s32[384,128]{1,0:T(8,128)S(1)} %copy-done.1, f32[384,128]{1,0:T(8,128)S(1)} %copy-done.2, f32[384,128]{1,0:T(8,128)S(1)} %copy-done.3, s32[1,128]{1,0:T(1,128)S(1)} %reshape.22.requests), custom_call_target="tpu_custom_call" | custom-call | flops 12582912 | bytes 12582912 | tf_op jit(solution)/shard_map/prep/pallas_call | solution.py:114
  35.3 4.3 %all-to-all-done.1.table = bf16[128,32,128]{2,1,0:T(8,128)(2,1)S(1)} async-done(((bf16[128,32,128]{2,1,0:T(8,128)(2,1)}), bf16[128,32,128]{2,1,0:T(8,128)(2,1)S(1)}, u32[]{:S(2)}, u32[]{:S(2)}) %all-to-all-start.1) | async-done | bytes 1048608 | tf_op jit(solution)/shard_map/all_to_all | solution.py:356
  39.6 16.7 %couple.1 = f32[1536,128]{1,0:T(8,128)S(1)} custom-call(s32[1,384]{1,0:T(1,128)S(1)} %reshape.23.use_slot.slot_row, s32[1,384]{1,0:T(1,128)S(1)} %reshape.24.ocean_block, s32[1,384]{1,0:T(1,128)S(1)} %reshape.23.use_slot.slot_row, bf16[128,32,128]{2,1,0:T(8,128)(2,1)S(1)} %all-to-all-done.1.table, bf16[384,128,128]{2,1,0:T(8,128)(2,1)} %weights.1, ...), custom_call_target="tpu_custom_call" | custom-call | tf_op jit(solution)/shard_map/couple/pallas_call | solution.py:267
  56.3 17.8 %all_to_all.28 = f32[32,48,128]{2,1,0:T(8,128)S(1)} all-to-all(f32[32,48,128]{2,1,0:T(8,128)S(1)} %bitcast.8), channel_id=1, replica_groups=mesh['ocn'=8,'atm'=32] {'atm'}, dimensions={0} | all-to-all | bytes 1572864 | tf_op jit(solution)/shard_map/all_to_all | solution.py:366
  74.1 0.8 owner_sums.1
  74.9 1.9 %collective-permute-start = (f32[256,128]{1,0:T(8,128)S(1)}, f32[256,128]{1,0:T(8,128)S(1)}, u32[]{:S(2)}, u32[]{:S(2)}) collective-permute-start(f32[256,128]{1,0:T(8,128)S(1)} %get-tuple-element.12), channel_id=1, source_target_pairs={{0,32},{32,0},{64,96},{96,64},{128,160},{160,128},{192,224},{224,1... | collective-permute-start | bytes 393224 | tf_op jit(solution)/shard_map/ppermute | solution.py:334
  76.8 3.9 %collective-permute-done = f32[256,128]{1,0:T(8,128)S(1)} collective-permute-done((f32[256,128]{1,0:T(8,128)S(1)}, f32[256,128]{1,0:T(8,128)S(1)}, u32[]{:S(2)}, u32[]{:S(2)}) %collective-permute-start) | collective-permute-done | bytes 131104 | tf_op jit(solution)/shard_map/ppermute | solution.py:334
  80.7 3.4 %collective-permute-start.1 = (f32[256,128]{1,0:T(8,128)S(1)}, f32[256,128]{1,0:T(8,128)S(1)}, u32[]{:S(2)}, u32[]{:S(2)}) collective-permute-start(f32[256,128]{1,0:T(8,128)S(1)} %add.9), channel_id=1, source_target_pairs={{0,64},{32,96},{64,0},{96,32},{128,192},{160,224},{192,128},{224,1... | collective-permute-start | bytes 393224 | tf_op jit(solution)/shard_map/ppermute | solution.py:334
  84.1 6.1 %collective-permute-done.1 = f32[256,128]{1,0:T(8,128)S(1)} collective-permute-done((f32[256,128]{1,0:T(8,128)S(1)}, f32[256,128]{1,0:T(8,128)S(1)}, u32[]{:S(2)}, u32[]{:S(2)}) %collective-permute-start.1) | collective-permute-done | bytes 131104 | tf_op jit(solution)/shard_map/ppermute | solution.py:334
  90.2 5.0 %collective-permute-start.2 = (f32[256,128]{1,0:T(8,128)S(1)}, f32[256,128]{1,0:T(8,128)S(1)}, u32[]{:S(2)}, u32[]{:S(2)}) collective-permute-start(f32[256,128]{1,0:T(8,128)S(1)} %add.10), channel_id=1, source_target_pairs={{0,224},{32,192},{64,160},{96,128},{128,96},{160,64},{192,32},{224... | collective-permute-start | bytes 393224 | tf_op jit(solution)/shard_map/ppermute | solution.py:334
  95.2 5.6 %collective-permute-done.2 = f32[256,128]{1,0:T(8,128)S(1)} collective-permute-done((f32[256,128]{1,0:T(8,128)S(1)}, f32[256,128]{1,0:T(8,128)S(1)}, u32[]{:S(2)}, u32[]{:S(2)}) %collective-permute-start.2) | collective-permute-done | bytes 131104 | tf_op jit(solution)/shard_map/ppermute | solution.py:334
  100.8 0.7 add.11
  (2 shorter events, 0.0 us)
Async XLA Ops:
  15.1 1.0 %copy-start = (bf16[64,32,128]{2,1,0:T(8,128)(2,1)S(1)}, bf16[64,32,128]{2,1,0:T(8,128)(2,1)}, u32[]{:S(2)}) copy-start(bf16[64,32,128]{2,1,0:T(8,128)(2,1)} %fields.1) | copy-start | bytes 1572868
  18.3 21.3 %all-to-all-start.1 = ((bf16[128,32,128]{2,1,0:T(8,128)(2,1)}), bf16[128,32,128]{2,1,0:T(8,128)(2,1)S(1)}, u32[]{:S(2)}, u32[]{:S(2)}) async-start(bf16[128,32,128]{2,1,0:T(8,128)(2,1)} %serve.1), calls=%async_computation.1 | async-start | bytes 2097152 | tf_op jit(solution)/shard_map/all_to_all | solution.py:356
  26.1 0.9 copy-start.1
  27.0 0.9 copy-start.2
  27.9 0.9 copy-start.3
  74.9 5.9 %collective-permute-start = (f32[256,128]{1,0:T(8,128)S(1)}, f32[256,128]{1,0:T(8,128)S(1)}, u32[]{:S(2)}, u32[]{:S(2)}) collective-permute-start(f32[256,128]{1,0:T(8,128)S(1)} %get-tuple-element.12), channel_id=1, source_target_pairs={{0,32},{32,0},{64,96},{96,64},{128,160},{160,128},{192,224},{224,1... | collective-permute-start | bytes 393224 | tf_op jit(solution)/shard_map/ppermute | solution.py:334
  80.7 9.5 %collective-permute-start.1 = (f32[256,128]{1,0:T(8,128)S(1)}, f32[256,128]{1,0:T(8,128)S(1)}, u32[]{:S(2)}, u32[]{:S(2)}) collective-permute-start(f32[256,128]{1,0:T(8,128)S(1)} %add.9), channel_id=1, source_target_pairs={{0,64},{32,96},{64,0},{96,32},{128,192},{160,224},{192,128},{224,1... | collective-permute-start | bytes 393224 | tf_op jit(solution)/shard_map/ppermute | solution.py:334
  90.2 10.6 %collective-permute-start.2 = (f32[256,128]{1,0:T(8,128)S(1)}, f32[256,128]{1,0:T(8,128)S(1)}, u32[]{:S(2)}, u32[]{:S(2)}) collective-permute-start(f32[256,128]{1,0:T(8,128)S(1)} %add.10), channel_id=1, source_target_pairs={{0,224},{32,192},{64,160},{96,128},{128,96},{160,64},{192,32},{224... | collective-permute-start | bytes 393224 | tf_op jit(solution)/shard_map/ppermute | solution.py:334

commit v5 on v3

--- a/solution.py
+++ b/solution.py
@@ -21,6 +21,7 @@
 
 GROUP = 64
 MIB = 1 << 20
+ADD_COST = pl.CostEstimate(flops=1500000000, bytes_accessed=3 << 17, transcendentals=0)
 VMEM = pltpu.VMEM
 SMEM = pltpu.SMEM
 
@@ -184,7 +185,7 @@
         for i in range(0, GROUP, 2):
             k = base + i
             both = lax.dot_general(
-                jnp.concatenate([table[use_slot[k]], table[use_slot[k + 1]]], axis=0),
+                jnp.concatenate([table[use_slot[0, k]], table[use_slot[0, k + 1]]], axis=0),
                 held[pl.ds(k, 2)].reshape(2 * BLK, ACELL),
                 (((1,), (1,)), ((), ())),
                 preferred_element_type=jnp.float32,
@@ -224,7 +225,7 @@
         put(p).wait()
 
 
-def fluxes_of(use_slot, table, weights, cells):
+def fluxes_of(slot_row, table, weights, cells):
     blocks = weights.shape[0]
     here = pl.BlockSpec(memory_space=VMEM)
     far = pl.BlockSpec(memory_space=pltpu.HBM)
@@ -246,85 +247,126 @@
         compiler_params=pltpu.CompilerParams(vmem_limit_bytes=30 * MIB),
         name="fluxes",
     )(
-        use_slot,
-        use_slot.reshape(1, -1),
+        slot_row,
+        slot_row,
         table,
         pltpu.with_memory_space_constraint(weights, pltpu.HBM),
         *cells,
     )
 
 
-def ocean_body(ocean_block, rows, hot, passive_weight, ocean_sums, partial):
-    step = pl.program_id(0)
-
-    @pl.when(step == 0)
-    def _():
-        ocean_sums[...] = jnp.zeros_like(ocean_sums)
-
+def ocean_body(ocean_block, rows_far, hot_far, passive_weight, ocean_sums, rows, hot, partial, sem):
+    parts = hot.shape[0] // GROUP
+
+    def fetch(p):
+        flat = pl.ds(pl.multiple_of(p * (GROUP * F), GROUP * F), GROUP * F)
+        share = pl.ds(pl.multiple_of(p * GROUP, GROUP), GROUP)
+        return (
+            pltpu.make_async_copy(rows_far.at[flat], rows.at[flat], sem.at[p]),
+            pltpu.make_async_copy(hot_far.at[share], hot.at[share], sem.at[parts + p]),
+        )
+
+    for p in range(parts):
+        for copy in fetch(p):
+            copy.start()
+    ocean_sums[...] = jnp.zeros_like(ocean_sums)
     is_flux = lax.broadcasted_iota(jnp.int32, (8, BLK), 0) < 4
-    for i in range(GROUP):
-        factor = passive_weight[i : i + 1, :]
-        value = rows[i * F : (i + 1) * F, :]
-        value = jnp.concatenate(
-            [jnp.where(is_flux, value[:8], value[:8] * factor), value[8:] * factor], axis=0
-        )
-        both = product(jnp.concatenate(two_parts(value), axis=0), hot[i])
-        partial[i * F : (i + 1) * F, :] = both[:F] + both[F:]
-    for i in range(GROUP):
-        target = ocean_block[step * GROUP + i]
-        ocean_sums[target] = ocean_sums[target] + partial[i * F : (i + 1) * F, :]
-
-
-def ocean_of(ocean_block, rows, hot, passive_weight, owners):
-    blocks = hot.shape[0]
+
+    def part(p, _):
+        for copy in fetch(p):
+            copy.wait()
+        for i in range(GROUP):
+            k = p * GROUP + i
+            factor = passive_weight[pl.ds(k, 1), :]
+            value = rows[pl.ds(pl.multiple_of(k * F, F), F), :]
+            value = jnp.concatenate(
+                [jnp.where(is_flux, value[:8], value[:8] * factor), value[8:] * factor], axis=0
+            )
+            both = product(jnp.concatenate(two_parts(value), axis=0), hot[k])
+            partial[i * F : (i + 1) * F, :] = both[:F] + both[F:]
+        for i in range(GROUP):
+            target = ocean_block[0, p * GROUP + i]
+            ocean_sums[target] = ocean_sums[target] + partial[i * F : (i + 1) * F, :]
+        return 0
+
+    lax.fori_loop(0, parts, part, 0)
+
+
+def ocean_of(block_row, rows, hot, passive_weight, owners):
+    here = pl.BlockSpec(memory_space=VMEM)
+    far = pl.BlockSpec(memory_space=pltpu.HBM)
     return pl.pallas_call(
         ocean_body,
         out_shape=jax.ShapeDtypeStruct((owners, F, OCELL), jnp.float32),
-        grid_spec=pltpu.PrefetchScalarGridSpec(
-            num_scalar_prefetch=1,
-            grid=(blocks // GROUP,),
-            in_specs=[
-                pl.BlockSpec((GROUP * F, BLK), lambda s, _: (s, 0)),
-                pl.BlockSpec((GROUP, BLK, OCELL), lambda s, _: (s, 0, 0)),
-                pl.BlockSpec((GROUP, BLK), lambda s, _: (s, 0)),
-            ],
-            out_specs=pl.BlockSpec((owners, F, OCELL), lambda s, _: (0, 0, 0)),
-            scratch_shapes=[pltpu.VMEM((GROUP * F, OCELL), jnp.float32)],
-        ),
-        compiler_params=pltpu.CompilerParams(vmem_limit_bytes=16 * MIB),
+        in_specs=[pl.BlockSpec(memory_space=SMEM), far, far, here],
+        out_specs=here,
+        scratch_shapes=[
+            pltpu.VMEM(rows.shape, rows.dtype),
+            pltpu.VMEM(hot.shape, hot.dtype),
+            pltpu.VMEM((GROUP * F, OCELL), jnp.float32),
+            pltpu.SemaphoreType.DMA((2 * (hot.shape[0] // GROUP),)),
+        ],
+        compiler_params=pltpu.CompilerParams(vmem_limit_bytes=28 * MIB),
         cost_estimate=pl.CostEstimate(
             flops=128 * rows.size, bytes_accessed=12 * rows.size, transcendentals=0
         ),
         name="ocean",
     )(
-        ocean_block,
+        block_row,
         pltpu.with_memory_space_constraint(rows, pltpu.HBM),
         pltpu.with_memory_space_constraint(hot, pltpu.HBM),
         passive_weight,
     )
 
 
-def owner_body(request_row, returned, out):
+def owner_body(request_row, returned, ocean_sums, out):
     sum_rows(one_hot(request_row[...], out.shape[0] // 4), returned, out, 4)
 
 
-def owner_sums_of(request_row, returned, local_blocks):
+def owner_sums_of(request_row, returned, ocean_sums, local_blocks):
     here = pl.BlockSpec(memory_space=VMEM)
     return pl.pallas_call(
         owner_body,
         out_shape=jax.ShapeDtypeStruct((local_blocks * 4, ACELL), jnp.float32),
+        in_specs=[here, here, pl.BlockSpec(memory_space=pl.ANY)],
+        out_specs=here,
+        compiler_params=pltpu.CompilerParams(vmem_limit_bytes=8 * MIB),
+        name="owner_sums",
+    )(request_row, returned, ocean_sums)
+
+
+def add_body(left, right, out):
+    out[...] = left[...] + right[...]
+
+
+def add(left, right):
+    here = pl.BlockSpec(memory_space=VMEM)
+    return pl.pallas_call(
+        add_body,
+        out_shape=jax.ShapeDtypeStruct(left.shape, left.dtype),
         in_specs=[here, here],
         out_specs=here,
         compiler_params=pltpu.CompilerParams(vmem_limit_bytes=8 * MIB),
-        name="owner_sums",
-    )(request_row, returned)
-
-
-def sum_over(x, axis):
-    ranks = lax.axis_size(axis)
+        cost_estimate=ADD_COST,
+        name="add",
+    )(left, right)
+
+
+def sum_over_ring(x, axis, other):
+    ranks, places = lax.axis_size(axis), lax.axis_size(other)
     bit = 1
     while bit < ranks:
-        x = x + lax.ppermute(x, axis, [(i, i ^ bit) for i in range(ranks)])
+        mask = ranks - 1 if 2 * bit == ranks else bit
+
+        def partner(i, turn):
+            return (((i - turn) % ranks) ^ mask) + turn
+
+        pairs = [
+            (i * places + p, partner(i, (p % 2) * (ranks // 4)) % ranks * places + p)
+            for i in range(ranks)
+            for p in range(places)
+        ]
+        x = add(x, lax.ppermute(x, (axis, other), pairs))
         bit *= 2
     return x
 
@@ -354,12 +396,12 @@
     log_mom = jnp.log(ref_height / roughness)
     cells = (surf_temp, surf_hum, 1.0 - 0.6 * ice_frac, log_mom, cell_weight)
     passive_weight = cell_weight * (1.0 - 0.7 * ice_frac)
-    rows, slot_sums = fluxes_of(use_slot, table, weights, cells)
+    rows, slot_sums = fluxes_of(use_slot.reshape(1, -1), table, weights, cells)
     returned = lax.all_to_all(slot_sums, "atm", split_axis=0, concat_axis=0, tiled=True)
-    ocean_sums = ocean_of(ocean_block, rows, hot, passive_weight, owners)
+    ocean_sums = ocean_of(ocean_block.reshape(1, -1), rows, hot, passive_weight, owners)
+    owner_sums = owner_sums_of(request_row, returned, ocean_sums, local_blocks)
     ocean_parts = lax.all_to_all(ocean_sums, "atm", split_axis=0, concat_axis=0, tiled=True)
-    owner_sums = owner_sums_of(request_row, returned, local_blocks)
-    atm_flux = sum_over(owner_sums, "ocn").reshape(local_blocks, 4, ACELL)
+    atm_flux = sum_over_ring(owner_sums, "ocn", "atm").reshape(local_blocks, 4, ACELL)
     ocean_flux = jnp.sum(ocean_parts, axis=0, keepdims=True)
     return (atm_flux, ocean_flux)
 

time: 105 us -> 93.4 us (0.89)
  waiting for transfers between devices: 18.9 us -> 11 us
  Pallas kernels: 32.4 us -> 31.1 us
  starting transfers between devices: 29.1 us -> 28 us
    ppermute x3, waiting for transfers between devices: 15.2 us -> 7.29 us  [sum_over_ring(): x = add(x, lax.ppermute(x, (axis, other), pairs))]
    pallas_call x1, Pallas kernels: 10.6 us -> 8.62 us  [ocean_of(): pl.pallas_call(ocean_body, out_shape=jax.ShapeDtypeStruct((owners, F, OCE...]
    ppermute x3, starting transfers between devices: 11.6 us -> 10.5 us  [sum_over_ring(): x = add(x, lax.ppermute(x, (axis, other), pairs))]
    unnamed x12 -> x10, local copies, waits for them, and re-layouts: 4.5 us -> 3.82 us
  transfers between devices with their start and end apart: 6 -> 6, of which waited for: 4 -> 3; matrix products, arithmetic and copies ran while one was open for 4% -> 4% of each run, Pallas kernels for 16% -> 16%
where the time goes in v5:
time: 93.4 us; the launch traced here: 92.9 us
  Pallas kernels  31.1 us (33%)
  starting transfers between devices  28 us (30%)
  blocking collectives  13.6 us (15%)
  waiting for transfers between devices  11 us (12%)
  local copies, waits for them, and re-layouts  5.89 us (6%)
  other arithmetic  2.58 us (3%)
    all_to_all x1, blocking collectives, per_device(): lax.all_to_all(need_list[0], 'atm', split_axis=0, concat_axis=0, tiled=True)  13.6 us
    pallas_call x1, Pallas kernels, fluxes_of(): pl.pallas_call(flux_body, out_shape=(pltpu.HBM((blocks * F, BLK), jnp.flo...  12.9 us
    ppermute x3, starting transfers between devices, sum_over_ring(): x = add(x, lax.ppermute(x, (axis, other), pairs))  10.5 us
    pallas_call x1, Pallas kernels, ocean_of(): pl.pallas_call(ocean_body, out_shape=jax.ShapeDtypeStruct((owners, F, OCE...  8.62 us
    all_to_all x1, starting transfers between devices, per_device(): lax.all_to_all(ocean_sums, 'atm', split_axis=0, concat_axis=0, tiled=True)  7.49 us
    ppermute x3, waiting for transfers between devices, sum_over_ring(): x = add(x, lax.ppermute(x, (axis, other), pairs))  7.29 us
    pallas_call x1, Pallas kernels, prep(): pl.pallas_call(prep_body, out_shape=(pltpu.HBM((blocks, BLK, OCELL), jnp....  6.43 us
    all_to_all x1, starting transfers between devices, per_device(): lax.all_to_all(serve(requests, atm_fields), 'atm', split_axis=0, concat_a...  5.03 us
  transfers between devices with their start and end apart: 6, of which 3 were waited for; matrix products, arithmetic and copies ran while one was open for 4% of the time, Pallas kernels for 16%

profile of v5, /device:TPU:2, one launch (start us, length us, event | category | flops | bytes accessed | tf_op | source)
XLA Modules:
  0.0 92.9 jit_solution(12061144432641205817)
XLA Ops:
  0.6 0.0 copy-start.4
  0.6 0.8 copy.18
  1.4 13.6 %all_to_all.32 = s32[32,1,4]{2,1,0:T(1,128)S(1)} all-to-all(s32[32,1,4]{2,1,0:T(1,128)S(1)} %copy.18), channel_id=1, replica_groups=mesh['ocn'=8,'atm'=32] {'atm'}, dimensions={0} | all-to-all | bytes 1024 | tf_op jit(solution)/shard_map/all_to_all | solution.py:390
  15.0 0.0 copy-start
  15.0 1.0 %copy-done = bf16[64,32,128]{2,1,0:T(8,128)(2,1)S(1)} copy-done((bf16[64,32,128]{2,1,0:T(8,128)(2,1)S(1)}, bf16[64,32,128]{2,1,0:T(8,128)(2,1)}, u32[]{:S(2)}) %copy-start) | copy-done | bytes 524312
  16.0 2.2 %serve.1 = bf16[128,32,128]{2,1,0:T(8,128)(2,1)} custom-call(s32[32,4]{1,0:T(8,128)S(1)} %bitcast.7, bf16[64,32,128]{2,1,0:T(8,128)(2,1)S(1)} %copy-done), custom_call_target="tpu_custom_call" | custom-call | tf_op jit(solution)/shard_map/serve/pallas_call | solution.py:89
  18.2 5.0 %all-to-all-start.1 = ((bf16[128,32,128]{2,1,0:T(8,128)(2,1)}), bf16[128,32,128]{2,1,0:T(8,128)(2,1)S(1)}, u32[]{:S(2)}, u32[]{:S(2)}) async-start(bf16[128,32,128]{2,1,0:T(8,128)(2,1)} %serve.1), calls=%async_computation.1 | async-start | bytes 2097152 | tf_op jit(solution)/shard_map/all_to_all | solution.py:391
  23.2 0.7 reshape.24.use_slot.slot_row
  23.9 1.2 %subtract_multiply_fusion = (f32[384,128]{1,0:T(8,128)S(1)}, f32[384,128]{1,0:T(8,128)S(1)}, f32[384,128]{1,0:T(8,128)S(1)}, f32[384,128]{1,0:T(8,128)S(1)}) fusion(s32[384,128]{1,0:T(8,128)} %param.23, f32[384,128]{1,0:T(8,128)} %param.17, s32[384]{0:T(512)} %param.22, f32[384,128]{1,0:T(8,128)} %param.16), kind=kLoop, calls=%fused_computation | loop fusion | flops 442368 | bytes 1377792 | tf_op jit(solution)/shard_map/mul | solution.py:398
  25.1 0.5 broadcast.10
  25.7 0.7 reduce.3
  26.4 0.1 reshape.23.requests
  26.5 0.0 copy-start.1
  26.5 0.9 copy-done.1
  27.4 0.0 copy-start.2
  27.4 0.9 copy-done.2
  28.3 0.0 copy-start.3
  28.3 0.9 copy-done.3
  29.2 6.4 %prep.1 = (bf16[384,128,128]{2,1,0:T(8,128)(2,1)}, f32[384,128]{1,0:T(8,128)S(1)}, f32[384,128]{1,0:T(8,128)S(1)}, s32[1,128]{1,0:T(1,128)S(1)}) custom-call(s32[384,128]{1,0:T(8,128)S(1)} %copy-done.1, f32[384,128]{1,0:T(8,128)S(1)} %copy-done.2, f32[384,128]{1,0:T(8,128)S(1)} %copy-done.3, s32[1,128]{1,0:T(1,128)S(1)} %reshape.23.requests), custom_call_target="tpu_custom_call" | custom-call | flops 12582912 | bytes 12582912 | tf_op jit(solution)/shard_map/prep/pallas_call | solution.py:113
  35.7 3.7 %all-to-all-done.1.table = bf16[128,32,128]{2,1,0:T(8,128)(2,1)S(1)} async-done(((bf16[128,32,128]{2,1,0:T(8,128)(2,1)}), bf16[128,32,128]{2,1,0:T(8,128)(2,1)S(1)}, u32[]{:S(2)}, u32[]{:S(2)}) %all-to-all-start.1) | async-done | bytes 1048608 | tf_op jit(solution)/shard_map/all_to_all | solution.py:391
  39.4 12.9 %fluxes.1 = (f32[12288,128]{1,0:T(8,128)}, f32[512,128]{1,0:T(8,128)}) custom-call(s32[1,384]{1,0:T(1,128)S(1)} %reshape.24.use_slot.slot_row, s32[1,384]{1,0:T(1,128)S(1)} %reshape.24.use_slot.slot_row, bf16[128,32,128]{2,1,0:T(8,128)(2,1)S(1)} %all-to-all-done.1.table, bf16[384,128,128]{2,1,0:T(8,128)(2,1)} %weights.1, ...), custom_call_target="tpu_custom_call" | custom-call | tf_op jit(solution)/shard_map/fluxes/pallas_call | solution.py:232
  52.4 5.0 %all-to-all-start.2 = ((f32[32,16,128]{2,1,0:T(8,128)}), f32[32,16,128]{2,1,0:T(8,128)S(1)}, u32[]{:S(2)}, u32[]{:S(2)}) async-start(f32[32,16,128]{2,1,0:T(8,128)} %bitcast.2), calls=%async_computation.2 | async-start | bytes 524288 | tf_op jit(solution)/shard_map/all_to_all | solution.py:400
  57.4 0.0 copy-done.4
  57.4 8.6 %ocean.1.ocean_sums = f32[32,32,128]{2,1,0:T(8,128)} custom-call(s32[1,384]{1,0:T(1,128)S(1)} %reshape.25.ocean_block, f32[12288,128]{1,0:T(8,128)} %get-tuple-element.12.rows_far, bf16[384,128,128]{2,1,0:T(8,128)(2,1)} %get-tuple-element.13.hot_far, f32[384,128]{1,0:T(8,128)S(1)} %get-tuple-element.14.passive_weight), custom_call_target="tpu_custom_call" | custom-call | flops 201326592 | bytes 18874368 | tf_op jit(solution)/shard_map/ocean/pallas_call | solution.py:298
  66.0 0.0 all-to-all-done.2
  66.0 0.2 owner_sums.1.left
  66.2 2.0 %collective-permute-start = (f32[256,128]{1,0:T(8,128)S(1)}, f32[256,128]{1,0:T(8,128)S(1)}, u32[]{:S(2)}, u32[]{:S(2)}) collective-permute-start(f32[256,128]{1,0:T(8,128)S(1)} %owner_sums.1.left), channel_id=1, source_target_pairs={{0,32},{1,33},{2,34},{3,35},{4,36},{5,37},{6,38},{7,39},{8,40},{9,... | collective-permute-start | bytes 393224 | tf_op jit(solution)/shard_map/ppermute | solution.py:369
  68.2 7.5 %all-to-all-start.3 = ((f32[32,32,128]{2,1,0:T(8,128)}), f32[32,32,128]{2,1,0:T(8,128)S(1)}, u32[]{:S(2)}, u32[]{:S(2)}) async-start(f32[32,32,128]{2,1,0:T(8,128)} %ocean.1.ocean_sums), calls=%async_computation.3 | async-start | bytes 1048576 | tf_op jit(solution)/shard_map/all_to_all | solution.py:403
  75.7 0.0 collective-permute-done.right
  75.8 3.4 %collective-permute-start.1 = (f32[256,128]{1,0:T(8,128)S(1)}, f32[256,128]{1,0:T(8,128)S(1)}, u32[]{:S(2)}, u32[]{:S(2)}) collective-permute-start(f32[256,128]{1,0:T(8,128)S(1)} %add.7.left), channel_id=1, source_target_pairs={{0,64},{1,193},{2,66},{3,195},{4,68},{5,197},{6,70},{7,199},{8,72}... | collective-permute-start | bytes 393224 | tf_op jit(solution)/shard_map/ppermute | solution.py:369
  79.1 3.9 %collective-permute-done.1.right = f32[256,128]{1,0:T(8,128)S(1)} collective-permute-done((f32[256,128]{1,0:T(8,128)S(1)}, f32[256,128]{1,0:T(8,128)S(1)}, u32[]{:S(2)}, u32[]{:S(2)}) %collective-permute-start.1) | collective-permute-done | bytes 131104 | tf_op jit(solution)/shard_map/ppermute | solution.py:369
  83.0 5.1 %collective-permute-start.2 = (f32[256,128]{1,0:T(8,128)S(1)}, f32[256,128]{1,0:T(8,128)S(1)}, u32[]{:S(2)}, u32[]{:S(2)}) collective-permute-start(f32[256,128]{1,0:T(8,128)S(1)} %add.8.left), channel_id=1, source_target_pairs={{0,224},{1,97},{2,226},{3,99},{4,228},{5,101},{6,230},{7,103},{8,2... | collective-permute-start | bytes 393224 | tf_op jit(solution)/shard_map/ppermute | solution.py:369
  88.2 0.0 all-to-all-done.3
  88.2 0.7 reduce_sum.9
  88.8 3.4 %collective-permute-done.2.right = f32[256,128]{1,0:T(8,128)S(1)} collective-permute-done((f32[256,128]{1,0:T(8,128)S(1)}, f32[256,128]{1,0:T(8,128)S(1)}, u32[]{:S(2)}, u32[]{:S(2)}) %collective-permute-start.2) | collective-permute-done | bytes 131104 | tf_op jit(solution)/shard_map/ppermute | solution.py:369
  92.2 0.7 add.9
  (3 shorter events, 0.0 us)
Async XLA Ops:
  0.6 56.8 %copy-start.4 = (s32[384]{0:T(512)S(1)}, s32[384]{0:T(512)}, u32[]{:S(2)}) copy-start(s32[384]{0:T(512)} %param.20) | copy-start | bytes 4612
  15.0 1.0 %copy-start = (bf16[64,32,128]{2,1,0:T(8,128)(2,1)S(1)}, bf16[64,32,128]{2,1,0:T(8,128)(2,1)}, u32[]{:S(2)}) copy-start(bf16[64,32,128]{2,1,0:T(8,128)(2,1)} %fields.1) | copy-start | bytes 1572868
  18.2 21.3 %all-to-all-start.1 = ((bf16[128,32,128]{2,1,0:T(8,128)(2,1)}), bf16[128,32,128]{2,1,0:T(8,128)(2,1)S(1)}, u32[]{:S(2)}, u32[]{:S(2)}) async-start(bf16[128,32,128]{2,1,0:T(8,128)(2,1)} %serve.1), calls=%async_computation.1 | async-start | bytes 2097152 | tf_op jit(solution)/shard_map/all_to_all | solution.py:391
  26.5 0.9 %copy-start.1 = (s32[384,128]{1,0:T(8,128)S(1)}, s32[384,128]{1,0:T(8,128)}, u32[]{:S(2)}) copy-start(s32[384,128]{1,0:T(8,128)} %ocean_cell.1) | copy-start | bytes 589828
  27.4 0.9 copy-start.2
  28.3 0.9 copy-start.3
  52.4 13.7 %all-to-all-start.2 = ((f32[32,16,128]{2,1,0:T(8,128)}), f32[32,16,128]{2,1,0:T(8,128)S(1)}, u32[]{:S(2)}, u32[]{:S(2)}) async-start(f32[32,16,128]{2,1,0:T(8,128)} %bitcast.2), calls=%async_computation.2 | async-start | bytes 524288 | tf_op jit(solution)/shard_map/all_to_all | solution.py:400
  66.2 9.5 %collective-permute-start = (f32[256,128]{1,0:T(8,128)S(1)}, f32[256,128]{1,0:T(8,128)S(1)}, u32[]{:S(2)}, u32[]{:S(2)}) collective-permute-start(f32[256,128]{1,0:T(8,128)S(1)} %owner_sums.1.left), channel_id=1, source_target_pairs={{0,32},{1,33},{2,34},{3,35},{4,36},{5,37},{6,38},{7,39},{8,40},{9,... | collective-permute-start | bytes 393224 | tf_op jit(solution)/shard_map/ppermute | solution.py:369
  68.2 20.0 %all-to-all-start.3 = ((f32[32,32,128]{2,1,0:T(8,128)}), f32[32,32,128]{2,1,0:T(8,128)S(1)}, u32[]{:S(2)}, u32[]{:S(2)}) async-start(f32[32,32,128]{2,1,0:T(8,128)} %ocean.1.ocean_sums), calls=%async_computation.3 | async-start | bytes 1048576 | tf_op jit(solution)/shard_map/all_to_all | solution.py:403
  75.8 7.2 %collective-permute-start.1 = (f32[256,128]{1,0:T(8,128)S(1)}, f32[256,128]{1,0:T(8,128)S(1)}, u32[]{:S(2)}, u32[]{:S(2)}) collective-permute-start(f32[256,128]{1,0:T(8,128)S(1)} %add.7.left), channel_id=1, source_target_pairs={{0,64},{1,193},{2,66},{3,195},{4,68},{5,197},{6,70},{7,199},{8,72}... | collective-permute-start | bytes 393224 | tf_op jit(solution)/shard_map/ppermute | solution.py:369
  83.0 9.2 %collective-permute-start.2 = (f32[256,128]{1,0:T(8,128)S(1)}, f32[256,128]{1,0:T(8,128)S(1)}, u32[]{:S(2)}, u32[]{:S(2)}) collective-permute-start(f32[256,128]{1,0:T(8,128)S(1)} %add.8.left), channel_id=1, source_target_pairs={{0,224},{1,97},{2,226},{3,99},{4,228},{5,101},{6,230},{7,103},{8,2... | collective-permute-start | bytes 393224 | tf_op jit(solution)/shard_map/ppermute | solution.py:369

commit v6 on v5

--- a/solution.py
+++ b/solution.py
@@ -20,8 +20,9 @@
 flux_scale = 40.0
 
 GROUP = 64
+FLUX_GROUP = 96
 MIB = 1 << 20
-ADD_COST = pl.CostEstimate(flops=1500000000, bytes_accessed=3 << 17, transcendentals=0)
+ADD_COST = pl.CostEstimate(flops=4000000000, bytes_accessed=3 << 17, transcendentals=0)
 VMEM = pltpu.VMEM
 SMEM = pltpu.SMEM
 
@@ -166,23 +167,23 @@
     out_sem,
 ):
     blocks = held.shape[0]
-    parts = blocks // GROUP
+    parts = blocks // FLUX_GROUP
 
     def fetch(p):
-        share = pl.ds(pl.multiple_of(p * GROUP, GROUP), GROUP)
+        share = pl.ds(pl.multiple_of(p * FLUX_GROUP, FLUX_GROUP), FLUX_GROUP)
         return pltpu.make_async_copy(weights.at[share], held.at[share], in_sem.at[p])
 
     def put(p):
-        share = pl.ds(pl.multiple_of(p * (GROUP * F), GROUP * F), GROUP * F)
+        share = pl.ds(pl.multiple_of(p * (FLUX_GROUP * F), FLUX_GROUP * F), FLUX_GROUP * F)
         return pltpu.make_async_copy(rows.at[share], rows_out.at[share], out_sem.at[p])
 
     for p in range(parts):
         fetch(p).start()
 
     def part(p, _):
-        base = p * GROUP
+        base = p * FLUX_GROUP
         fetch(p).wait()
-        for i in range(0, GROUP, 2):
+        for i in range(0, FLUX_GROUP, 2):
             k = base + i
             both = lax.dot_general(
                 jnp.concatenate([table[use_slot[0, k]], table[use_slot[0, k + 1]]], axis=0),
@@ -192,8 +193,8 @@
             )
             rows[pl.ds(pl.multiple_of(k * F, F), F), :] = both[:F, :BLK]
             rows[pl.ds(pl.multiple_of(k * F + F, F), F), :] = both[F:, BLK:]
-        mine = pl.ds(pl.multiple_of(base, GROUP), GROUP)
-        row = lambda f: pl.ds(base * F + f, GROUP, stride=F)
+        mine = pl.ds(pl.multiple_of(base, FLUX_GROUP), FLUX_GROUP)
+        row = lambda f: pl.ds(base * F + f, FLUX_GROUP, stride=F)
         fluxes = flux_rows(
             *(rows[row(f), :] for f in range(4)),
             surf_temp[mine, :],
@@ -205,7 +206,7 @@
         for f in range(4):
             rows[row(f), :] = weight * fluxes[f]
         put(p).start()
-        for i in range(0, GROUP, 2):
+        for i in range(0, FLUX_GROUP, 2):
             k = base + i
             left = jnp.concatenate(
                 [
@@ -241,8 +242,8 @@
             pltpu.VMEM(weights.shape, weights.dtype),
             pltpu.VMEM((blocks * F, BLK), jnp.float32),
             pltpu.VMEM((blocks * 8, ACELL), jnp.float32),
-            pltpu.SemaphoreType.DMA((blocks // GROUP,)),
-            pltpu.SemaphoreType.DMA((blocks // GROUP,)),
+            pltpu.SemaphoreType.DMA((blocks // FLUX_GROUP,)),
+            pltpu.SemaphoreType.DMA((blocks // FLUX_GROUP,)),
         ],
         compiler_params=pltpu.CompilerParams(vmem_limit_bytes=30 * MIB),
         name="fluxes",

time: 93.4 us -> 98.1 us (1.050)
  the two profiles are of different devices: /device:TPU:2 before, /device:TPU:1 now
where the time goes in v6:
time: 98.1 us; the launch traced here: 97.5 us
  Pallas kernels  30.3 us (31%)
  starting transfers between devices  24 us (24%)
  waiting for transfers between devices  18.6 us (19%)
  blocking collectives  15.3 us (16%)
  local copies, waits for them, and re-layouts  5.89 us (6%)
  other arithmetic  2.58 us (3%)
    all_to_all x1, blocking collectives, per_device(): lax.all_to_all(need_list[0], 'atm', split_axis=0, concat_axis=0, tiled=True)  15.3 us
    pallas_call x1, Pallas kernels, fluxes_of(): pl.pallas_call(flux_body, out_shape=(pltpu.HBM((blocks * F, BLK), jnp.flo...  12.2 us
    all_to_all x1, waiting for transfers between devices, per_device(): lax.all_to_all(ocean_sums, 'atm', split_axis=0, concat_axis=0, tiled=True)  9.8 us
    ppermute x3, starting transfers between devices, sum_over_ring(): x = add(x, lax.ppermute(x, (axis, other), pairs))  9.13 us
    pallas_call x1, Pallas kernels, ocean_of(): pl.pallas_call(ocean_body, out_shape=jax.ShapeDtypeStruct((owners, F, OCE...  8.62 us
    all_to_all x1, starting transfers between devices, per_device(): lax.all_to_all(ocean_sums, 'atm', split_axis=0, concat_axis=0, tiled=True)  6.75 us
    pallas_call x1, Pallas kernels, prep(): pl.pallas_call(prep_body, out_shape=(pltpu.HBM((blocks, BLK, OCELL), jnp....  6.43 us
    all_to_all x1, waiting for transfers between devices, per_device(): lax.all_to_all(serve(requests, atm_fields), 'atm', split_axis=0, concat_a...  4.81 us
  transfers between devices with their start and end apart: 6, of which 4 were waited for; matrix products, arithmetic and copies ran while one was open for 4% of the time, Pallas kernels for 15%

profile of v6, /device:TPU:1, one launch (start us, length us, event | category | flops | bytes accessed | tf_op | source)
XLA Modules:
  0.0 97.5 jit_solution(3252458650930693282)
XLA Ops:
  0.6 0.0 copy-start.4
  0.6 0.8 copy.18
  1.4 15.3 %all_to_all.32 = s32[32,1,4]{2,1,0:T(1,128)S(1)} all-to-all(s32[32,1,4]{2,1,0:T(1,128)S(1)} %copy.18), channel_id=1, replica_groups=mesh['ocn'=8,'atm'=32] {'atm'}, dimensions={0} | all-to-all | bytes 1024 | tf_op jit(solution)/shard_map/all_to_all | solution.py:391
  16.7 0.0 copy-start
  16.7 1.0 %copy-done = bf16[64,32,128]{2,1,0:T(8,128)(2,1)S(1)} copy-done((bf16[64,32,128]{2,1,0:T(8,128)(2,1)S(1)}, bf16[64,32,128]{2,1,0:T(8,128)(2,1)}, u32[]{:S(2)}) %copy-start) | copy-done | bytes 524312
  17.8 2.2 %serve.1 = bf16[128,32,128]{2,1,0:T(8,128)(2,1)} custom-call(s32[32,4]{1,0:T(8,128)S(1)} %bitcast.7, bf16[64,32,128]{2,1,0:T(8,128)(2,1)S(1)} %copy-done), custom_call_target="tpu_custom_call" | custom-call | tf_op jit(solution)/shard_map/serve/pallas_call | solution.py:90
  19.9 4.2 %all-to-all-start.1 = ((bf16[128,32,128]{2,1,0:T(8,128)(2,1)}), bf16[128,32,128]{2,1,0:T(8,128)(2,1)S(1)}, u32[]{:S(2)}, u32[]{:S(2)}) async-start(bf16[128,32,128]{2,1,0:T(8,128)(2,1)} %serve.1), calls=%async_computation.1 | async-start | bytes 2097152 | tf_op jit(solution)/shard_map/all_to_all | solution.py:392
  24.2 0.7 reshape.24.use_slot.slot_row
  24.9 1.2 %subtract_multiply_fusion = (f32[384,128]{1,0:T(8,128)S(1)}, f32[384,128]{1,0:T(8,128)S(1)}, f32[384,128]{1,0:T(8,128)S(1)}, f32[384,128]{1,0:T(8,128)S(1)}) fusion(s32[384,128]{1,0:T(8,128)} %param.23, f32[384,128]{1,0:T(8,128)} %param.17, s32[384]{0:T(512)} %param.22, f32[384,128]{1,0:T(8,128)} %param.16), kind=kLoop, calls=%fused_computation | loop fusion | flops 442368 | bytes 1377792 | tf_op jit(solution)/shard_map/mul | solution.py:399
  26.1 0.5 broadcast.10
  26.6 0.7 reduce.3
  27.3 0.1 reshape.23.requests
  27.4 0.0 copy-start.1
  27.4 0.9 copy-done.1
  28.4 0.0 copy-start.2
  28.4 0.9 copy-done.2
  29.3 0.0 copy-start.3
  29.3 0.9 copy-done.3
  30.2 6.4 %prep.1 = (bf16[384,128,128]{2,1,0:T(8,128)(2,1)}, f32[384,128]{1,0:T(8,128)S(1)}, f32[384,128]{1,0:T(8,128)S(1)}, s32[1,128]{1,0:T(1,128)S(1)}) custom-call(s32[384,128]{1,0:T(8,128)S(1)} %copy-done.1, f32[384,128]{1,0:T(8,128)S(1)} %copy-done.2, f32[384,128]{1,0:T(8,128)S(1)} %copy-done.3, s32[1,128]{1,0:T(1,128)S(1)} %reshape.23.requests), custom_call_target="tpu_custom_call" | custom-call | flops 12582912 | bytes 12582912 | tf_op jit(solution)/shard_map/prep/pallas_call | solution.py:114
  36.6 4.8 %all-to-all-done.1.table = bf16[128,32,128]{2,1,0:T(8,128)(2,1)S(1)} async-done(((bf16[128,32,128]{2,1,0:T(8,128)(2,1)}), bf16[128,32,128]{2,1,0:T(8,128)(2,1)S(1)}, u32[]{:S(2)}, u32[]{:S(2)}) %all-to-all-start.1) | async-done | bytes 1048608 | tf_op jit(solution)/shard_map/all_to_all | solution.py:392
  41.5 12.2 %fluxes.1 = (f32[12288,128]{1,0:T(8,128)}, f32[512,128]{1,0:T(8,128)}) custom-call(s32[1,384]{1,0:T(1,128)S(1)} %reshape.24.use_slot.slot_row, s32[1,384]{1,0:T(1,128)S(1)} %reshape.24.use_slot.slot_row, bf16[128,32,128]{2,1,0:T(8,128)(2,1)S(1)} %all-to-all-done.1.table, bf16[384,128,128]{2,1,0:T(8,128)(2,1)} %weights.1, ...), custom_call_target="tpu_custom_call" | custom-call | tf_op jit(solution)/shard_map/fluxes/pallas_call | solution.py:233
  53.7 3.9 %all-to-all-start.2 = ((f32[32,16,128]{2,1,0:T(8,128)}), f32[32,16,128]{2,1,0:T(8,128)S(1)}, u32[]{:S(2)}, u32[]{:S(2)}) async-start(f32[32,16,128]{2,1,0:T(8,128)} %bitcast.2), calls=%async_computation.2 | async-start | bytes 524288 | tf_op jit(solution)/shard_map/all_to_all | solution.py:401
  57.6 0.0 copy-done.4
  57.6 8.6 %ocean.1.ocean_sums = f32[32,32,128]{2,1,0:T(8,128)} custom-call(s32[1,384]{1,0:T(1,128)S(1)} %reshape.25.ocean_block, f32[12288,128]{1,0:T(8,128)} %get-tuple-element.12.rows_far, bf16[384,128,128]{2,1,0:T(8,128)(2,1)} %get-tuple-element.13.hot_far, f32[384,128]{1,0:T(8,128)S(1)} %get-tuple-element.14.passive_weight), custom_call_target="tpu_custom_call" | custom-call | flops 201326592 | bytes 18874368 | tf_op jit(solution)/shard_map/ocean/pallas_call | solution.py:299
  66.2 0.4 all-to-all-done.2
  66.6 0.2 owner_sums.1.left
  66.8 1.7 %collective-permute-start = (f32[256,128]{1,0:T(8,128)S(1)}, f32[256,128]{1,0:T(8,128)S(1)}, u32[]{:S(2)}, u32[]{:S(2)}) collective-permute-start(f32[256,128]{1,0:T(8,128)S(1)} %owner_sums.1.left), channel_id=1, source_target_pairs={{0,32},{1,33},{2,34},{3,35},{4,36},{5,37},{6,38},{7,39},{8,40},{9,... | collective-permute-start | bytes 393224 | tf_op jit(solution)/shard_map/ppermute | solution.py:370
  68.5 3.6 %collective-permute-done.right = f32[256,128]{1,0:T(8,128)S(1)} collective-permute-done((f32[256,128]{1,0:T(8,128)S(1)}, f32[256,128]{1,0:T(8,128)S(1)}, u32[]{:S(2)}, u32[]{:S(2)}) %collective-permute-start) | collective-permute-done | bytes 131104 | tf_op jit(solution)/shard_map/ppermute | solution.py:370
  72.1 5.7 %collective-permute-start.1 = (f32[256,128]{1,0:T(8,128)S(1)}, f32[256,128]{1,0:T(8,128)S(1)}, u32[]{:S(2)}, u32[]{:S(2)}) collective-permute-start(f32[256,128]{1,0:T(8,128)S(1)} %add.7.left), channel_id=1, source_target_pairs={{0,64},{1,193},{2,66},{3,195},{4,68},{5,197},{6,70},{7,199},{8,72}... | collective-permute-start | bytes 393224 | tf_op jit(solution)/shard_map/ppermute | solution.py:370
  77.9 6.7 %all-to-all-start.3 = ((f32[32,32,128]{2,1,0:T(8,128)}), f32[32,32,128]{2,1,0:T(8,128)S(1)}, u32[]{:S(2)}, u32[]{:S(2)}) async-start(f32[32,32,128]{2,1,0:T(8,128)} %ocean.1.ocean_sums), calls=%async_computation.3 | async-start | bytes 1048576 | tf_op jit(solution)/shard_map/all_to_all | solution.py:404
  84.6 0.0 collective-permute-done.1.right
  84.6 1.7 %collective-permute-start.2 = (f32[256,128]{1,0:T(8,128)S(1)}, f32[256,128]{1,0:T(8,128)S(1)}, u32[]{:S(2)}, u32[]{:S(2)}) collective-permute-start(f32[256,128]{1,0:T(8,128)S(1)} %add.8.left), channel_id=1, source_target_pairs={{0,224},{1,97},{2,226},{3,99},{4,228},{5,101},{6,230},{7,103},{8,2... | collective-permute-start | bytes 393224 | tf_op jit(solution)/shard_map/ppermute | solution.py:370
  86.4 9.8 %all-to-all-done.3 = f32[32,32,128]{2,1,0:T(8,128)S(1)} async-done(((f32[32,32,128]{2,1,0:T(8,128)}), f32[32,32,128]{2,1,0:T(8,128)S(1)}, u32[]{:S(2)}, u32[]{:S(2)}) %all-to-all-start.3) | async-done | bytes 524320 | tf_op jit(solution)/shard_map/all_to_all | solution.py:404
  96.2 0.6 reduce_sum.9
  96.8 0.0 collective-permute-done.2.right
  96.8 0.7 add.9
  (3 shorter events, 0.0 us)
Async XLA Ops:
  0.6 57.0 %copy-start.4 = (s32[384]{0:T(512)S(1)}, s32[384]{0:T(512)}, u32[]{:S(2)}) copy-start(s32[384]{0:T(512)} %param.20) | copy-start | bytes 4612
  16.7 1.0 %copy-start = (bf16[64,32,128]{2,1,0:T(8,128)(2,1)S(1)}, bf16[64,32,128]{2,1,0:T(8,128)(2,1)}, u32[]{:S(2)}) copy-start(bf16[64,32,128]{2,1,0:T(8,128)(2,1)} %fields.1) | copy-start | bytes 1572868
  19.9 21.5 %all-to-all-start.1 = ((bf16[128,32,128]{2,1,0:T(8,128)(2,1)}), bf16[128,32,128]{2,1,0:T(8,128)(2,1)S(1)}, u32[]{:S(2)}, u32[]{:S(2)}) async-start(bf16[128,32,128]{2,1,0:T(8,128)(2,1)} %serve.1), calls=%async_computation.1 | async-start | bytes 2097152 | tf_op jit(solution)/shard_map/all_to_all | solution.py:392
  27.4 0.9 copy-start.1
  28.4 0.9 copy-start.2
  29.3 0.9 copy-start.3
  53.7 12.9 %all-to-all-start.2 = ((f32[32,16,128]{2,1,0:T(8,128)}), f32[32,16,128]{2,1,0:T(8,128)S(1)}, u32[]{:S(2)}, u32[]{:S(2)}) async-start(f32[32,16,128]{2,1,0:T(8,128)} %bitcast.2), calls=%async_computation.2 | async-start | bytes 524288 | tf_op jit(solution)/shard_map/all_to_all | solution.py:401
  66.8 5.3 %collective-permute-start = (f32[256,128]{1,0:T(8,128)S(1)}, f32[256,128]{1,0:T(8,128)S(1)}, u32[]{:S(2)}, u32[]{:S(2)}) collective-permute-start(f32[256,128]{1,0:T(8,128)S(1)} %owner_sums.1.left), channel_id=1, source_target_pairs={{0,32},{1,33},{2,34},{3,35},{4,36},{5,37},{6,38},{7,39},{8,40},{9,... | collective-permute-start | bytes 393224 | tf_op jit(solution)/shard_map/ppermute | solution.py:370
  72.1 12.5 %collective-permute-start.1 = (f32[256,128]{1,0:T(8,128)S(1)}, f32[256,128]{1,0:T(8,128)S(1)}, u32[]{:S(2)}, u32[]{:S(2)}) collective-permute-start(f32[256,128]{1,0:T(8,128)S(1)} %add.7.left), channel_id=1, source_target_pairs={{0,64},{1,193},{2,66},{3,195},{4,68},{5,197},{6,70},{7,199},{8,72}... | collective-permute-start | bytes 393224 | tf_op jit(solution)/shard_map/ppermute | solution.py:370
  77.9 18.3 %all-to-all-start.3 = ((f32[32,32,128]{2,1,0:T(8,128)}), f32[32,32,128]{2,1,0:T(8,128)S(1)}, u32[]{:S(2)}, u32[]{:S(2)}) async-start(f32[32,32,128]{2,1,0:T(8,128)} %ocean.1.ocean_sums), calls=%async_computation.3 | async-start | bytes 1048576 | tf_op jit(solution)/shard_map/all_to_all | solution.py:404
  84.6 12.2 %collective-permute-start.2 = (f32[256,128]{1,0:T(8,128)S(1)}, f32[256,128]{1,0:T(8,128)S(1)}, u32[]{:S(2)}, u32[]{:S(2)}) collective-permute-start(f32[256,128]{1,0:T(8,128)S(1)} %add.8.left), channel_id=1, source_target_pairs={{0,224},{1,97},{2,226},{3,99},{4,228},{5,101},{6,230},{7,103},{8,2... | collective-permute-start | bytes 393224 | tf_op jit(solution)/shard_map/ppermute | solution.py:370

commit v7 on v6

--- a/solution.py
+++ b/solution.py
@@ -22,7 +22,7 @@
 GROUP = 64
 FLUX_GROUP = 96
 MIB = 1 << 20
-ADD_COST = pl.CostEstimate(flops=4000000000, bytes_accessed=3 << 17, transcendentals=0)
+ADD_COST = pl.CostEstimate(flops=1500000000, bytes_accessed=3 << 17, transcendentals=0)
 VMEM = pltpu.VMEM
 SMEM = pltpu.SMEM
 
@@ -355,9 +355,8 @@
 
 def sum_over_ring(x, axis, other):
     ranks, places = lax.axis_size(axis), lax.axis_size(other)
-    bit = 1
-    while bit < ranks:
-        mask = ranks - 1 if 2 * bit == ranks else bit
+    masks = [ranks - 1] + [1 << bit for bit in range(ranks.bit_length() - 2)]
+    for mask in masks:
 
         def partner(i, turn):
             return (((i - turn) % ranks) ^ mask) + turn
@@ -368,7 +367,6 @@
             for p in range(places)
         ]
         x = add(x, lax.ppermute(x, (axis, other), pairs))
-        bit *= 2
     return x
 
 

time: 98.1 us -> 93.8 us (0.956)
  the two profiles are of different devices: /device:TPU:1 before, /device:TPU:2 now
where the time goes in v7:
time: 93.8 us; the launch traced here: 92.4 us
  Pallas kernels  30.3 us (32%)
  starting transfers between devices  27.7 us (30%)
  blocking collectives  13.6 us (14%)
  waiting for transfers between devices  11.6 us (12%)
  local copies, waits for them, and re-layouts  5.89 us (6%)
  other arithmetic  2.58 us (3%)
    all_to_all x1, blocking collectives, per_device(): lax.all_to_all(need_list[0], 'atm', split_axis=0, concat_axis=0, tiled=True)  13.6 us
    pallas_call x1, Pallas kernels, fluxes_of(): pl.pallas_call(flux_body, out_shape=(pltpu.HBM((blocks * F, BLK), jnp.flo...  12.2 us
    ppermute x3, starting transfers between devices, sum_over_ring(): x = add(x, lax.ppermute(x, (axis, other), pairs))  10.2 us
    pallas_call x1, Pallas kernels, ocean_of(): pl.pallas_call(ocean_body, out_shape=jax.ShapeDtypeStruct((owners, F, OCE...  8.62 us
    all_to_all x1, starting transfers between devices, per_device(): lax.all_to_all(ocean_sums, 'atm', split_axis=0, concat_axis=0, tiled=True)  7.49 us
    pallas_call x1, Pallas kernels, prep(): pl.pallas_call(prep_body, out_shape=(pltpu.HBM((blocks, BLK, OCELL), jnp....  6.43 us
    ppermute x3, waiting for transfers between devices, sum_over_ring(): x = add(x, lax.ppermute(x, (axis, other), pairs))  5.51 us
    all_to_all x1, starting transfers between devices, per_device(): lax.all_to_all(serve(requests, atm_fields), 'atm', split_axis=0, concat_a...  5.03 us
  transfers between devices with their start and end apart: 6, of which 4 were waited for; matrix products, arithmetic and copies ran while one was open for 4% of the time, Pallas kernels for 16%

profile of v7, /device:TPU:2, one launch (start us, length us, event | category | flops | bytes accessed | tf_op | source)
XLA Modules:
  0.0 92.4 jit_solution(16521811518322713648)
XLA Ops:
  0.6 0.0 copy-start.4
  0.6 0.8 copy.18
  1.4 13.6 %all_to_all.32 = s32[32,1,4]{2,1,0:T(1,128)S(1)} all-to-all(s32[32,1,4]{2,1,0:T(1,128)S(1)} %copy.18), channel_id=1, replica_groups=mesh['ocn'=8,'atm'=32] {'atm'}, dimensions={0} | all-to-all | bytes 1024 | tf_op jit(solution)/shard_map/all_to_all | solution.py:389
  15.0 0.0 copy-start
  15.0 1.0 %copy-done = bf16[64,32,128]{2,1,0:T(8,128)(2,1)S(1)} copy-done((bf16[64,32,128]{2,1,0:T(8,128)(2,1)S(1)}, bf16[64,32,128]{2,1,0:T(8,128)(2,1)}, u32[]{:S(2)}) %copy-start) | copy-done | bytes 524312
  16.0 2.2 %serve.1 = bf16[128,32,128]{2,1,0:T(8,128)(2,1)} custom-call(s32[32,4]{1,0:T(8,128)S(1)} %bitcast.7, bf16[64,32,128]{2,1,0:T(8,128)(2,1)S(1)} %copy-done), custom_call_target="tpu_custom_call" | custom-call | tf_op jit(solution)/shard_map/serve/pallas_call | solution.py:90
  18.2 5.0 %all-to-all-start.1 = ((bf16[128,32,128]{2,1,0:T(8,128)(2,1)}), bf16[128,32,128]{2,1,0:T(8,128)(2,1)S(1)}, u32[]{:S(2)}, u32[]{:S(2)}) async-start(bf16[128,32,128]{2,1,0:T(8,128)(2,1)} %serve.1), calls=%async_computation.1 | async-start | bytes 2097152 | tf_op jit(solution)/shard_map/all_to_all | solution.py:390
  23.2 0.7 reshape.24.use_slot.slot_row
  23.9 1.2 %subtract_multiply_fusion = (f32[384,128]{1,0:T(8,128)S(1)}, f32[384,128]{1,0:T(8,128)S(1)}, f32[384,128]{1,0:T(8,128)S(1)}, f32[384,128]{1,0:T(8,128)S(1)}) fusion(s32[384,128]{1,0:T(8,128)} %param.23, f32[384,128]{1,0:T(8,128)} %param.17, s32[384]{0:T(512)} %param.22, f32[384,128]{1,0:T(8,128)} %param.16), kind=kLoop, calls=%fused_computation | loop fusion | flops 442368 | bytes 1377792 | tf_op jit(solution)/shard_map/mul | solution.py:397
  25.1 0.5 broadcast.10
  25.7 0.7 reduce.3
  26.4 0.1 reshape.23.requests
  26.5 0.0 copy-start.1
  26.5 0.9 copy-done.1
  27.4 0.0 copy-start.2
  27.4 0.9 %copy-done.2 = f32[384,128]{1,0:T(8,128)S(1)} copy-done((f32[384,128]{1,0:T(8,128)S(1)}, f32[384,128]{1,0:T(8,128)}, u32[]{:S(2)}) %copy-start.2) | copy-done | bytes 196632
  28.3 0.0 copy-start.3
  28.3 0.9 %copy-done.3 = f32[384,128]{1,0:T(8,128)S(1)} copy-done((f32[384,128]{1,0:T(8,128)S(1)}, f32[384,128]{1,0:T(8,128)}, u32[]{:S(2)}) %copy-start.3) | copy-done | bytes 196632
  29.2 6.4 %prep.1 = (bf16[384,128,128]{2,1,0:T(8,128)(2,1)}, f32[384,128]{1,0:T(8,128)S(1)}, f32[384,128]{1,0:T(8,128)S(1)}, s32[1,128]{1,0:T(1,128)S(1)}) custom-call(s32[384,128]{1,0:T(8,128)S(1)} %copy-done.1, f32[384,128]{1,0:T(8,128)S(1)} %copy-done.2, f32[384,128]{1,0:T(8,128)S(1)} %copy-done.3, s32[1,128]{1,0:T(1,128)S(1)} %reshape.23.requests), custom_call_target="tpu_custom_call" | custom-call | flops 12582912 | bytes 12582912 | tf_op jit(solution)/shard_map/prep/pallas_call | solution.py:114
  35.7 3.7 %all-to-all-done.1.table = bf16[128,32,128]{2,1,0:T(8,128)(2,1)S(1)} async-done(((bf16[128,32,128]{2,1,0:T(8,128)(2,1)}), bf16[128,32,128]{2,1,0:T(8,128)(2,1)S(1)}, u32[]{:S(2)}, u32[]{:S(2)}) %all-to-all-start.1) | async-done | bytes 1048608 | tf_op jit(solution)/shard_map/all_to_all | solution.py:390
  39.4 12.2 %fluxes.1 = (f32[12288,128]{1,0:T(8,128)}, f32[512,128]{1,0:T(8,128)}) custom-call(s32[1,384]{1,0:T(1,128)S(1)} %reshape.24.use_slot.slot_row, s32[1,384]{1,0:T(1,128)S(1)} %reshape.24.use_slot.slot_row, bf16[128,32,128]{2,1,0:T(8,128)(2,1)S(1)} %all-to-all-done.1.table, bf16[384,128,128]{2,1,0:T(8,128)(2,1)} %weights.1, ...), custom_call_target="tpu_custom_call" | custom-call | tf_op jit(solution)/shard_map/fluxes/pallas_call | solution.py:233
  51.6 5.0 %all-to-all-start.2 = ((f32[32,16,128]{2,1,0:T(8,128)}), f32[32,16,128]{2,1,0:T(8,128)S(1)}, u32[]{:S(2)}, u32[]{:S(2)}) async-start(f32[32,16,128]{2,1,0:T(8,128)} %bitcast.2), calls=%async_computation.2 | async-start | bytes 524288 | tf_op jit(solution)/shard_map/all_to_all | solution.py:399
  56.6 0.0 copy-done.4
  56.6 8.6 %ocean.1.ocean_sums = f32[32,32,128]{2,1,0:T(8,128)} custom-call(s32[1,384]{1,0:T(1,128)S(1)} %reshape.25.ocean_block, f32[12288,128]{1,0:T(8,128)} %get-tuple-element.12.rows_far, bf16[384,128,128]{2,1,0:T(8,128)(2,1)} %get-tuple-element.13.hot_far, f32[384,128]{1,0:T(8,128)S(1)} %get-tuple-element.14.passive_weight), custom_call_target="tpu_custom_call" | custom-call | flops 201326592 | bytes 18874368 | tf_op jit(solution)/shard_map/ocean/pallas_call | solution.py:299
  65.3 0.0 all-to-all-done.2
  65.3 0.2 owner_sums.1.left
  65.5 5.9 %collective-permute-start = (f32[256,128]{1,0:T(8,128)S(1)}, f32[256,128]{1,0:T(8,128)S(1)}, u32[]{:S(2)}, u32[]{:S(2)}) collective-permute-start(f32[256,128]{1,0:T(8,128)S(1)} %owner_sums.1.left), channel_id=1, source_target_pairs={{0,224},{1,97},{2,226},{3,99},{4,228},{5,101},{6,230},{7,103},{8,2... | collective-permute-start | bytes 393224 | tf_op jit(solution)/shard_map/ppermute | solution.py:369
  71.4 7.5 %all-to-all-start.3 = ((f32[32,32,128]{2,1,0:T(8,128)}), f32[32,32,128]{2,1,0:T(8,128)S(1)}, u32[]{:S(2)}, u32[]{:S(2)}) async-start(f32[32,32,128]{2,1,0:T(8,128)} %ocean.1.ocean_sums), calls=%async_computation.3 | async-start | bytes 1048576 | tf_op jit(solution)/shard_map/all_to_all | solution.py:402
  78.9 0.0 collective-permute-done.right
  79.0 2.0 %collective-permute-start.1 = (f32[256,128]{1,0:T(8,128)S(1)}, f32[256,128]{1,0:T(8,128)S(1)}, u32[]{:S(2)}, u32[]{:S(2)}) collective-permute-start(f32[256,128]{1,0:T(8,128)S(1)} %add.7.left), channel_id=1, source_target_pairs={{0,32},{1,33},{2,34},{3,35},{4,36},{5,37},{6,38},{7,39},{8,40},{9,... | collective-permute-start | bytes 393224 | tf_op jit(solution)/shard_map/ppermute | solution.py:369
  80.9 3.8 %collective-permute-done.1.right = f32[256,128]{1,0:T(8,128)S(1)} collective-permute-done((f32[256,128]{1,0:T(8,128)S(1)}, f32[256,128]{1,0:T(8,128)S(1)}, u32[]{:S(2)}, u32[]{:S(2)}) %collective-permute-start.1) | collective-permute-done | bytes 131104 | tf_op jit(solution)/shard_map/ppermute | solution.py:369
  84.8 2.3 %collective-permute-start.2 = (f32[256,128]{1,0:T(8,128)S(1)}, f32[256,128]{1,0:T(8,128)S(1)}, u32[]{:S(2)}, u32[]{:S(2)}) collective-permute-start(f32[256,128]{1,0:T(8,128)S(1)} %add.8.left), channel_id=1, source_target_pairs={{0,64},{1,193},{2,66},{3,195},{4,68},{5,197},{6,70},{7,199},{8,72}... | collective-permute-start | bytes 393224 | tf_op jit(solution)/shard_map/ppermute | solution.py:369
  87.0 2.4 %all-to-all-done.3 = f32[32,32,128]{2,1,0:T(8,128)S(1)} async-done(((f32[32,32,128]{2,1,0:T(8,128)}), f32[32,32,128]{2,1,0:T(8,128)S(1)}, u32[]{:S(2)}, u32[]{:S(2)}) %all-to-all-start.3) | async-done | bytes 524320 | tf_op jit(solution)/shard_map/all_to_all | solution.py:402
  89.4 0.6 reduce_sum.9
  90.1 1.7 %collective-permute-done.2.right = f32[256,128]{1,0:T(8,128)S(1)} collective-permute-done((f32[256,128]{1,0:T(8,128)S(1)}, f32[256,128]{1,0:T(8,128)S(1)}, u32[]{:S(2)}, u32[]{:S(2)}) %collective-permute-start.2) | collective-permute-done | bytes 131104 | tf_op jit(solution)/shard_map/ppermute | solution.py:369
  91.8 0.7 add.9
  (3 shorter events, 0.0 us)
Async XLA Ops:
  0.6 56.0 %copy-start.4 = (s32[384]{0:T(512)S(1)}, s32[384]{0:T(512)}, u32[]{:S(2)}) copy-start(s32[384]{0:T(512)} %param.20) | copy-start | bytes 4612
  15.0 1.0 %copy-start = (bf16[64,32,128]{2,1,0:T(8,128)(2,1)S(1)}, bf16[64,32,128]{2,1,0:T(8,128)(2,1)}, u32[]{:S(2)}) copy-start(bf16[64,32,128]{2,1,0:T(8,128)(2,1)} %fields.1) | copy-start | bytes 1572868
  18.2 21.3 %all-to-all-start.1 = ((bf16[128,32,128]{2,1,0:T(8,128)(2,1)}), bf16[128,32,128]{2,1,0:T(8,128)(2,1)S(1)}, u32[]{:S(2)}, u32[]{:S(2)}) async-start(bf16[128,32,128]{2,1,0:T(8,128)(2,1)} %serve.1), calls=%async_computation.1 | async-start | bytes 2097152 | tf_op jit(solution)/shard_map/all_to_all | solution.py:390
  26.5 0.9 %copy-start.1 = (s32[384,128]{1,0:T(8,128)S(1)}, s32[384,128]{1,0:T(8,128)}, u32[]{:S(2)}) copy-start(s32[384,128]{1,0:T(8,128)} %ocean_cell.1) | copy-start | bytes 589828
  27.4 0.9 %copy-start.2 = (f32[384,128]{1,0:T(8,128)S(1)}, f32[384,128]{1,0:T(8,128)}, u32[]{:S(2)}) copy-start(f32[384,128]{1,0:T(8,128)} %surf_temp.1) | copy-start | bytes 589828
  28.3 0.9 %copy-start.3 = (f32[384,128]{1,0:T(8,128)S(1)}, f32[384,128]{1,0:T(8,128)}, u32[]{:S(2)}) copy-start(f32[384,128]{1,0:T(8,128)} %surf_hum.1) | copy-start | bytes 589828
  51.6 13.7 %all-to-all-start.2 = ((f32[32,16,128]{2,1,0:T(8,128)}), f32[32,16,128]{2,1,0:T(8,128)S(1)}, u32[]{:S(2)}, u32[]{:S(2)}) async-start(f32[32,16,128]{2,1,0:T(8,128)} %bitcast.2), calls=%async_computation.2 | async-start | bytes 524288 | tf_op jit(solution)/shard_map/all_to_all | solution.py:399
  65.5 13.4 %collective-permute-start = (f32[256,128]{1,0:T(8,128)S(1)}, f32[256,128]{1,0:T(8,128)S(1)}, u32[]{:S(2)}, u32[]{:S(2)}) collective-permute-start(f32[256,128]{1,0:T(8,128)S(1)} %owner_sums.1.left), channel_id=1, source_target_pairs={{0,224},{1,97},{2,226},{3,99},{4,228},{5,101},{6,230},{7,103},{8,2... | collective-permute-start | bytes 393224 | tf_op jit(solution)/shard_map/ppermute | solution.py:369
  71.4 18.0 %all-to-all-start.3 = ((f32[32,32,128]{2,1,0:T(8,128)}), f32[32,32,128]{2,1,0:T(8,128)S(1)}, u32[]{:S(2)}, u32[]{:S(2)}) async-start(f32[32,32,128]{2,1,0:T(8,128)} %ocean.1.ocean_sums), calls=%async_computation.3 | async-start | bytes 1048576 | tf_op jit(solution)/shard_map/all_to_all | solution.py:402
  79.0 5.8 %collective-permute-start.1 = (f32[256,128]{1,0:T(8,128)S(1)}, f32[256,128]{1,0:T(8,128)S(1)}, u32[]{:S(2)}, u32[]{:S(2)}) collective-permute-start(f32[256,128]{1,0:T(8,128)S(1)} %add.7.left), channel_id=1, source_target_pairs={{0,32},{1,33},{2,34},{3,35},{4,36},{5,37},{6,38},{7,39},{8,40},{9,... | collective-permute-start | bytes 393224 | tf_op jit(solution)/shard_map/ppermute | solution.py:369
  84.8 7.0 %collective-permute-start.2 = (f32[256,128]{1,0:T(8,128)S(1)}, f32[256,128]{1,0:T(8,128)S(1)}, u32[]{:S(2)}, u32[]{:S(2)}) collective-permute-start(f32[256,128]{1,0:T(8,128)S(1)} %add.8.left), channel_id=1, source_target_pairs={{0,64},{1,193},{2,66},{3,195},{4,68},{5,197},{6,70},{7,199},{8,72}... | collective-permute-start | bytes 393224 | tf_op jit(solution)/shard_map/ppermute | solution.py:369

commit v8 on v5

--- a/solution.py
+++ b/solution.py
@@ -20,6 +20,7 @@
 flux_scale = 40.0
 
 GROUP = 64
+FLUX_PARTS = (32,96,128,128)
 MIB = 1 << 20
 ADD_COST = pl.CostEstimate(flops=1500000000, bytes_accessed=3 << 17, transcendentals=0)
 VMEM = pltpu.VMEM
@@ -76,24 +77,43 @@
     return drag * wind_u, drag * wind_v, carry * temp_diff, carry * hum_diff
 
 
-def serve_body(requests, fields, out):
-    def owner(d, _):
-        for c in range(CAP):
-            out[d * CAP + c] = fields[requests[d, c]]
-        return 0
-
-    lax.fori_loop(0, out.shape[0] // CAP, owner, 0)
+def serve_body(requests, fields_far, out_far, fields, out, in_sem, out_sem):
+    quarters = out_sem.shape[0]
+    owners = requests.shape[0] // quarters
+
+    def put(q):
+        share = pl.ds(q * owners * CAP, owners * CAP)
+        return pltpu.make_async_copy(out.at[share], out_far.at[share], out_sem.at[q])
+
+    fetch = pltpu.make_async_copy(fields_far, fields, in_sem)
+    fetch.start()
+    fetch.wait()
+    for q in range(quarters):
+        for d in range(q * owners, (q + 1) * owners):
+            for c in range(CAP):
+                out[d * CAP + c] = fields[requests[d, c]]
+        put(q).start()
+    for q in range(quarters):
+        put(q).wait()
 
 
 def serve(requests, fields):
+    far = pl.BlockSpec(memory_space=pltpu.HBM)
+    shape = (requests.size,) + fields.shape[1:]
     return pl.pallas_call(
         serve_body,
-        out_shape=jax.ShapeDtypeStruct((requests.size,) + fields.shape[1:], fields.dtype),
-        in_specs=[pl.BlockSpec(memory_space=SMEM), pl.BlockSpec(memory_space=VMEM)],
-        out_specs=pl.BlockSpec(memory_space=VMEM),
+        out_shape=pltpu.HBM(shape, fields.dtype),
+        in_specs=[pl.BlockSpec(memory_space=SMEM), far],
+        out_specs=far,
+        scratch_shapes=[
+            pltpu.VMEM(fields.shape, fields.dtype),
+            pltpu.VMEM(shape, fields.dtype),
+            pltpu.SemaphoreType.DMA,
+            pltpu.SemaphoreType.DMA((4,)),
+        ],
         compiler_params=pltpu.CompilerParams(vmem_limit_bytes=8 * MIB),
         name="serve",
-    )(requests, fields)
+    )(requests, pltpu.with_memory_space_constraint(fields, pltpu.HBM))
 
 
 def prep_body(ocean_cell, surf_temp, surf_hum, requests, hot, temp, hum, request_row):
@@ -165,35 +185,37 @@
     in_sem,
     out_sem,
 ):
-    blocks = held.shape[0]
-    parts = blocks // GROUP
+    firsts = [sum(FLUX_PARTS[:p]) for p in range(len(FLUX_PARTS))]
 
     def fetch(p):
-        share = pl.ds(pl.multiple_of(p * GROUP, GROUP), GROUP)
+        share = pl.ds(firsts[p], FLUX_PARTS[p])
         return pltpu.make_async_copy(weights.at[share], held.at[share], in_sem.at[p])
 
     def put(p):
-        share = pl.ds(pl.multiple_of(p * (GROUP * F), GROUP * F), GROUP * F)
+        share = pl.ds(firsts[p] * F, FLUX_PARTS[p] * F)
         return pltpu.make_async_copy(rows.at[share], rows_out.at[share], out_sem.at[p])
 
-    for p in range(parts):
-        fetch(p).start()
-
-    def part(p, _):
-        base = p * GROUP
-        fetch(p).wait()
-        for i in range(0, GROUP, 2):
-            k = base + i
-            both = lax.dot_general(
-                jnp.concatenate([table[use_slot[0, k]], table[use_slot[0, k + 1]]], axis=0),
-                held[pl.ds(k, 2)].reshape(2 * BLK, ACELL),
-                (((1,), (1,)), ((), ())),
-                preferred_element_type=jnp.float32,
-            )
-            rows[pl.ds(pl.multiple_of(k * F, F), F), :] = both[:F, :BLK]
-            rows[pl.ds(pl.multiple_of(k * F + F, F), F), :] = both[F:, BLK:]
-        mine = pl.ds(pl.multiple_of(base, GROUP), GROUP)
-        row = lambda f: pl.ds(base * F + f, GROUP, stride=F)
+    def map_pair(k):
+        both = lax.dot_general(
+            jnp.concatenate([table[use_slot[0, k]], table[use_slot[0, k + 1]]], axis=0),
+            held[k : k + 2].reshape(2 * BLK, ACELL),
+            (((1,), (1,)), ((), ())),
+            preferred_element_type=jnp.float32,
+        )
+        rows[k * F : (k + 1) * F, :] = both[:F, :BLK]
+        rows[(k + 1) * F : (k + 2) * F, :] = both[F:, BLK:]
+
+    def contribute_pair(k):
+        left = jnp.concatenate(
+            [rows[k * F : k * F + 8, :], rows[(k + 1) * F : (k + 1) * F + 8, :]], axis=0
+        ).astype(jnp.bfloat16)
+        both = product(left, jnp.concatenate([held[k], held[k + 1]], axis=1))
+        contrib[k * 8 : (k + 1) * 8, :] = both[:8, :ACELL]
+        contrib[(k + 1) * 8 : (k + 2) * 8, :] = both[8:, ACELL:]
+
+    def flux_part(p):
+        mine = pl.ds(firsts[p], FLUX_PARTS[p])
+        row = lambda f: pl.ds(firsts[p] * F + f, FLUX_PARTS[p], stride=F)
         fluxes = flux_rows(
             *(rows[row(f), :] for f in range(4)),
             surf_temp[mine, :],
@@ -205,23 +227,21 @@
         for f in range(4):
             rows[row(f), :] = weight * fluxes[f]
         put(p).start()
-        for i in range(0, GROUP, 2):
-            k = base + i
-            left = jnp.concatenate(
-                [
-                    rows[pl.ds(pl.multiple_of(k * F, F), 8), :],
-                    rows[pl.ds(pl.multiple_of(k * F + F, F), 8), :],
-                ],
-                axis=0,
-            ).astype(jnp.bfloat16)
-            both = product(left, jnp.concatenate([held[k], held[k + 1]], axis=1))
-            contrib[pl.ds(pl.multiple_of(k * 8, 8), 8), :] = both[:8, :ACELL]
-            contrib[pl.ds(pl.multiple_of(k * 8 + 8, 8), 8), :] = both[8:, ACELL:]
-        return 0
-
-    lax.fori_loop(0, parts, part, 0)
+
+    def pairs(p):
+        return range(firsts[p], firsts[p] + FLUX_PARTS[p], 2)
+
+    for p in range(len(FLUX_PARTS)):
+        fetch(p).start()
+    for p in range(len(FLUX_PARTS)):
+        fetch(p).wait()
+        for k in pairs(p):
+            map_pair(k)
+        flux_part(p)
+        for k in pairs(p):
+            contribute_pair(k)
     sum_rows(one_hot(slot_row[...], table.shape[0]), contrib, slot_sums, 8)
-    for p in range(parts):
+    for p in range(len(FLUX_PARTS)):
         put(p).wait()
 
 
@@ -241,8 +261,8 @@
             pltpu.VMEM(weights.shape, weights.dtype),
             pltpu.VMEM((blocks * F, BLK), jnp.float32),
             pltpu.VMEM((blocks * 8, ACELL), jnp.float32),
-            pltpu.SemaphoreType.DMA((blocks // GROUP,)),
-            pltpu.SemaphoreType.DMA((blocks // GROUP,)),
+            pltpu.SemaphoreType.DMA((len(FLUX_PARTS),)),
+            pltpu.SemaphoreType.DMA((len(FLUX_PARTS),)),
         ],
         compiler_params=pltpu.CompilerParams(vmem_limit_bytes=30 * MIB),
         name="fluxes",

time: 93.4 us -> 92.2 us (0.987)
  local copies, waits for them, and re-layouts: 5.89 us -> 4.85 us
    pallas_call x1, Pallas kernels: 12.9 us -> 11.9 us  [fluxes_of(): pl.pallas_call(flux_body, out_shape=(pltpu.HBM((blocks * F, BLK), jnp.flo...]
    unnamed x10 -> x8, local copies, waits for them, and re-layouts: 3.82 us -> 2.78 us
where the time goes in v8:
time: 92.2 us; the launch traced here: 91.6 us
  Pallas kernels  30.8 us (33%)
  starting transfers between devices  28 us (30%)
  blocking collectives  13.6 us (15%)
  waiting for transfers between devices  11.1 us (12%)
  local copies, waits for them, and re-layouts  4.85 us (5%)
  other arithmetic  2.58 us (3%)
    all_to_all x1, blocking collectives, per_device(): lax.all_to_all(need_list[0], 'atm', split_axis=0, concat_axis=0, tiled=True)  13.6 us
    pallas_call x1, Pallas kernels, fluxes_of(): pl.pallas_call(flux_body, out_shape=(pltpu.HBM((blocks * F, BLK), jnp.flo...  11.9 us
    ppermute x3, starting transfers between devices, sum_over_ring(): x = add(x, lax.ppermute(x, (axis, other), pairs))  10.5 us
    pallas_call x1, Pallas kernels, ocean_of(): pl.pallas_call(ocean_body, out_shape=jax.ShapeDtypeStruct((owners, F, OCE...  8.63 us
    all_to_all x1, starting transfers between devices, per_device(): lax.all_to_all(ocean_sums, 'atm', split_axis=0, concat_axis=0, tiled=True)  7.49 us
    ppermute x3, waiting for transfers between devices, sum_over_ring(): x = add(x, lax.ppermute(x, (axis, other), pairs))  7.33 us
    pallas_call x1, Pallas kernels, prep(): pl.pallas_call(prep_body, out_shape=(pltpu.HBM((blocks, BLK, OCELL), jnp....  6.45 us
    all_to_all x1, starting transfers between devices, per_device(): lax.all_to_all(serve(requests, atm_fields), 'atm', split_axis=0, concat_a...  5.04 us
  transfers between devices with their start and end apart: 6, of which 3 were waited for; matrix products, arithmetic and copies ran while one was open for 4% of the time, Pallas kernels for 16%

profile of v8, /device:TPU:2, one launch (start us, length us, event | category | flops | bytes accessed | tf_op | source)
XLA Modules:
  0.0 91.6 jit_solution(18327338306783837495)
XLA Ops:
  0.6 0.0 copy-start.3
  0.6 0.8 copy.18
  1.4 13.6 %all_to_all.32 = s32[32,1,4]{2,1,0:T(1,128)S(1)} all-to-all(s32[32,1,4]{2,1,0:T(1,128)S(1)} %copy.18), channel_id=1, replica_groups=mesh['ocn'=8,'atm'=32] {'atm'}, dimensions={0} | all-to-all | bytes 1024 | tf_op jit(solution)/shard_map/all_to_all | solution.py:410
  15.0 3.0 %serve.1 = bf16[128,32,128]{2,1,0:T(8,128)(2,1)} custom-call(s32[32,4]{1,0:T(8,128)S(1)} %bitcast.7, bf16[64,32,128]{2,1,0:T(8,128)(2,1)} %fields_far.1), custom_call_target="tpu_custom_call" | custom-call | tf_op jit(solution)/shard_map/serve/pallas_call | solution.py:103
  17.9 5.0 %all-to-all-start.1 = ((bf16[128,32,128]{2,1,0:T(8,128)(2,1)}), bf16[128,32,128]{2,1,0:T(8,128)(2,1)S(1)}, u32[]{:S(2)}, u32[]{:S(2)}) async-start(bf16[128,32,128]{2,1,0:T(8,128)(2,1)} %serve.1), calls=%async_computation.1 | async-start | bytes 2097152 | tf_op jit(solution)/shard_map/all_to_all | solution.py:411
  23.0 0.7 reshape.24.use_slot.slot_row
  23.7 1.2 %subtract_multiply_fusion = (f32[384,128]{1,0:T(8,128)S(1)}, f32[384,128]{1,0:T(8,128)S(1)}, f32[384,128]{1,0:T(8,128)S(1)}, f32[384,128]{1,0:T(8,128)S(1)}) fusion(s32[384,128]{1,0:T(8,128)} %param.23, f32[384,128]{1,0:T(8,128)} %param.17, s32[384]{0:T(512)} %param.22, f32[384,128]{1,0:T(8,128)} %param.16), kind=kLoop, calls=%fused_computation | loop fusion | flops 442368 | bytes 1377792 | tf_op jit(solution)/shard_map/mul | solution.py:418
  24.9 0.5 broadcast.10
  25.4 0.7 reduce.3
  26.1 0.1 reshape.23.requests
  26.2 0.0 copy-start
  26.2 0.9 %copy-done = s32[384,128]{1,0:T(8,128)S(1)} copy-done((s32[384,128]{1,0:T(8,128)S(1)}, s32[384,128]{1,0:T(8,128)}, u32[]{:S(2)}) %copy-start) | copy-done | bytes 196632
  27.2 0.0 copy-start.1
  27.2 0.9 %copy-done.1 = f32[384,128]{1,0:T(8,128)S(1)} copy-done((f32[384,128]{1,0:T(8,128)S(1)}, f32[384,128]{1,0:T(8,128)}, u32[]{:S(2)}) %copy-start.1) | copy-done | bytes 196632
  28.1 0.0 copy-start.2
  28.1 0.9 %copy-done.2 = f32[384,128]{1,0:T(8,128)S(1)} copy-done((f32[384,128]{1,0:T(8,128)S(1)}, f32[384,128]{1,0:T(8,128)}, u32[]{:S(2)}) %copy-start.2) | copy-done | bytes 196632
  29.0 6.5 %prep.1 = (bf16[384,128,128]{2,1,0:T(8,128)(2,1)}, f32[384,128]{1,0:T(8,128)S(1)}, f32[384,128]{1,0:T(8,128)S(1)}, s32[1,128]{1,0:T(1,128)S(1)}) custom-call(s32[384,128]{1,0:T(8,128)S(1)} %copy-done, f32[384,128]{1,0:T(8,128)S(1)} %copy-done.1, f32[384,128]{1,0:T(8,128)S(1)} %copy-done.2, s32[1,128]{1,0:T(1,128)S(1)} %reshape.23.requests), custom_call_target="tpu_custom_call" | custom-call | flops 12582912 | bytes 12582912 | tf_op jit(solution)/shard_map/prep/pallas_call | solution.py:133
  35.5 3.7 %all-to-all-done.1.table = bf16[128,32,128]{2,1,0:T(8,128)(2,1)S(1)} async-done(((bf16[128,32,128]{2,1,0:T(8,128)(2,1)}), bf16[128,32,128]{2,1,0:T(8,128)(2,1)S(1)}, u32[]{:S(2)}, u32[]{:S(2)}) %all-to-all-start.1) | async-done | bytes 1048608 | tf_op jit(solution)/shard_map/all_to_all | solution.py:411
  39.2 11.9 %fluxes.1 = (f32[12288,128]{1,0:T(8,128)}, f32[512,128]{1,0:T(8,128)}) custom-call(s32[1,384]{1,0:T(1,128)S(1)} %reshape.24.use_slot.slot_row, s32[1,384]{1,0:T(1,128)S(1)} %reshape.24.use_slot.slot_row, bf16[128,32,128]{2,1,0:T(8,128)(2,1)S(1)} %all-to-all-done.1.table, bf16[384,128,128]{2,1,0:T(8,128)(2,1)} %weights.1, ...), custom_call_target="tpu_custom_call" | custom-call | tf_op jit(solution)/shard_map/fluxes/pallas_call | solution.py:252
  51.1 5.0 %all-to-all-start.2 = ((f32[32,16,128]{2,1,0:T(8,128)}), f32[32,16,128]{2,1,0:T(8,128)S(1)}, u32[]{:S(2)}, u32[]{:S(2)}) async-start(f32[32,16,128]{2,1,0:T(8,128)} %bitcast.2), calls=%async_computation.2 | async-start | bytes 524288 | tf_op jit(solution)/shard_map/all_to_all | solution.py:420
  56.1 0.0 copy-done.3
  56.1 8.6 %ocean.1.ocean_sums = f32[32,32,128]{2,1,0:T(8,128)} custom-call(s32[1,384]{1,0:T(1,128)S(1)} %reshape.25.ocean_block, f32[12288,128]{1,0:T(8,128)} %get-tuple-element.12.rows_far, bf16[384,128,128]{2,1,0:T(8,128)(2,1)} %get-tuple-element.13.hot_far, f32[384,128]{1,0:T(8,128)S(1)} %get-tuple-element.14.passive_weight), custom_call_target="tpu_custom_call" | custom-call | flops 201326592 | bytes 18874368 | tf_op jit(solution)/shard_map/ocean/pallas_call | solution.py:318
  64.8 0.0 all-to-all-done.2
  64.8 0.2 owner_sums.1.left
  65.0 2.0 %collective-permute-start = (f32[256,128]{1,0:T(8,128)S(1)}, f32[256,128]{1,0:T(8,128)S(1)}, u32[]{:S(2)}, u32[]{:S(2)}) collective-permute-start(f32[256,128]{1,0:T(8,128)S(1)} %owner_sums.1.left), channel_id=1, source_target_pairs={{0,32},{1,33},{2,34},{3,35},{4,36},{5,37},{6,38},{7,39},{8,40},{9,... | collective-permute-start | bytes 393224 | tf_op jit(solution)/shard_map/ppermute | solution.py:389
  66.9 7.5 %all-to-all-start.3 = ((f32[32,32,128]{2,1,0:T(8,128)}), f32[32,32,128]{2,1,0:T(8,128)S(1)}, u32[]{:S(2)}, u32[]{:S(2)}) async-start(f32[32,32,128]{2,1,0:T(8,128)} %ocean.1.ocean_sums), calls=%async_computation.3 | async-start | bytes 1048576 | tf_op jit(solution)/shard_map/all_to_all | solution.py:423
  74.4 0.0 collective-permute-done.right
  74.5 3.4 %collective-permute-start.1 = (f32[256,128]{1,0:T(8,128)S(1)}, f32[256,128]{1,0:T(8,128)S(1)}, u32[]{:S(2)}, u32[]{:S(2)}) collective-permute-start(f32[256,128]{1,0:T(8,128)S(1)} %add.7.left), channel_id=1, source_target_pairs={{0,64},{1,193},{2,66},{3,195},{4,68},{5,197},{6,70},{7,199},{8,72}... | collective-permute-start | bytes 393224 | tf_op jit(solution)/shard_map/ppermute | solution.py:389
  77.8 3.9 %collective-permute-done.1.right = f32[256,128]{1,0:T(8,128)S(1)} collective-permute-done((f32[256,128]{1,0:T(8,128)S(1)}, f32[256,128]{1,0:T(8,128)S(1)}, u32[]{:S(2)}, u32[]{:S(2)}) %collective-permute-start.1) | collective-permute-done | bytes 131104 | tf_op jit(solution)/shard_map/ppermute | solution.py:389
  81.7 5.1 %collective-permute-start.2 = (f32[256,128]{1,0:T(8,128)S(1)}, f32[256,128]{1,0:T(8,128)S(1)}, u32[]{:S(2)}, u32[]{:S(2)}) collective-permute-start(f32[256,128]{1,0:T(8,128)S(1)} %add.8.left), channel_id=1, source_target_pairs={{0,224},{1,97},{2,226},{3,99},{4,228},{5,101},{6,230},{7,103},{8,2... | collective-permute-start | bytes 393224 | tf_op jit(solution)/shard_map/ppermute | solution.py:389
  86.9 0.0 all-to-all-done.3
  86.9 0.7 reduce_sum.9
  87.5 3.4 %collective-permute-done.2.right = f32[256,128]{1,0:T(8,128)S(1)} collective-permute-done((f32[256,128]{1,0:T(8,128)S(1)}, f32[256,128]{1,0:T(8,128)S(1)}, u32[]{:S(2)}, u32[]{:S(2)}) %collective-permute-start.2) | collective-permute-done | bytes 131104 | tf_op jit(solution)/shard_map/ppermute | solution.py:389
  91.0 0.7 add.9
  (3 shorter events, 0.0 us)
Async XLA Ops:
  0.6 55.5 %copy-start.3 = (s32[384]{0:T(512)S(1)}, s32[384]{0:T(512)}, u32[]{:S(2)}) copy-start(s32[384]{0:T(512)} %param.20) | copy-start | bytes 4612
  17.9 21.3 %all-to-all-start.1 = ((bf16[128,32,128]{2,1,0:T(8,128)(2,1)}), bf16[128,32,128]{2,1,0:T(8,128)(2,1)S(1)}, u32[]{:S(2)}, u32[]{:S(2)}) async-start(bf16[128,32,128]{2,1,0:T(8,128)(2,1)} %serve.1), calls=%async_computation.1 | async-start | bytes 2097152 | tf_op jit(solution)/shard_map/all_to_all | solution.py:411
  26.2 0.9 %copy-start = (s32[384,128]{1,0:T(8,128)S(1)}, s32[384,128]{1,0:T(8,128)}, u32[]{:S(2)}) copy-start(s32[384,128]{1,0:T(8,128)} %ocean_cell.1) | copy-start | bytes 589828
  27.2 0.9 %copy-start.1 = (f32[384,128]{1,0:T(8,128)S(1)}, f32[384,128]{1,0:T(8,128)}, u32[]{:S(2)}) copy-start(f32[384,128]{1,0:T(8,128)} %surf_temp.1) | copy-start | bytes 589828
  28.1 0.9 %copy-start.2 = (f32[384,128]{1,0:T(8,128)S(1)}, f32[384,128]{1,0:T(8,128)}, u32[]{:S(2)}) copy-start(f32[384,128]{1,0:T(8,128)} %surf_hum.1) | copy-start | bytes 589828
  51.1 13.7 %all-to-all-start.2 = ((f32[32,16,128]{2,1,0:T(8,128)}), f32[32,16,128]{2,1,0:T(8,128)S(1)}, u32[]{:S(2)}, u32[]{:S(2)}) async-start(f32[32,16,128]{2,1,0:T(8,128)} %bitcast.2), calls=%async_computation.2 | async-start | bytes 524288 | tf_op jit(solution)/shard_map/all_to_all | solution.py:420
  65.0 9.5 %collective-permute-start = (f32[256,128]{1,0:T(8,128)S(1)}, f32[256,128]{1,0:T(8,128)S(1)}, u32[]{:S(2)}, u32[]{:S(2)}) collective-permute-start(f32[256,128]{1,0:T(8,128)S(1)} %owner_sums.1.left), channel_id=1, source_target_pairs={{0,32},{1,33},{2,34},{3,35},{4,36},{5,37},{6,38},{7,39},{8,40},{9,... | collective-permute-start | bytes 393224 | tf_op jit(solution)/shard_map/ppermute | solution.py:389
  66.9 19.9 %all-to-all-start.3 = ((f32[32,32,128]{2,1,0:T(8,128)}), f32[32,32,128]{2,1,0:T(8,128)S(1)}, u32[]{:S(2)}, u32[]{:S(2)}) async-start(f32[32,32,128]{2,1,0:T(8,128)} %ocean.1.ocean_sums), calls=%async_computation.3 | async-start | bytes 1048576 | tf_op jit(solution)/shard_map/all_to_all | solution.py:423
  74.5 7.3 %collective-permute-start.1 = (f32[256,128]{1,0:T(8,128)S(1)}, f32[256,128]{1,0:T(8,128)S(1)}, u32[]{:S(2)}, u32[]{:S(2)}) collective-permute-start(f32[256,128]{1,0:T(8,128)S(1)} %add.7.left), channel_id=1, source_target_pairs={{0,64},{1,193},{2,66},{3,195},{4,68},{5,197},{6,70},{7,199},{8,72}... | collective-permute-start | bytes 393224 | tf_op jit(solution)/shard_map/ppermute | solution.py:389
  81.7 9.2 %collective-permute-start.2 = (f32[256,128]{1,0:T(8,128)S(1)}, f32[256,128]{1,0:T(8,128)S(1)}, u32[]{:S(2)}, u32[]{:S(2)}) collective-permute-start(f32[256,128]{1,0:T(8,128)S(1)} %add.8.left), channel_id=1, source_target_pairs={{0,224},{1,97},{2,226},{3,99},{4,228},{5,101},{6,230},{7,103},{8,2... | collective-permute-start | bytes 393224 | tf_op jit(solution)/shard_map/ppermute | solution.py:389
